TPU v7x, 32 devices: a whole 2x2x4 slice. The times are simulated.
32 devices in a mesh: dp: 4 (over y, x), fsdp: 8 (over z, core).
Axes of the slice: x: 2, y: 2, z: 4, core: 2. Of those that a mesh axis runs over, the one named last changes fastest.
Arguments:
- tokens: bfloat16 [96, 256, 1152], P(('dp', 'fsdp')), may hold values from -6 to 6
- timesteps: int32 [96], P(('dp', 'fsdp')), may hold values from 0 to 999
- labels: int32 [96], P(('dp', 'fsdp')), may hold values from 0 to 999
- head_mask: int32 [96, 16], P(('dp', 'fsdp')), may hold values 0 or 1
- keep_mask: int32 [96, 256], P(('dp', 'fsdp')), may hold values from 0 to 1, as said below
- cotangent: bfloat16 [96, 256, 1152], P(('dp', 'fsdp')), may hold values from -6 to 6
- time_weight: bfloat16 [256, 1152], P('fsdp'), may hold values from -0.375 to 0.375
- class_table: bfloat16 [1000, 1152], P(None, 'fsdp'), may hold values from -6 to 6
- ada_weight: bfloat16 [1152, 6912], P(None, 'fsdp'), may hold values from -0.1875 to 0.1875
- head_router: bfloat16 [1152, 16], P('fsdp'), may hold values from -0.1875 to 0.1875
- qkv_weight: bfloat16 [1152, 3456], P('fsdp'), may hold values from -0.1875 to 0.1875
- proj_weight: bfloat16 [1152, 1152], P('fsdp'), may hold values from -0.5 to 0.5
- fc1_weight: bfloat16 [1152, 4608], P('fsdp'), may hold values from -0.1875 to 0.1875
- fc2_weight: bfloat16 [4608, 1152], P('fsdp'), may hold values from -0.1875 to 0.1875
- token_router: bfloat16 [1152, 1], P('fsdp'), may hold values from -0.1875 to 0.1875
Outputs:
- output: bfloat16 [96, 256, 1152], P(('dp', 'fsdp'))
- grad_tokens: float32 [96, 256, 1152], P(('dp', 'fsdp'))
- grad_time_weight: float32 [256, 1152], P('fsdp')
- grad_class_table: float32 [1000, 1152], P(None, 'fsdp')
- grad_ada_weight: float32 [1152, 6912], P(None, 'fsdp')
- grad_head_router: float32 [1152, 16], P('fsdp')
- grad_qkv_weight: float32 [1152, 3456], P('fsdp')
- grad_proj_weight: float32 [1152, 1152], P('fsdp')
- grad_fc1_weight: float32 [1152, 4608], P('fsdp')
- grad_fc2_weight: float32 [4608, 1152], P('fsdp')
- grad_token_router: float32 [1152, 1], P('fsdp')
Inputs may be any that keep to these rules, and one draw needn't show every extreme that they name: `keep_mask`: each image keeps between one fifth (rounded up) and all of its 256 tokens.
All inputs are finite; a program needn't handle non-finite values. No bound on the sum of `head_mask` on one device may be relied on, other than what follows from the above.
Results may differ from a plain program's by a relative error of at most 0.02.
Values may be sent and summed in bfloat16 or wider, within the bound.
A program may use at most 256 MiB of HBM per device.

v0:
```python
from functools import partial
import math

import jax
import jax.numpy as jnp
from jax import lax
from jax.sharding import PartitionSpec as P

EPSILON = 1e-06


def sinusoid(steps, entries):
    half = entries // 2
    freqs = jnp.exp(-math.log(10000.0) * jnp.arange(half, dtype=jnp.float32) / half)
    angles = steps.astype(jnp.float32)[:, None] * freqs[None, :]
    return jnp.concatenate([jnp.cos(angles), jnp.sin(angles)], axis=1)


def layer_norm(value):
    centered = value - jnp.mean(value, axis=-1, keepdims=True)
    return centered * lax.rsqrt(jnp.mean(centered * centered, axis=-1, keepdims=True) + EPSILON)


def norm_back(value, grad):
    _, pull = jax.vjp(layer_norm, value)
    return pull(grad)[0]


def matmul(left, right):
    return jnp.dot(left, right, preferred_element_type=jnp.float32)


def times_rows(left, right):
    return lax.dot_general(
        left, right, (((0,), (0,)), ((), ())), preferred_element_type=jnp.float32
    )


def times_back(left, right):
    return lax.dot_general(
        left, right, (((1,), (1,)), ((), ())), preferred_element_type=jnp.float32
    )


def body(
    tokens,
    timesteps,
    labels,
    head_mask,
    keep_mask,
    cotangent,
    time_weight,
    class_table,
    ada_weight,
    head_router,
    qkv_weight,
    proj_weight,
    fc1_weight,
    fc2_weight,
    token_router,
):
    images, seq, width = tokens.shape
    heads = head_mask.shape[1]
    size = width // heads
    scale = size ** (-0.5)
    count = images * seq
    triple, merger, expand, shrink, picker = (
        lax.all_gather(qkv_weight, "fsdp", axis=0, tiled=True),
        lax.all_gather(proj_weight, "fsdp", axis=0, tiled=True),
        lax.all_gather(fc1_weight, "fsdp", axis=0, tiled=True),
        lax.all_gather(fc2_weight, "fsdp", axis=0, tiled=True),
        lax.all_gather(token_router, "fsdp", axis=0, tiled=True),
    )
    time_full, table_full, chooser = (
        lax.all_gather(time_weight, "fsdp", axis=0, tiled=True),
        lax.all_gather(class_table, "fsdp", axis=1, tiled=True),
        lax.all_gather(head_router, "fsdp", axis=0, tiled=True),
    )
    embedded = sinusoid(timesteps, time_full.shape[0]).astype(jnp.bfloat16)
    label_rows = (
        labels[:, None] == jnp.arange(table_full.shape[0], dtype=jnp.int32)[None, :]
    ).astype(jnp.bfloat16)
    pre_cond = matmul(embedded, time_full) + matmul(label_rows, table_full)
    cond = jax.nn.silu(pre_cond).astype(jnp.bfloat16)
    ada_full = lax.all_gather(ada_weight, "fsdp", axis=1, tiled=True)
    modulation = matmul(cond, ada_full)
    shift_one, scale_one, gate_one, shift_two, scale_two, gate_two = jnp.split(
        modulation[:, None, :], 6, axis=2
    )
    router_sig = jax.nn.sigmoid(matmul(cond, chooser))
    mask_float = head_mask.astype(jnp.float32)
    head_gates = mask_float * router_sig
    inputs = tokens.astype(jnp.float32)
    normed_one = layer_norm(inputs)
    flat_one = (
        (normed_one * (1.0 + scale_one) + shift_one).astype(jnp.bfloat16).reshape(count, width)
    )
    joint = matmul(flat_one, triple).astype(jnp.bfloat16)
    query = joint[:, :width].reshape(images, seq, heads, size)
    keys = joint[:, width : 2 * width].reshape(images, seq, heads, size)
    values = joint[:, 2 * width :].reshape(images, seq, heads, size)
    raw = jnp.einsum("ishe,ithe->ihst", query, keys, preferred_element_type=jnp.float32) * scale
    peak = jnp.max(raw, axis=-1, keepdims=True)
    expo = jnp.exp(raw - peak)
    total = jnp.sum(expo, axis=-1, keepdims=True)
    log_total = peak + jnp.log(total)
    probs_low = (expo / total).astype(jnp.bfloat16)
    attended = jnp.einsum("ihst,ithe->ishe", probs_low, values, preferred_element_type=jnp.float32)
    mixed = (attended * head_gates[:, None, :, None]).astype(jnp.bfloat16).reshape(count, width)
    attn = matmul(mixed, merger).reshape(images, seq, width)
    middle = inputs + gate_one * attn
    normed_two = layer_norm(middle)
    flat_two = (
        (normed_two * (1.0 + scale_two) + shift_two).astype(jnp.bfloat16).reshape(count, width)
    )
    rate = jax.nn.sigmoid(matmul(flat_two, picker)).reshape(images, seq, 1)
    upward = matmul(flat_two, expand)
    active = jax.nn.gelu(upward, approximate=True).astype(jnp.bfloat16)
    downward = matmul(active, shrink).reshape(images, seq, width)
    kept = keep_mask.astype(jnp.float32)[:, :, None]
    kept_rate = kept * rate
    output = (middle + gate_two * kept_rate * downward).astype(jnp.bfloat16)
    triple, merger, expand, shrink, picker = (
        lax.all_gather(qkv_weight, "fsdp", axis=0, tiled=True),
        lax.all_gather(proj_weight, "fsdp", axis=0, tiled=True),
        lax.all_gather(fc1_weight, "fsdp", axis=0, tiled=True),
        lax.all_gather(fc2_weight, "fsdp", axis=0, tiled=True),
        lax.all_gather(token_router, "fsdp", axis=0, tiled=True),
    )
    grad_out = cotangent.astype(jnp.float32)
    grad_gate_two = jnp.sum(grad_out * kept_rate * downward, axis=1)
    grad_down = (grad_out * gate_two * kept_rate).astype(jnp.bfloat16).reshape(count, width)
    grad_rate = jnp.sum(grad_out * gate_two * downward, axis=-1, keepdims=True) * kept
    grad_logit = (grad_rate * rate * (1.0 - rate)).astype(jnp.bfloat16).reshape(count, 1)
    grad_shrink = times_rows(active, grad_down)
    _, gelu_pull = jax.vjp(partial(jax.nn.gelu, approximate=True), upward)
    grad_up = gelu_pull(times_back(grad_down, shrink))[0].astype(jnp.bfloat16)
    grad_expand = times_rows(flat_two, grad_up)
    grad_picker = times_rows(flat_two, grad_logit)
    grad_h_two = (times_back(grad_up, expand) + times_back(grad_logit, picker)).reshape(
        images, seq, width
    )
    grad_shift_two = jnp.sum(grad_h_two, axis=1)
    grad_scale_two = jnp.sum(grad_h_two * normed_two, axis=1)
    grad_middle = grad_out + norm_back(middle, grad_h_two * (1.0 + scale_two))
    grad_gate_one = jnp.sum(grad_middle * attn, axis=1)
    grad_attn = (grad_middle * gate_one).astype(jnp.bfloat16).reshape(count, width)
    grad_merger = times_rows(mixed, grad_attn)
    grad_mixed = (
        times_back(grad_attn, merger).astype(jnp.bfloat16).reshape(images, seq, heads, size)
    )
    grad_gates = jnp.sum(grad_mixed * attended, axis=(1, 3))
    grad_router = (grad_gates * mask_float * router_sig * (1.0 - router_sig)).astype(jnp.bfloat16)
    grad_attended = (grad_mixed * head_gates[:, None, :, None]).astype(jnp.bfloat16)
    again_raw = (
        jnp.einsum("ishe,ithe->ihst", query, keys, preferred_element_type=jnp.float32) * scale
    )
    probs = jnp.exp(again_raw - log_total)
    grad_values = jnp.einsum(
        "ihst,ishe->ithe",
        probs.astype(jnp.bfloat16),
        grad_attended,
        preferred_element_type=jnp.float32,
    )
    grad_probs = jnp.einsum(
        "ishe,ithe->ihst", grad_attended, values, preferred_element_type=jnp.float32
    )
    inner = jnp.sum(grad_probs * probs, axis=-1, keepdims=True)
    grad_scores = (probs * (grad_probs - inner) * scale).astype(jnp.bfloat16)
    grad_query = jnp.einsum(
        "ihst,ithe->ishe", grad_scores, keys, preferred_element_type=jnp.float32
    )
    grad_keys = jnp.einsum(
        "ihst,ishe->ithe", grad_scores, query, preferred_element_type=jnp.float32
    )
    grad_joint = jnp.concatenate(
        [
            grad_query.reshape(count, width),
            grad_keys.reshape(count, width),
            grad_values.reshape(count, width),
        ],
        axis=1,
    ).astype(jnp.bfloat16)
    grad_triple = times_rows(flat_one, grad_joint)
    grad_h_one = times_back(grad_joint, triple).reshape(images, seq, width)
    grad_shift_one = jnp.sum(grad_h_one, axis=1)
    grad_scale_one = jnp.sum(grad_h_one * normed_one, axis=1)
    grad_inputs = grad_middle + norm_back(inputs, grad_h_one * (1.0 + scale_one))
    grad_modulation = jnp.concatenate(
        [
            grad_shift_one,
            grad_scale_one,
            grad_gate_one,
            grad_shift_two,
            grad_scale_two,
            grad_gate_two,
        ],
        axis=1,
    ).astype(jnp.bfloat16)
    grad_cond = times_back(grad_modulation, ada_full)
    grad_ada = lax.psum_scatter(
        times_rows(cond, grad_modulation), "fsdp", scatter_dimension=1, tiled=True
    )
    grad_cond = grad_cond + times_back(grad_router, chooser)
    _, silu_pull = jax.vjp(jax.nn.silu, pre_cond)
    grad_pre = silu_pull(grad_cond)[0].astype(jnp.bfloat16)
    grad_time = times_rows(embedded, grad_pre)
    grad_table = times_rows(label_rows, grad_pre)
    grad_chooser = times_rows(cond, grad_router)
    shards = (
        lax.psum_scatter(grad_time, "fsdp", scatter_dimension=0, tiled=True),
        lax.psum_scatter(grad_table, "fsdp", scatter_dimension=1, tiled=True),
        lax.psum_scatter(grad_chooser, "fsdp", scatter_dimension=0, tiled=True),
        lax.psum_scatter(grad_triple, "fsdp", scatter_dimension=0, tiled=True),
        lax.psum_scatter(grad_merger, "fsdp", scatter_dimension=0, tiled=True),
        lax.psum_scatter(grad_expand, "fsdp", scatter_dimension=0, tiled=True),
        lax.psum_scatter(grad_shrink, "fsdp", scatter_dimension=0, tiled=True),
        lax.psum_scatter(grad_picker, "fsdp", scatter_dimension=0, tiled=True),
    )
    summed = lax.psum(
        (
            shards[0],
            shards[1],
            grad_ada,
            shards[2],
            shards[3],
            shards[4],
            shards[5],
            shards[6],
            shards[7],
        ),
        "dp",
    )
    return (
        output,
        grad_inputs,
        summed[0],
        summed[1],
        summed[2],
        summed[3],
        summed[4],
        summed[5],
        summed[6],
        summed[7],
        summed[8],
    )


def solution(mesh):
    in_specs = (
        P(("dp", "fsdp"), None, None),
        P(("dp", "fsdp")),
        P(("dp", "fsdp")),
        P(("dp", "fsdp"), None),
        P(("dp", "fsdp"), None),
        P(("dp", "fsdp"), None, None),
        P("fsdp", None),
        P(None, "fsdp"),
        P(None, "fsdp"),
        P("fsdp", None),
        P("fsdp", None),
        P("fsdp", None),
        P("fsdp", None),
        P("fsdp", None),
        P("fsdp", None),
    )
    out_specs = (
        P(("dp", "fsdp"), None, None),
        P(("dp", "fsdp"), None, None),
        P("fsdp", None),
        P(None, "fsdp"),
        P(None, "fsdp"),
        P("fsdp", None),
        P("fsdp", None),
        P("fsdp", None),
        P("fsdp", None),
        P("fsdp", None),
        P("fsdp", None),
    )
    return jax.shard_map(body, mesh=mesh, in_specs=in_specs, out_specs=out_specs, check_vma=False)
```

profile of v0, /device:TPU:0, one launch (start us, length us, event | category | flops | bytes accessed | tf_op | source)
XLA Modules:
  0.0 2053.9 jit_solution(8653730872954830014)
XLA Ops:
  12.8 18.4 all-reduce
  32.5 14.1 all-gather
  47.9 16.9 all_gather.32
  68.2 121.9 %all-gather.10.cloned.1.call-done = bf16[1152,6912]{0,1:T(8,128)(2,1)} async-done(((bf16[1152,864]{0,1:T(8,128)(2,1)}), bf16[1152,6912]{0,1:T(8,128)(2,1)}) %all-gather.10.cloned.1.call-update) | async-done | bytes 15925264 | tf_op jit(solution)/shard_map/all_gather | solution.py:85
  190.2 9.7 convolution_bitcast_fusion
  202.5 67.1 %all-gather.12.cloned.1.call-done = bf16[1152,3456]{1,0:T(8,128)(2,1)} async-done(((bf16[144,3456]{1,0:T(8,128)(2,1)}), bf16[1152,3456]{1,0:T(8,128)(2,1)}) %all-gather.12.cloned.1.call-update) | async-done | bytes 7962640 | tf_op jit(solution)/shard_map/all_gather | solution.py:68
  269.6 9.8 convolution_convert_fusion
  325.8 7.6 fusion.95
  341.9 62.9 %all-gather.16.cloned.1.call-done = bf16[1152,4608]{1,0:T(8,128)(2,1)} async-done(((bf16[144,4608]{1,0:T(8,128)(2,1)}), bf16[1152,4608]{1,0:T(8,128)(2,1)}) %all-gather.16.cloned.1.call-update) | async-done | bytes 10616848 | tf_op jit(solution)/shard_map/all_gather | solution.py:70
  404.8 15.9 fusion.97
  420.8 84.4 %all-gather.18.cloned.1.call-done = bf16[4608,1152]{1,0:T(8,128)(2,1)} async-done(((bf16[576,1152]{1,0:T(8,128)(2,1)}), bf16[4608,1152]{1,0:T(8,128)(2,1)}) %all-gather.18.cloned.1.call-update) | async-done | bytes 10616848 | tf_op jit(solution)/shard_map/all_gather | solution.py:71
  505.2 16.2 fusion.93
  526.9 23.2 %fusion.7 = bf16[768,4608]{1,0:T(8,128)(2,1)} fusion(f32[768,4608]{1,0:T(8,128)} %fusion.97, bf16[768,1152]{1,0:T(8,128)(2,1)} %bitcast.136, bf16[4608,1152]{1,0:T(8,128)(2,1)} %all-gather.18.cloned.1.call-done), kind=kOutput, calls=%fused_computation.9 | convolution fusion | flops 8224505856 | bytes 33619968 | tf_op jit(solution)/shard_map/dot_general | solution.py:40
  550.1 13.5 convolution_add_fusion
  584.9 7.9 fusion.64
  592.8 8.3 convert_bitcast_fusion
  601.2 20.2 convert_bitcast_fusion.2
  621.4 20.6 %convert_bitcast_fusion.1 = bf16[3,256,16,72]{1,3,2,0:T(8,128)(2,1)} fusion(bf16[3,256,16,72]{1,3,2,0:T(8,128)(2,1)} %copy.62, f32[3,16,256,256]{2,3,1,0:T(8,128)} %fusion.64, f32[3,16,256,256]{2,3,1,0:T(8,128)} %copy-done, f32[3,16,256]{2,1,0:T(8,128)} %log_add_fusion), kind=kOutput, calls=%fused_computation.79 | convolution fusion | flops 482193664 | bytes 28753920 | tf_op jit(solution)/shard_map/ihst,ishe->ithe/dot_general | solution.py:173
  654.6 13.1 fusion.98
  690.4 12.2 fusion.100
  704.1 17.9 fusion.92
  723.6 14.8 fusion.102
  738.7 16.1 fusion.91
  764.1 61.3 %reduce-scatter.22.cloned.1.call-done = f32[144,1152]{1,0:T(8,128)} async-done(((f32[1152,1152]{1,0:T(8,128)}), f32[144,1152]{1,0:T(8,128)}) %reduce-scatter.22.cloned.1.call-update) | async-done | bytes 663568 | tf_op jit(solution)/shard_map/reduce_scatter | solution.py:215
  825.3 161.4 %reduce-scatter.20.cloned.1.call-done = f32[144,3456]{1,0:T(8,128)} async-done(((f32[1152,3456]{1,0:T(8,128)}), f32[144,3456]{1,0:T(8,128)}) %reduce-scatter.20.cloned.1.call-update) | async-done | bytes 1990672 | tf_op jit(solution)/shard_map/reduce_scatter | solution.py:214
  986.7 211.0 %reduce-scatter.26.cloned.1.call-done = f32[576,1152]{1,0:T(8,128)} async-done(((f32[4608,1152]{1,0:T(8,128)}), f32[576,1152]{1,0:T(8,128)}) %reduce-scatter.26.cloned.1.call-update) | async-done | bytes 2654224 | tf_op jit(solution)/shard_map/reduce_scatter | solution.py:217
  1197.7 210.8 %reduce-scatter.24.cloned.1.call-done = f32[144,4608]{1,0:T(8,128)} async-done(((f32[1152,4608]{1,0:T(8,128)}), f32[144,4608]{1,0:T(8,128)}) %reduce-scatter.24.cloned.1.call-update) | async-done | bytes 2654224 | tf_op jit(solution)/shard_map/reduce_scatter | solution.py:216
  1408.5 311.5 %reduce-scatter.18.cloned.1.call-done = f32[1152,864]{0,1:T(8,128)} async-done(((f32[1152,6912]{0,1:T(8,128)}), f32[1152,864]{0,1:T(8,128)}) %reduce-scatter.18.cloned.1.call-update) | async-done | bytes 3981328 | tf_op jit(solution)/shard_map/reduce_scatter | solution.py:201
  1726.5 25.7 %reduce-scatter.30.cloned.1.call-done = f32[144,1]{1,0:T(8,128)} async-done(((f32[1152,1]{1,0:T(8,128)}), f32[144,1]{1,0:T(8,128)}) %reduce-scatter.30.cloned.1.call-update) | async-done | bytes 592
  1753.2 31.2 %reduce-scatter.28.cloned.1.call-done = f32[144,16]{1,0:T(8,128)} async-done(((f32[1152,16]{1,0:T(8,128)}), f32[144,16]{1,0:T(8,128)}) %reduce-scatter.28.cloned.1.call-update) | async-done | bytes 9232
  1785.3 17.4 all-reduce.1
  1802.7 230.3 %all-reduce.5.cloned.1.call-done = (f32[32,1152]{1,0:T(8,128)}, f32[1000,144]{0,1:T(8,128)}, f32[1152,864]{0,1:T(8,128)}, f32[144,3456]{1,0:T(8,128)}, f32[144,1...) async-done(((f32[32,1152]{1,0:T(8,128)}, f32[1000,144]{0,1:T(8,128)}, f32[1152,864]{0,1:T(8,128)}, f32[144,3456]{1,0:T(8,128)}, f32[144,1152]{1,0:T(8,128)}, ...) | async-done | bytes 12667408 | tf_op jit(solution)/shard_map/psum | solution.py:220
  (283 shorter events, 164.2 us)
Async XLA Ops:
  7.2 25.2 %copy-start.72 = (s32[3]{0:T(128)S(1)}, s32[3]{0:T(128)}, u32[]{:S(2)}) copy-start(s32[3]{0:T(128)} %param.16) | copy-start | bytes 40
  7.2 25.2 %copy-start.61 = (bf16[144,16]{0,1:T(8,128)(2,1)S(1)}, bf16[144,16]{0,1:T(8,128)(2,1)}, u32[]{:S(2)}) copy-start(bf16[144,16]{0,1:T(8,128)(2,1)} %param.24) | copy-start | bytes 13828
  7.2 39.5 %copy-start.1 = (bf16[3,256,1152]{2,1,0:T(8,128)(2,1)S(1)}, bf16[3,256,1152]{2,1,0:T(8,128)(2,1)}, u32[]{:S(2)}) copy-start(bf16[3,256,1152]{2,1,0:T(8,128)(2,1)} %param.15) | copy-start | bytes 5308420
  7.2 57.7 %all-gather.8.cloned.1.call-start = ((), (), s32[]{:S(2)}) async-start(), calls=%async_computation.9 | async-start | bytes 2654208 | tf_op jit(solution)/shard_map/all_gather | solution.py:76
  8.0 182.2 %all-gather.10.cloned.1.call-start = ((), (), s32[]{:S(2)}) async-start(), calls=%async_computation.10 | async-start | bytes 17915904 | tf_op jit(solution)/shard_map/all_gather | solution.py:85
  8.7 260.9 %all-gather.12.cloned.1.call-start = ((), (), s32[]{:S(2)}) async-start(), calls=%async_computation.11 | async-start | bytes 8957952 | tf_op jit(solution)/shard_map/all_gather | solution.py:68
  9.5 38.4 %copy-start.38 = (bf16[32,1152]{1,0:T(8,128)(2,1)S(1)}, bf16[32,1152]{1,0:T(8,128)(2,1)}, u32[]{:S(2)}) copy-start(bf16[32,1152]{1,0:T(8,128)(2,1)} %param.21) | copy-start | bytes 221188
  9.5 316.3 %all-gather.14.cloned.1.call-start = ((), (), s32[]{:S(2)}) async-start(), calls=%async_computation.12 | async-start | bytes 2985984 | tf_op jit(solution)/shard_map/all_gather | solution.py:69
  10.0 394.8 %all-gather.16.cloned.1.call-start = ((), (), s32[]{:S(2)}) async-start(), calls=%async_computation.13 | async-start | bytes 11943936 | tf_op jit(solution)/shard_map/all_gather | solution.py:70
  10.6 54.3 %copy-start.68 = (s32[3]{0:T(128)S(1)}, s32[3]{0:T(128)}, u32[]{:S(2)}) copy-start(s32[3]{0:T(128)} %param.17) | copy-start | bytes 40
  10.6 494.6 %all-gather.18.cloned.1.call-start = ((), (), s32[]{:S(2)}) async-start(), calls=%async_computation.14 | async-start | bytes 11943936 | tf_op jit(solution)/shard_map/all_gather | solution.py:71
  11.2 747.7 %reduce-scatter.14.cloned.1.call-start = ((), (), s32[]{:S(2)}) async-start(), calls=%async_computation.15 | async-start | bytes 1327104 | tf_op jit(solution)/shard_map/reduce_scatter | solution.py:211
  46.7 20.8 %copy-start.50 = (bf16[1152,16]{0,1:T(8,128)(2,1)}, bf16[1152,16]{0,1:T(8,128)(2,1)S(1)}, u32[]{:S(2)}) copy-start(bf16[1152,16]{0,1:T(8,128)(2,1)S(1)} %reshape.199) | copy-start | bytes 110596
  46.7 20.7 %copy-start.65 = (s32[3,16]{1,0:T(4,128)S(1)}, s32[3,16]{1,0:T(4,128)}, u32[]{:S(2)}) copy-start(s32[3,16]{1,0:T(4,128)} %param.18) | copy-start | bytes 580
  47.2 153.4 %copy-start.34 = (f32[3,256]{1,0:T(4,128)}, f32[3,256]{1,0:T(4,128)S(1)}, u32[]{:S(2)}) copy-start(f32[3,256]{1,0:T(4,128)S(1)} %broadcast_multiply_fusion.1) | copy-start | bytes 9220
  47.9 152.7 %copy-start.40 = (f32[3,256]{1,0:T(4,128)}, f32[3,256]{1,0:T(4,128)S(1)}, u32[]{:S(2)}) copy-start(f32[3,256]{1,0:T(4,128)S(1)} %fusion.73) | copy-start | bytes 9220
  67.5 132.4 %copy-start.28 = (f32[3,1152]{1,0:T(4,128)}, f32[3,1152]{1,0:T(4,128)S(1)}, u32[]{:S(2)}) copy-start(f32[3,1152]{1,0:T(4,128)S(1)} %convolution_add_fusion.1) | copy-start | bytes 41476
  202.4 77.0 %copy-start.18 = (bf16[3,256,1152]{2,1,0:T(8,128)(2,1)}, bf16[3,256,1152]{2,1,0:T(8,128)(2,1)S(1)}, u32[]{:S(2)}) copy-start(bf16[3,256,1152]{2,1,0:T(8,128)(2,1)S(1)} %fusion.41) | copy-start | bytes 5308420
  526.9 23.2 %copy-start.62 = (f32[1152]{0:T(1024)S(1)}, f32[1152]{0:T(1024)}, u32[]{:S(2)}) copy-start(f32[1152]{0:T(1024)} %convert.51) | copy-start | bytes 13828
  526.9 23.2 %copy-start.64 = (f32[768]{0:T(1024)S(1)}, f32[768]{0:T(1024)}, u32[]{:S(2)}) copy-start(f32[768]{0:T(1024)} %reshape.193) | copy-start | bytes 9220
  651.9 21.5 %slice-start = ((s8[15925248]{0:T(1024)(128)(4,1)}), s8[4194304]{0:T(1024)(128)(4,1)S(1)}, s32[]{:S(2)}) async-start(s8[15925248]{0:T(1024)(128)(4,1)} %bitcast.112), calls=%async_computation.25 | async-start | bytes 8388608
  654.6 18.8 slice-start.2
  654.6 18.8 slice-start.3
  677.3 86.8 %reduce-scatter.16.cloned.1.call-start = ((), (), s32[]{:S(2)}) async-start(), calls=%async_computation.16 | async-start | bytes 5308416 | tf_op jit(solution)/shard_map/reduce_scatter | solution.py:212
  680.3 145.0 %reduce-scatter.22.cloned.1.call-start = ((), (), s32[]{:S(2)}) async-start(), calls=%async_computation.19 | async-start | bytes 5971968 | tf_op jit(solution)/shard_map/reduce_scatter | solution.py:215
  688.9 297.7 %reduce-scatter.20.cloned.1.call-start = ((), (), s32[]{:S(2)}) async-start(), calls=%async_computation.18 | async-start | bytes 17915904 | tf_op jit(solution)/shard_map/reduce_scatter | solution.py:214
  702.7 495.0 %reduce-scatter.26.cloned.1.call-start = ((), (), s32[]{:S(2)}) async-start(), calls=%async_computation.21 | async-start | bytes 23887872 | tf_op jit(solution)/shard_map/reduce_scatter | solution.py:217
  722.1 686.4 %reduce-scatter.24.cloned.1.call-start = ((), (), s32[]{:S(2)}) async-start(), calls=%async_computation.20 | async-start | bytes 23887872 | tf_op jit(solution)/shard_map/reduce_scatter | solution.py:216
  738.4 981.5 %reduce-scatter.18.cloned.1.call-start = ((), (), s32[]{:S(2)}) async-start(), calls=%async_computation.17 | async-start | bytes 35831808 | tf_op jit(solution)/shard_map/reduce_scatter | solution.py:201
  754.8 997.4 %reduce-scatter.30.cloned.1.call-start = ((), (), s32[]{:S(2)}) async-start(), calls=%async_computation.23 | async-start | bytes 663552
  756.9 1027.4 %reduce-scatter.28.cloned.1.call-start = ((), (), s32[]{:S(2)}) async-start(), calls=%async_computation.22 | async-start | bytes 663552
  758.9 1274.1 %all-reduce.5.cloned.1.call-start = ((), (), s32[]{:S(2)}) async-start(), calls=%async_computation.24 | async-start | bytes 25362432 | tf_op jit(solution)/shard_map/psum | solution.py:220
  (62 other events, 315.7 us)
Sparse Core Ops, SparseCore 0:
  9.7 35.0 all-gather.7
  46.4 143.6 all-gather.9
  191.8 77.7 all-gather.11
  271.1 32.7 all-gather.13
  305.3 99.4 all-gather.15
  406.3 98.8 all-gather.17
  677.4 31.2 reduce-scatter.13
  711.0 53.0 reduce-scatter.15
  766.4 58.8 reduce-scatter.21
  827.5 159.0 reduce-scatter.19
  989.1 208.5 reduce-scatter.25
  1199.9 208.5 reduce-scatter.23
  1411.0 308.9 reduce-scatter.17
  1722.7 29.5 reduce-scatter.29
  1754.9 29.3 reduce-scatter.27
  1789.0 243.9 all-reduce.4
where the time goes:
time: 2060 us; the launch traced here: 2050 us
  waiting for transfers between devices  1590 us (77%)
  matrix products  257 us (12%)
  local copies, waits for them, and re-layouts  89.9 us (4%)
  blocking collectives  66.8 us (3%)
  other arithmetic  34.3 us (2%)
    reduce_scatter x1, waiting for transfers between devices, body(): lax.psum_scatter(times_rows(cond, grad_modulation), 'fsdp', scatter_dimen...  311 us
    psum x1, waiting for transfers between devices, body(): lax.psum((shards[0], shards[1], grad_ada, shards[2], shards[3], shards[4]...  230 us
    reduce_scatter x1, waiting for transfers between devices, body(): lax.psum_scatter(grad_shrink, 'fsdp', scatter_dimension=0, tiled=True)  211 us
    reduce_scatter x1, waiting for transfers between devices, body(): lax.psum_scatter(grad_expand, 'fsdp', scatter_dimension=0, tiled=True)  211 us
    reduce_scatter x1, waiting for transfers between devices, body(): lax.psum_scatter(grad_triple, 'fsdp', scatter_dimension=0, tiled=True)  161 us
    all_gather x1, waiting for transfers between devices, body(): ada_full = lax.all_gather(ada_weight, 'fsdp', axis=1, tiled=True)  122 us
    all_gather x1, waiting for transfers between devices, body(): lax.all_gather(fc2_weight, 'fsdp', axis=0, tiled=True)  84.4 us
    dot_general x8, matrix products, times_rows(): lax.dot_general(left, right, (((0,), (0,)), ((), ())), preferred_element_...  71.7 us
  transfers between devices with their start and end apart: 16, of which 13 were waited for; matrix products, arithmetic and copies ran while one was open for 9% of the time, Pallas kernels for 0%

commit v1 on v0

v1 whole, which is shorter than its diff:
```python
from functools import partial
import math

import jax
import jax.numpy as jnp
from jax import lax
from jax.experimental import pallas as pl
from jax.experimental.pallas import tpu as pltpu
from jax.sharding import PartitionSpec as P

EPSILON = 1e-06
MESH = pl.DeviceIdType.MESH
QUARTERS = 4


def sinusoid(steps, entries):
    half = entries // 2
    freqs = jnp.exp(-math.log(10000.0) * jnp.arange(half, dtype=jnp.float32) / half)
    angles = steps.astype(jnp.float32)[:, None] * freqs[None, :]
    return jnp.concatenate([jnp.cos(angles), jnp.sin(angles)], axis=1)


def layer_norm(value):
    centered = value - jnp.mean(value, axis=-1, keepdims=True)
    return centered * lax.rsqrt(jnp.mean(centered * centered, axis=-1, keepdims=True) + EPSILON)


def norm_back(value, grad):
    _, pull = jax.vjp(layer_norm, value)
    return pull(grad)[0]


def matmul(left, right):
    return jnp.dot(left, right, preferred_element_type=jnp.float32)


def times_rows(left, right):
    return lax.dot_general(
        left, right, (((0,), (0,)), ((), ())), preferred_element_type=jnp.float32
    )


def times_back(left, right):
    return lax.dot_general(
        left, right, (((1,), (1,)), ((), ())), preferred_element_type=jnp.float32
    )


class Place:
    def __init__(self, ring):
        self.ring = ring
        d = lax.axis_index("dp")
        f = lax.axis_index("fsdp")
        self.d, self.f = d, f
        self.z = f // 2
        self.c = f % 2
        self.q = d % QUARTERS
        dx = d + 1 - 2 * (d % 2)
        dy = d + 2 - 4 * ((d // 2) % 2)
        self.qx = dx % QUARTERS
        self.qy = dy % QUARTERS
        self.qd = (self.qx + self.qy - self.q + QUARTERS) % QUARTERS
        self.core = (d, f + 1 - 2 * (f % 2))
        self.x = (dx, f)
        self.y = (dy, f)
        self.up = (d, ((self.z + 1) % ring) * 2 + self.c)
        self.down = (d, ((self.z + ring - 1) % ring) * 2 + self.c)

    def shard(self, back):
        return ((self.z + self.ring - back) % self.ring) * 2 + self.c

    def greet(self):
        barrier = pltpu.get_barrier_semaphore()
        near = [self.core, self.x, self.y, self.up, self.down]
        for other in near:
            pl.semaphore_signal(barrier, inc=1, device_id=other, device_id_type=MESH)
        pl.semaphore_wait(barrier, len(near))


def remote(src, dst, send, recv, device):
    return pltpu.make_async_remote_copy(
        src_ref=src, dst_ref=dst, send_sem=send, recv_sem=recv, device_id=device, device_id_type=MESH
    )


def cut(width):
    first = ((width // 128 + 1) // 2) * 128
    return (0, first), (first, width - first)


def view(ref, lead, q, width, part=None):
    start, size = (0, width) if part is None else part
    flat = ref.shape[-1] != width
    if flat:
        column = pl.multiple_of(q * width + start, 128)
        return ref.at[(*lead, slice(None), pl.ds(column, size))]
    return ref.at[(*lead, q, slice(None), pl.ds(start, size))]


def gather_kernel(ring, width, *refs):
    weights = 3
    shards, fulls = refs[:weights], refs[weights : 2 * weights]
    (own_sem, core_s, core_r, ring_s, ring_r, x_s, x_r, y_s, y_r, a_s, a_r, b_s, b_r) = refs[2 * weights :]
    at = Place(ring)
    part_a, part_b = cut(width)
    at.greet()
    sent, landed = [], []

    def go(copy):
        copy.start()
        sent.append(copy)
        return copy

    def ring_copy(k, step):
        index = at.shard(step - 1)
        if step == 1:
            src = view(shards[k], (), at.q, width)
        else:
            src = view(fulls[k], (index,), at.q, width)
        return remote(src, view(fulls[k], (index,), at.q, width), ring_s.at[k, step - 1], ring_r.at[k, step - 1], at.up)

    items = [(k, step) for k in range(weights) for step in range(1, ring)]
    rings = {items[0]: go(ring_copy(*items[0]))}
    locals_ = []
    for k in range(weights):
        copy = pltpu.make_async_copy(shards[k], fulls[k].at[at.f], own_sem.at[k])
        copy.start()
        locals_.append(copy)
        landed.append(go(remote(shards[k], fulls[k].at[at.f], core_s.at[k, 0], core_r.at[k, 0], at.core)))
    flights = {}
    for turn in range(len(items) + 2):
        if turn < len(items):
            k, step = items[turn]
            rings[k, step].wait_recv()
            if turn + 1 < len(items):
                rings[items[turn + 1]] = go(ring_copy(*items[turn + 1]))
            mine = view(fulls[k], (at.shard(step),), at.q, width)
            flights[turn] = (
                go(remote(mine, mine, x_s.at[k, step - 1], x_r.at[k, step - 1], at.x)),
                go(remote(mine, mine, y_s.at[k, step - 1], y_r.at[k, step - 1], at.y)),
            )
        if 0 <= turn - 1 < len(items):
            k, step = items[turn - 1]
            by_x, by_y = flights[turn - 1]
            by_x.wait_recv()
            half = view(fulls[k], (at.shard(step),), at.qx, width, part_a)
            first = go(remote(half, half, a_s.at[k, step - 1], a_r.at[k, step - 1], at.y))
            by_y.wait_recv()
            half = view(fulls[k], (at.shard(step),), at.qy, width, part_b)
            second = go(remote(half, half, b_s.at[k, step - 1], b_r.at[k, step - 1], at.x))
            flights[turn - 1] = (first, second)
        if 0 <= turn - 2 < len(items):
            k, step = items[turn - 2]
            for copy in flights[turn - 2]:
                copy.wait_recv()
            whole = fulls[k].at[at.shard(step)]
            landed.append(go(remote(whole, whole, core_s.at[k, step], core_r.at[k, step], at.core)))
    for copy in landed:
        copy.wait_recv()
    for copy in locals_:
        copy.wait()
    for copy in sent:
        copy.wait_send()


def gather_weights(shards, width, fsdp):
    ring = fsdp // 2
    dma = pltpu.SemaphoreType.DMA
    steps = dma((3, ring - 1))
    return pl.pallas_call(
        partial(gather_kernel, ring, width),
        out_shape=[jax.ShapeDtypeStruct((fsdp, *s.shape), s.dtype) for s in shards],
        in_specs=[pl.BlockSpec(memory_space=pl.ANY)] * 3,
        out_specs=[pl.BlockSpec(memory_space=pl.ANY)] * 3,
        scratch_shapes=[dma((3,)), dma((3, ring)), dma((3, ring))] + [steps] * 10,
        compiler_params=pltpu.CompilerParams(collective_id=0, has_side_effects=True),
        name="gather",
    )(*shards)


def reduce_kernel(ring, width, *refs):
    weights = 3
    terms, outs = refs[:weights], refs[weights : 2 * weights]
    (
        own, pair, first_a, first_b, second_a, second_b, hops, done,
        load, core_s, core_r, xa_s, xa_r, yb_s, yb_r, ya_s, ya_r, xb_s, xb_r, ring_s, ring_r,
        end_s, end_r, out_sem,
    ) = refs[2 * weights :]
    at = Place(ring)
    part_a, part_b = cut(width)
    cols_a, cols_b = pl.ds(*part_a), pl.ds(*part_b)
    rows = slice(None)
    sent = []

    def go(copy):
        copy.start()
        sent.append(copy)
        return copy

    at.greet()
    items = [(k, j) for k in range(weights) for j in range(ring)]
    loads, pairs = {}, {}
    other = 1 - 2 * at.c
    for k, j in items:
        back = (j + 1) % ring
        mine = at.shard(back)
        loads[k, j] = []
        for q in range(QUARTERS):
            copy = pltpu.make_async_copy(view(terms[k], (mine,), q, width), own.at[k, j, q], load.at[k, j, q])
            copy.start()
            loads[k, j].append(copy)
        pairs[k, j] = [
            go(remote(view(terms[k], (mine + other,), q, width), pair.at[k, j, q], core_s.at[k, j, q], core_r.at[k, j, q], at.core))
            for q in range(QUARTERS)
        ]
    flights, rings, ends = {}, {}, {}

    def stage_one(k, j):
        for q in range(QUARTERS):
            loads[k, j][q].wait()
            pairs[k, j][q].wait_recv()
            own[k, j, q] = own[k, j, q] + pair[k, j, q]
        flights[k, j] = [
            go(remote(own.at[k, j, at.qx, rows, cols_a], first_a.at[k, j, 0], xa_s.at[k, j, 0], xa_r.at[k, j, 0], at.x)),
            go(remote(own.at[k, j, at.qd, rows, cols_a], first_a.at[k, j, 1], xa_s.at[k, j, 1], xa_r.at[k, j, 1], at.x)),
            go(remote(own.at[k, j, at.qy, rows, cols_b], first_b.at[k, j, 0], yb_s.at[k, j, 0], yb_r.at[k, j, 0], at.y)),
            go(remote(own.at[k, j, at.qd, rows, cols_b], first_b.at[k, j, 1], yb_s.at[k, j, 1], yb_r.at[k, j, 1], at.y)),
        ]

    def stage_two(k, j):
        one, two, three, four = flights[k, j]
        two.wait_recv()
        own[k, j, at.qy, :, cols_a] = own[k, j, at.qy, :, cols_a] + first_a[k, j, 1]
        next_a = go(remote(own.at[k, j, at.qy, rows, cols_a], second_a.at[k, j], ya_s.at[k, j], ya_r.at[k, j], at.y))
        four.wait_recv()
        own[k, j, at.qx, :, cols_b] = own[k, j, at.qx, :, cols_b] + first_b[k, j, 1]
        next_b = go(remote(own.at[k, j, at.qx, rows, cols_b], second_b.at[k, j], xb_s.at[k, j], xb_r.at[k, j], at.x))
        one.wait_recv()
        own[k, j, at.q, :, cols_a] = own[k, j, at.q, :, cols_a] + first_a[k, j, 0]
        three.wait_recv()
        own[k, j, at.q, :, cols_b] = own[k, j, at.q, :, cols_b] + first_b[k, j, 0]
        flights[k, j] = [next_a, next_b]

    def stage_three(k, j):
        for copy in flights[k, j]:
            copy.wait_recv()
        own[k, j, at.q, :, cols_a] = own[k, j, at.q, :, cols_a] + second_a[k, j]
        own[k, j, at.q, :, cols_b] = own[k, j, at.q, :, cols_b] + second_b[k, j]
        if j > 0:
            rings[k, j - 1].wait_recv()
            own[k, j, at.q] = own[k, j, at.q] + hops[k, j - 1]
        if j < ring - 1:
            rings[k, j] = go(remote(own.at[k, j, at.q], hops.at[k, j], ring_s.at[k, j], ring_r.at[k, j], at.up))
            return
        done[k, at.q] = own[k, j, at.q]
        mine = done.at[k, at.q]
        ends[k] = [
            go(remote(mine, mine, end_s.at[k, 0], end_r.at[k, 0], at.x)),
            go(remote(mine, mine, end_s.at[k, 1], end_r.at[k, 1], at.y)),
        ]

    def stage_four(k):
        by_x, by_y = ends[k]
        by_x.wait_recv()
        half = done.at[k, at.qx, rows, cols_a]
        first = go(remote(half, half, end_s.at[k, 2], end_r.at[k, 2], at.y))
        by_y.wait_recv()
        half = done.at[k, at.qy, rows, cols_b]
        second = go(remote(half, half, end_s.at[k, 3], end_r.at[k, 3], at.x))
        ends[k] = [first, second]

    outgoing = []

    def stage_five(k):
        for copy in ends[k]:
            copy.wait_recv()
        copy = pltpu.make_async_copy(done.at[k], outs[k], out_sem.at[k])
        copy.start()
        outgoing.append(copy)

    for turn in range(len(items) + 4):
        if turn < len(items):
            stage_one(*items[turn])
        if 0 <= turn - 1 < len(items):
            stage_two(*items[turn - 1])
        if 0 <= turn - 2 < len(items):
            stage_three(*items[turn - 2])
        if 0 <= turn - 3 < len(items) and items[turn - 3][1] == ring - 1:
            stage_four(items[turn - 3][0])
        if 0 <= turn - 4 < len(items) and items[turn - 4][1] == ring - 1:
            stage_five(items[turn - 4][0])
    for copy in outgoing:
        copy.wait()
    for copy in sent:
        copy.wait_send()


def reduce_terms(terms, rows, width, fsdp):
    ring = fsdp // 2
    dma = pltpu.SemaphoreType.DMA
    low = jnp.bfloat16
    (_, size_a), (_, size_b) = cut(width)
    vmem = pltpu.VMEM
    scratch = [
        vmem((3, ring, QUARTERS, rows, width), low),
        vmem((3, ring, QUARTERS, rows, width), low),
        vmem((3, ring, 2, rows, size_a), low),
        vmem((3, ring, 2, rows, size_b), low),
        vmem((3, ring, rows, size_a), low),
        vmem((3, ring, rows, size_b), low),
        vmem((3, ring - 1, rows, width), low),
        vmem((3, QUARTERS, rows, width), low),
    ]
    sems = (
        [dma((3, ring, QUARTERS))] * 3
        + [dma((3, ring, 2))] * 4
        + [dma((3, ring))] * 4
        + [dma((3, ring - 1))] * 2
        + [dma((3, 4))] * 2
        + [dma((3,))]
    )
    return pl.pallas_call(
        partial(reduce_kernel, ring, width),
        out_shape=[jax.ShapeDtypeStruct((QUARTERS, rows, width), low)] * 3,
        in_specs=[pl.BlockSpec(memory_space=pl.ANY)] * 3,
        out_specs=[pl.BlockSpec(memory_space=pl.ANY)] * 3,
        scratch_shapes=scratch + sems,
        compiler_params=pltpu.CompilerParams(
            collective_id=1, has_side_effects=True, vmem_limit_bytes=60 * 2**20
        ),
        name="reduce",
    )(*terms)


def body(
    dp,
    fsdp,
    tokens,
    timesteps,
    labels,
    head_mask,
    keep_mask,
    cotangent,
    time_weight,
    class_table,
    ada_weight,
    head_router,
    qkv_weight,
    proj_weight,
    fc1_weight,
    fc2_weight,
    token_router,
):
    images, seq, width = tokens.shape
    heads = head_mask.shape[1]
    size = width // heads
    scale = size ** (-0.5)
    count = images * seq
    rows = qkv_weight.shape[0]
    hidden = fc1_weight.shape[1]
    entries = time_weight.shape[0] * fsdp
    group = images * fsdp
    me_dp, me_fsdp = lax.axis_index("dp"), lax.axis_index("fsdp")
    everyone = ("dp", "fsdp")

    joint_full, fc1_full, fc2_full = gather_weights(
        [
            jnp.concatenate([qkv_weight, proj_weight], axis=1),
            fc1_weight,
            fc2_weight.reshape(QUARTERS, rows, width),
        ],
        width,
        fsdp,
    )
    joint_full = joint_full.reshape(width, 4 * width)
    triple, merger = joint_full[:, : 3 * width], joint_full[:, 3 * width :]
    expand = fc1_full.reshape(width, hidden)
    shrink = fc2_full.reshape(hidden, width)

    asked = lax.all_gather(jnp.stack([timesteps, labels], axis=1), everyone, axis=0, tiled=True)
    all_steps, all_labels = asked[:, 0], asked[:, 1]
    packed = jnp.concatenate(
        [time_weight.reshape(-1), head_router.reshape(-1), token_router.reshape(-1)]
    )
    parts = lax.all_gather(packed, "fsdp", axis=0, tiled=False)
    cut_one = time_weight.size
    cut_two = cut_one + head_router.size
    time_full = parts[:, :cut_one].reshape(entries, width)
    chooser = parts[:, cut_one:cut_two].reshape(width, heads)
    picker = parts[:, cut_two:].reshape(width, 1)

    table_rows = jnp.arange(class_table.shape[0], dtype=jnp.int32)
    all_rows = (all_labels[:, None] == table_rows[None, :]).astype(jnp.bfloat16)
    group_rows = lax.dynamic_slice_in_dim(all_rows, me_dp * group, group, axis=0)
    picked = matmul(group_rows, class_table).astype(jnp.bfloat16)
    class_part = lax.all_to_all(picked, "fsdp", split_axis=0, concat_axis=1, tiled=True)
    all_embedded = sinusoid(all_steps, entries).astype(jnp.bfloat16)
    embedded = sinusoid(timesteps, entries).astype(jnp.bfloat16)
    pre_cond = matmul(embedded, time_full) + class_part.astype(jnp.float32)
    cond = jax.nn.silu(pre_cond).astype(jnp.bfloat16)
    all_cond = lax.all_gather(cond, everyone, axis=0, tiled=True)
    group_cond = lax.dynamic_slice_in_dim(all_cond, me_dp * group, group, axis=0)
    modulation = lax.all_to_all(
        matmul(group_cond, ada_weight), "fsdp", split_axis=0, concat_axis=1, tiled=True
    )
    shift_one, scale_one, gate_one, shift_two, scale_two, gate_two = jnp.split(
        modulation[:, None, :], 6, axis=2
    )
    router_sig = jax.nn.sigmoid(matmul(cond, chooser))
    mask_float = head_mask.astype(jnp.float32)
    head_gates = mask_float * router_sig
    inputs = tokens.astype(jnp.float32)
    normed_one = layer_norm(inputs)
    flat_one = (
        (normed_one * (1.0 + scale_one) + shift_one).astype(jnp.bfloat16).reshape(count, width)
    )
    joint = matmul(flat_one, triple).astype(jnp.bfloat16)
    query = joint[:, :width].reshape(images, seq, heads, size)
    keys = joint[:, width : 2 * width].reshape(images, seq, heads, size)
    values = joint[:, 2 * width :].reshape(images, seq, heads, size)
    raw = jnp.einsum("ishe,ithe->ihst", query, keys, preferred_element_type=jnp.float32) * scale
    peak = jnp.max(raw, axis=-1, keepdims=True)
    expo = jnp.exp(raw - peak)
    total = jnp.sum(expo, axis=-1, keepdims=True)
    log_total = peak + jnp.log(total)
    probs_low = (expo / total).astype(jnp.bfloat16)
    attended = jnp.einsum("ihst,ithe->ishe", probs_low, values, preferred_element_type=jnp.float32)
    mixed = (attended * head_gates[:, None, :, None]).astype(jnp.bfloat16).reshape(count, width)
    attn = matmul(mixed, merger).reshape(images, seq, width)
    middle = inputs + gate_one * attn
    normed_two = layer_norm(middle)
    flat_two = (
        (normed_two * (1.0 + scale_two) + shift_two).astype(jnp.bfloat16).reshape(count, width)
    )
    rate = jax.nn.sigmoid(matmul(flat_two, picker)).reshape(images, seq, 1)
    upward = matmul(flat_two, expand)
    active = jax.nn.gelu(upward, approximate=True).astype(jnp.bfloat16)
    downward = matmul(active, shrink).reshape(images, seq, width)
    kept = keep_mask.astype(jnp.float32)[:, :, None]
    kept_rate = kept * rate
    output = (middle + gate_two * kept_rate * downward).astype(jnp.bfloat16)
    grad_out = cotangent.astype(jnp.float32)
    grad_gate_two = jnp.sum(grad_out * kept_rate * downward, axis=1)
    grad_down = (grad_out * gate_two * kept_rate).astype(jnp.bfloat16).reshape(count, width)
    grad_rate = jnp.sum(grad_out * gate_two * downward, axis=-1, keepdims=True) * kept
    grad_logit = (grad_rate * rate * (1.0 - rate)).astype(jnp.bfloat16).reshape(count, 1)
    grad_shrink = times_rows(active, grad_down).astype(jnp.bfloat16)
    _, gelu_pull = jax.vjp(partial(jax.nn.gelu, approximate=True), upward)
    grad_up = gelu_pull(times_back(grad_down, shrink))[0].astype(jnp.bfloat16)
    grad_expand = times_rows(flat_two, grad_up).astype(jnp.bfloat16)
    grad_picker = times_rows(grad_logit, flat_two)
    grad_h_two = (times_back(grad_up, expand) + times_back(grad_logit, picker)).reshape(
        images, seq, width
    )
    grad_shift_two = jnp.sum(grad_h_two, axis=1)
    grad_scale_two = jnp.sum(grad_h_two * normed_two, axis=1)
    grad_middle = grad_out + norm_back(middle, grad_h_two * (1.0 + scale_two))
    grad_gate_one = jnp.sum(grad_middle * attn, axis=1)
    grad_attn = (grad_middle * gate_one).astype(jnp.bfloat16).reshape(count, width)
    grad_merger = times_rows(mixed, grad_attn).astype(jnp.bfloat16)
    grad_mixed = (
        times_back(grad_attn, merger).astype(jnp.bfloat16).reshape(images, seq, heads, size)
    )
    grad_gates = jnp.sum(grad_mixed * attended, axis=(1, 3))
    grad_router = (grad_gates * mask_float * router_sig * (1.0 - router_sig)).astype(jnp.bfloat16)
    grad_attended = (grad_mixed * head_gates[:, None, :, None]).astype(jnp.bfloat16)
    again_raw = (
        jnp.einsum("ishe,ithe->ihst", query, keys, preferred_element_type=jnp.float32) * scale
    )
    probs = jnp.exp(again_raw - log_total)
    grad_values = jnp.einsum(
        "ihst,ishe->ithe",
        probs.astype(jnp.bfloat16),
        grad_attended,
        preferred_element_type=jnp.float32,
    )
    grad_probs = jnp.einsum(
        "ishe,ithe->ihst", grad_attended, values, preferred_element_type=jnp.float32
    )
    inner = jnp.sum(grad_probs * probs, axis=-1, keepdims=True)
    grad_scores = (probs * (grad_probs - inner) * scale).astype(jnp.bfloat16)
    grad_query = jnp.einsum(
        "ihst,ithe->ishe", grad_scores, keys, preferred_element_type=jnp.float32
    )
    grad_keys = jnp.einsum(
        "ihst,ishe->ithe", grad_scores, query, preferred_element_type=jnp.float32
    )
    grad_joint = jnp.concatenate(
        [
            grad_query.reshape(count, width),
            grad_keys.reshape(count, width),
            grad_values.reshape(count, width),
        ],
        axis=1,
    ).astype(jnp.bfloat16)
    grad_triple = times_rows(flat_one, grad_joint).astype(jnp.bfloat16)
    grad_h_one = times_back(grad_joint, triple).reshape(images, seq, width)
    grad_shift_one = jnp.sum(grad_h_one, axis=1)
    grad_scale_one = jnp.sum(grad_h_one * normed_one, axis=1)
    grad_inputs = grad_middle + norm_back(inputs, grad_h_one * (1.0 + scale_one))
    grad_modulation = jnp.concatenate(
        [
            grad_shift_one,
            grad_scale_one,
            grad_gate_one,
            grad_shift_two,
            grad_scale_two,
            grad_gate_two,
        ],
        axis=1,
    ).astype(jnp.bfloat16)

    sums = reduce_terms(
        [
            jnp.concatenate([grad_triple, grad_merger], axis=1).reshape(fsdp, rows, 4 * width),
            grad_expand.reshape(fsdp, rows, hidden),
            grad_shrink.reshape(fsdp, QUARTERS, rows, width),
        ],
        rows,
        width,
        fsdp,
    )
    if dp > QUARTERS:
        parts = list(sums)
        for hop in range(QUARTERS, dp, QUARTERS):
            pairs = [(i, (i + hop) % dp) for i in range(dp)]
            parts = [
                part.astype(jnp.float32) + lax.ppermute(s, "dp", pairs).astype(jnp.float32)
                for part, s in zip(parts, sums)
            ]
        sums = parts
    sums = [s.astype(jnp.float32) for s in sums]
    sum_triple = jnp.concatenate([sums[0][0], sums[0][1], sums[0][2]], axis=1)
    sum_merger = sums[0][3]
    sum_expand = jnp.concatenate([sums[1][i] for i in range(QUARTERS)], axis=1)
    sum_shrink = sums[2].reshape(QUARTERS * rows, width)

    group_grad = lax.all_to_all(grad_modulation, "fsdp", split_axis=1, concat_axis=0, tiled=True)
    all_grad = lax.all_gather(group_grad, "dp", axis=0, tiled=True)
    sum_ada = times_rows(all_cond, all_grad)
    grad_cond = lax.psum_scatter(
        times_back(group_grad, ada_weight), "fsdp", scatter_dimension=0, tiled=True
    )
    grad_cond = grad_cond + times_back(grad_router, chooser)
    _, silu_pull = jax.vjp(jax.nn.silu, pre_cond)
    grad_pre = silu_pull(grad_cond)[0].astype(jnp.bfloat16)
    both = lax.all_gather(
        jnp.concatenate([grad_pre, grad_router], axis=1), everyone, axis=0, tiled=True
    )
    all_pre, all_router = both[:, :width], both[:, width:]
    sum_time = times_rows(
        lax.dynamic_slice_in_dim(all_embedded, me_fsdp * (entries // fsdp), entries // fsdp, axis=1),
        all_pre,
    )
    sum_table = times_rows(
        all_rows, lax.dynamic_slice_in_dim(all_pre, me_fsdp * rows, rows, axis=1)
    )
    sum_chooser = times_rows(
        lax.dynamic_slice_in_dim(all_cond, me_fsdp * rows, rows, axis=1), all_router
    )
    all_picker = lax.all_gather(grad_picker, everyone, axis=0, tiled=True)
    sum_picker = lax.dynamic_slice_in_dim(
        jnp.sum(all_picker, axis=0), me_fsdp * rows, rows, axis=0
    )[:, None]
    return (
        output,
        grad_inputs,
        sum_time,
        sum_table,
        sum_ada,
        sum_chooser,
        sum_triple,
        sum_merger,
        sum_expand,
        sum_shrink,
        sum_picker,
    )


def solution(mesh):
    images = P(("dp", "fsdp"), None, None)
    pairs = P(("dp", "fsdp"), None)
    single = P(("dp", "fsdp"))
    by_row, by_column = P("fsdp", None), P(None, "fsdp")
    in_specs = (
        images, single, single, pairs, pairs, images,
        by_row, by_column, by_column, by_row, by_row, by_row, by_row, by_row, by_row,
    )
    out_specs = (
        images, images,
        by_row, by_column, by_column, by_row, by_row, by_row, by_row, by_row, by_row,
    )
    return jax.shard_map(
        partial(body, mesh.shape["dp"], mesh.shape["fsdp"]),
        mesh=mesh, in_specs=in_specs, out_specs=out_specs, check_vma=False,
    )
```

time: 2060 us -> 933 us (0.45)
  waiting for transfers between devices: 1590 us -> 52 us
  Pallas kernels: 0 us -> 313 us
  blocking collectives: 66.8 us -> 174 us
  matrix products: 257 us -> 226 us
    reduce_scatter x7 -> x0, waiting for transfers between devices: 961 us -> none  [the longest x1 311 us: body(): lax.psum_scatter(times_rows(cond, grad_modulation), 'fsdp', scatter_dimen...]
    all_gather x6 -> x0, waiting for transfers between devices: 336 us -> none  [the longest x1 122 us: body(): ada_full = lax.all_gather(ada_weight, 'fsdp', axis=1, tiled=True)]
    pallas_call x0 -> x2, Pallas kernels: none -> 313 us  [the longest x1 186 us: reduce_terms(): pl.pallas_call(partial(reduce_kernel, ring, width), out_shape=[jax.ShapeD...]
    psum x1 -> x0, waiting for transfers between devices: 230 us -> none  [body(): lax.psum((shards[0], shards[1], grad_ada, shards[2], shards[3], shards[4]...]
    all_gather x2 -> x5, blocking collectives: 31 us -> 174 us  [the longest x1 43.3 us: body(): lax.all_gather(jnp.stack([timesteps, labels], axis=1), everyone, axis=0,...]
    dot_general x8 -> x9, matrix products: 71.7 us -> 44.9 us  [times_rows(): lax.dot_general(left, right, (((0,), (0,)), ((), ())), preferred_element_...]
    unnamed x18 -> x4, waiting for transfers between devices: 60.7 us -> 46.5 us
  transfers between devices with their start and end apart: 16 -> 5, of which waited for: 13 -> 2; matrix products, arithmetic and copies ran while one was open for 9% -> 3% of each run, Pallas kernels for 0% -> 14%
where the time goes in v1:
time: 933 us; the launch traced here: 926 us
  Pallas kernels  313 us (34%)
  matrix products  226 us (24%)
  blocking collectives  174 us (19%)
  local copies, waits for them, and re-layouts  90.4 us (10%)
  waiting for transfers between devices  52 us (6%)
  other arithmetic  44.9 us (5%)
  between operations  16.7 us (2%)
  starting transfers between devices  10.3 us (1%)
    pallas_call x1, Pallas kernels, reduce_terms(): pl.pallas_call(partial(reduce_kernel, ring, width), out_shape=[jax.ShapeD...  186 us
    pallas_call x1, Pallas kernels, gather_weights(): pl.pallas_call(partial(gather_kernel, ring, width), out_shape=[jax.ShapeD...  127 us
    dot_general x9, matrix products, matmul(): return jnp.dot(left, right, preferred_element_type=jnp.float32)  63.1 us
    dot_general x6, matrix products, times_back(): lax.dot_general(left, right, (((1,), (1,)), ((), ())), preferred_element_...  50.7 us
    unnamed x4, waiting for transfers between devices  46.5 us
    dot_general x9, matrix products, times_rows(): lax.dot_general(left, right, (((0,), (0,)), ((), ())), preferred_element_...  44.9 us
    all_gather x1, blocking collectives, body(): lax.all_gather(jnp.stack([timesteps, labels], axis=1), everyone, axis=0,...  43.3 us
    all_gather x1, blocking collectives, body(): lax.all_gather(jnp.concatenate([grad_pre, grad_router], axis=1), everyone...  43.3 us
  transfers between devices with their start and end apart: 5, of which 2 were waited for; matrix products, arithmetic and copies ran while one was open for 3% of the time, Pallas kernels for 14%

profile of v1, /device:TPU:0, one launch (start us, length us, event | category | flops | bytes accessed | tf_op | source)
XLA Modules:
  0.0 926.4 jit_solution(15574987357094101942)
XLA Ops:
  8.0 43.3 %all-gather.2 = s32[32,3,2]{1,2,0:T(2,128)S(1)} all-gather(s32[1,3,2]{1,2,0:T(2,128)S(1)} %add_bitcast_fusion), channel_id=1, replica_groups=mesh['dp'=4,'fsdp'=8] {'dp','fsdp'}, dimensions={0}, use_global_device_ids=true | all-gather | bytes 792 | tf_op jit(solution)/shard_map/all_gather | solution.py:380
  71.2 126.6 %gather.1 = (bf16[8,144,4608]{2,1,0:T(8,128)(2,1)}, bf16[8,144,4608]{2,1,0:T(8,128)(2,1)}, bf16[8,4,144,1152]{3,2,1,0:T(8,128)(2,1)}) custom-call(bf16[144,4608]{1,0:T(8,128)(2,1)} %pad_maximum_fusion.3.refs_0_, bf16[144,4608]{1,0:T(8,128)(2,1)} %refs_1_.1, bf16[4,144,1152]{2,1,0:T(8,128)(2,1)} %bitcast.175), custom_call_target="tpu_custom_call" | custom-call | tf_op jit(solution)/shard_map/gather/pallas_call | solution.py:170
  200.7 38.9 %all-gather.3 = bf16[32,3,1152]{2,1,0:T(4,128)(2,1)S(1)} all-gather(bf16[1,3,1152]{2,1,0:T(4,128)(2,1)S(1)} %fusion.115), channel_id=1, replica_groups=mesh['dp'=4,'fsdp'=8] {'dp','fsdp'}, dimensions={0}, use_global_device_ids=true | all-gather | bytes 228096 | tf_op jit(solution)/shard_map/all_gather | solution.py:401
  245.8 5.4 all-to-all-done.1
  254.2 10.3 %fusion.23 = bf16[768,3456]{1,0:T(8,128)(2,1)S(1)} fusion(bf16[768,1152]{1,0:T(8,128)(2,1)S(1)} %bitcast.169, bf16[1152,4608]{1,0:T(8,128)(2,1)} %bitcast.182), kind=kOutput, calls=%fused_computation.31 | convolution fusion | flops 6117949440 | bytes 15040512 | tf_op jit(solution)/shard_map/dot_general | solution.py:34
  267.1 7.6 reshape.295
  274.8 4.7 copy.100
  279.4 7.6 reshape.294
  291.6 7.6 reshape.293
  299.3 4.8 copy.101
  320.1 6.6 fusion.118
  332.4 15.7 %fusion.121 = f32[768,4608]{1,0:T(8,128)} fusion(bf16[768,1152]{1,0:T(8,128)(2,1)S(1)} %bitcast.171, bf16[4608,1152]{1,0:T(8,128)(2,1)} %bitcast.188), kind=kOutput, calls=%fused_computation.201 | convolution fusion | flops 8153726976 | bytes 26542080 | tf_op jit(solution)/shard_map/dot_general | solution.py:44
  348.1 26.0 %fusion.7 = (bf16[768,4608]{1,0:T(8,128)(2,1)}, bf16[768,4608]{1,0:T(8,128)(2,1)}) fusion(f32[768,4608]{1,0:T(8,128)} %fusion.121, bf16[768,1152]{1,0:T(8,128)(2,1)} %bitcast.154, bf16[1152,4608]{1,0:T(8,128)(2,1)} %bitcast.186), kind=kOutput, calls=%fused_computation.12 | convolution fusion | flops 8231583744 | bytes 40697856 | tf_op jit(solution)/shard_map/dot_general | solution.py:34
  374.0 16.9 %fusion.55 = (bf16[3,1152]{1,0:T(4,128)(2,1)}, f32[3,256]{1,0:T(4,128)S(1)}, bf16[3,256,1152]{2,1,0:T(8,128)(2,1)}) fusion(bf16[3,256,1152]{2,1,0:T(8,128)(2,1)} %param.20, f32[3,256]{1,0:T(4,128)S(1)} %convert_multiply_fusion.2, f32[3,1152]{1,0:T(4,128)S(1)} %get-tuple-element.51, f32[3,256,1152]{2,1,0:T(8,128)S(1)} %copy-done.7, ...), kind=kOutput, calls=%fused_computation.65 | convolution fusion | flops 8163454976 | bytes 24799488 | tf_op jit(solution)/shard_map/dot_general | solution.py:34
  391.0 14.0 %convolution_add_fusion = f32[768,1152]{1,0:T(8,128)S(1)} fusion(bf16[768,4608]{1,0:T(8,128)(2,1)} %get-tuple-element.35, bf16[1152,4608]{1,0:T(8,128)(2,1)} %bitcast.187, f32[1152]{0:T(1024)S(1)} %convert.60, f32[768]{0:T(1024)S(1)} %reshape.264), kind=kOutput, calls=%fused_computation.56 | convolution fusion | flops 8155496448 | bytes 21241344 | tf_op jit(solution)/shard_map/dot_general | solution.py:44
  412.1 6.3 fusion.58
  418.3 8.0 reshape.296
  426.3 6.1 copy.105
  432.4 9.1 fusion.73
  441.6 8.5 convert_bitcast_fusion
  450.0 20.3 %convert_bitcast_fusion.1 = bf16[3,256,16,72]{1,3,2,0:T(8,128)(2,1)} fusion(bf16[3,256,16,72]{1,3,2,0:T(8,128)(2,1)} %copy.99, f32[3,16,256,256]{2,3,1,0:T(8,128)} %fusion.73, f32[3,16,256,256]{2,3,1,0:T(8,128)} %copy-done.1, f32[3,16,256]{2,1,0:T(8,128)S(1)} %copy-done.45), kind=kOutput, calls=%fused_computation.91 | convolution fusion | flops 482193664 | bytes 28753920 | tf_op jit(solution)/shard_map/ihst,ishe->ithe/dot_general | solution.py:485
  470.3 20.6 %convert_bitcast_fusion.2 = bf16[3,256,16,72]{1,3,2,0:T(8,128)(2,1)} fusion(bf16[3,256,16,72]{1,3,2,0:T(8,128)(2,1)} %copy.100, f32[3,16,256,256]{2,3,1,0:T(8,128)} %fusion.73, f32[3,16,256,256]{2,3,1,0:T(8,128)} %copy-done.1, f32[3,16,256]{2,1,0:T(8,128)S(1)} %copy-done.45), kind=kOutput, calls=%fused_computation.92 | convolution fusion | flops 482193664 | bytes 28753920 | tf_op jit(solution)/shard_map/ihst,ithe->ishe/dot_general | solution.py:482
  490.9 15.0 %convolution_convert_fusion = bf16[4608,1152]{1,0:T(8,128)(2,1)} fusion(bf16[768,4608]{1,0:T(8,128)(2,1)} %get-tuple-element.36, bf16[768,1152]{1,0:T(8,128)(2,1)} %bitcast.172), kind=kOutput, calls=%fused_computation.3 | convolution fusion | flops 8159035392 | bytes 19464192 | tf_op jit(solution)/shard_map/dot_general | solution.py:38
  505.9 14.2 %convolution_convert_fusion.1 = bf16[1152,4608]{1,0:T(8,128)(2,1)} fusion(bf16[768,1152]{1,0:T(8,128)(2,1)S(1)} %bitcast.155, bf16[768,4608]{1,0:T(8,128)(2,1)} %get-tuple-element.35), kind=kOutput, calls=%fused_computation.4 | convolution fusion | flops 8159035392 | bytes 19464192 | tf_op jit(solution)/shard_map/dot_general | solution.py:38
  527.7 7.3 convolution_convert_fusion.2
  535.1 12.6 %fusion.19 = f32[768,1152]{1,0:T(8,128)} fusion(bf16[768,3456]{0,1:T(8,128)(2,1)S(1)} %constant_dynamic-update-slice_fusion, bf16[1152,4608]{1,0:T(8,128)(2,1)} %bitcast.185), kind=kOutput, calls=%fused_computation.27 | convolution fusion | flops 6115295232 | bytes 16809984 | tf_op jit(solution)/shard_map/dot_general | solution.py:44
  551.6 4.8 pad_maximum_fusion
  556.4 186.3 %reduce.5 = (bf16[4,144,1152]{2,1,0:T(8,128)(2,1)}, bf16[4,144,1152]{2,1,0:T(8,128)(2,1)}, bf16[4,144,1152]{2,1,0:T(8,128)(2,1)}) custom-call(bf16[8,144,4608]{2,1,0:T(8,128)(2,1)} %bitcast.149, bf16[8,144,4608]{2,1,0:T(8,128)(2,1)} %bitcast.159, bf16[8,4,144,1152]{3,2,1,0:T(8,128)(2,1)} %bitcast.158), custom_call_target="tpu_custom_call" | custom-call | tf_op jit(solution)/shard_map/reduce/pallas_call | solution.py:322
  772.4 40.7 %all-gather.5 = f32[32,1,1152]{2,1,0:T(1,128)S(1)} all-gather(f32[1,1,1152]{2,1,0:T(1,128)S(1)} %convolution_bitcast_fusion), channel_id=3, replica_groups=mesh['dp'=4,'fsdp'=8] {'dp','fsdp'}, dimensions={0}, use_global_device_ids=true | all-gather | bytes 152064 | tf_op jit(solution)/shard_map/all_gather | solution.py:561
  813.9 7.6 all_gather.26
  825.3 46.5 %all-reduce.7.cloned.1.call-done = f32[24,1152]{1,0:T(8,128)} async-done(((f32[24,1152]{1,0:T(8,128)}), f32[24,1152]{1,0:T(8,128)}) %all-reduce.7.cloned.1.call-update) | async-done | bytes 110608
  872.9 43.3 %all-gather.4 = bf16[32,3,1168]{2,1,0:T(4,128)(2,1)S(1)} all-gather(bf16[1,3,1168]{2,1,0:T(4,128)(2,1)S(1)} %maximum_bitcast_fusion), channel_id=1, replica_groups=mesh['dp'=4,'fsdp'=8] {'dp','fsdp'}, dimensions={0}, use_global_device_ids=true | all-gather | bytes 231264 | tf_op jit(solution)/shard_map/all_gather | solution.py:547
  (257 shorter events, 116.7 us)
Async XLA Ops:
  7.2 232.6 %copy-start = (bf16[1152,864]{0,1:T(8,128)(2,1)S(1)}, bf16[1152,864]{0,1:T(8,128)(2,1)}, u32[]{:S(2)}) copy-start(bf16[1152,864]{0,1:T(8,128)(2,1)} %param.23) | copy-start | bytes 5971972
  7.2 61.2 %copy-start.42 = (bf16[144,1152]{1,0:T(8,128)(2,1)S(1)}, bf16[144,1152]{1,0:T(8,128)(2,1)}, u32[]{:S(2)}) copy-start(bf16[144,1152]{1,0:T(8,128)(2,1)} %param.26) | copy-start | bytes 995332
  53.8 144.0 %all-to-all-start = ((bf16[8,2,216]{2,1,0:T(2,128)(2,1)}), bf16[8,2,216]{2,1,0:T(2,128)(2,1)S(1)}, u32[]{:S(2)}, u32[]{:S(2)}) async-start(bf16[8,2,216]{2,1,0:T(2,128)(2,1)} %reshape.299), calls=%async_computation | async-start | bytes 16384 | tf_op jit(solution)/shard_map/all_to_all | solution.py:396
  57.2 140.9 %all-reduce.5.cloned.1.call-start = ((), (), s32[]{:S(2)}) async-start(), calls=%async_computation.3 | async-start | bytes 1261568
  66.2 185.2 %copy-start.46 = (f32[3,256]{1,0:T(4,128)}, f32[3,256]{1,0:T(4,128)S(1)}, u32[]{:S(2)}) copy-start(f32[3,256]{1,0:T(4,128)S(1)} %broadcast_multiply_fusion.1) | copy-start | bytes 9220
  68.3 129.6 %copy-start.54 = (f32[3,256]{1,0:T(4,128)}, f32[3,256]{1,0:T(4,128)S(1)}, u32[]{:S(2)}) copy-start(f32[3,256]{1,0:T(4,128)S(1)} %fusion.52) | copy-start | bytes 9220
  68.4 183.0 %copy-start.52 = (f32[3,256]{1,0:T(4,128)}, f32[3,256]{1,0:T(4,128)S(1)}, u32[]{:S(2)}) copy-start(f32[3,256]{1,0:T(4,128)S(1)} %fusion.92) | copy-start | bytes 9220
  199.9 45.1 %copy-start.62 = (s32[3,16]{1,0:T(4,128)S(1)}, s32[3,16]{1,0:T(4,128)}, u32[]{:S(2)}) copy-start(s32[3,16]{1,0:T(4,128)} %param.18) | copy-start | bytes 580
  200.7 53.5 %copy-start.50 = (f32[3,1152]{1,0:T(4,128)}, f32[3,1152]{1,0:T(4,128)S(1)}, u32[]{:S(2)}) copy-start(f32[3,1152]{1,0:T(4,128)S(1)} %convolution_add_fusion.2) | copy-start | bytes 41476
  239.8 14.4 %copy-start.35 = (bf16[96,1152]{1,0:T(8,128)(2,1)}, bf16[96,1152]{1,0:T(8,128)(2,1)S(1)}, u32[]{:S(2)}) copy-start(bf16[96,1152]{1,0:T(8,128)(2,1)S(1)} %reshape.276) | copy-start | bytes 663556
  241.2 10.0 %all-to-all-start.1 = ((f32[8,3,864]{2,1,0:T(4,128)}), f32[8,3,864]{2,1,0:T(4,128)S(1)}, u32[]{:S(2)}, u32[]{:S(2)}) async-start(f32[8,3,864]{2,1,0:T(4,128)} %all_to_all.36), calls=%async_computation.1 | async-start | bytes 229376 | tf_op jit(solution)/shard_map/all_to_all | solution.py:403
  245.0 6.2 copy-start.43
  251.4 13.2 %copy-start.40 = (f32[3,1152]{1,0:T(4,128)}, f32[3,1152]{1,0:T(4,128)S(1)}, u32[]{:S(2)}) copy-start(f32[3,1152]{1,0:T(4,128)S(1)} %get-tuple-element.55) | copy-start | bytes 41476
  254.2 10.4 %copy-start.30 = (bf16[3,256,1152]{2,1,0:T(8,128)(2,1)}, bf16[3,256,1152]{2,1,0:T(8,128)(2,1)S(1)}, u32[]{:S(2)}) copy-start(bf16[3,256,1152]{2,1,0:T(8,128)(2,1)S(1)} %fusion.48) | copy-start | bytes 5308420
  332.4 15.7 %copy-start.32 = (bf16[3,256,1152]{2,1,0:T(8,128)(2,1)}, bf16[3,256,1152]{2,1,0:T(8,128)(2,1)S(1)}, u32[]{:S(2)}) copy-start(bf16[3,256,1152]{2,1,0:T(8,128)(2,1)S(1)} %fusion.50) | copy-start | bytes 5308420
  348.1 26.0 %copy-start.7 = (f32[3,256,1152]{2,1,0:T(8,128)S(1)}, f32[3,256,1152]{2,1,0:T(8,128)}, u32[]{:S(2)}) copy-start(f32[3,256,1152]{2,1,0:T(8,128)} %copy-done.6) | copy-start | bytes 10616836
  391.0 14.0 %copy-start.56 = (bf16[3,256]{1,0:T(4,128)(2,1)}, bf16[3,256]{1,0:T(4,128)(2,1)S(1)}, u32[]{:S(2)}) copy-start(bf16[3,256]{1,0:T(4,128)(2,1)S(1)} %multiply_convert_fusion.7) | copy-start | bytes 4612
  391.0 14.0 %copy-start.8 = (f32[3,256,1152]{2,1,0:T(8,128)S(1)}, f32[3,256,1152]{2,1,0:T(8,128)}, u32[]{:S(2)}) copy-start(f32[3,256,1152]{2,1,0:T(8,128)} %copy-done.6) | copy-start | bytes 10616836
  432.4 9.1 copy-start.2
  432.4 9.1 copy-start.45
  490.9 15.0 %copy-start.13 = (bf16[3,256,1152]{2,1,0:T(8,128)(2,1)S(1)}, bf16[3,256,1152]{2,1,0:T(8,128)(2,1)}, u32[]{:S(2)}) copy-start(bf16[3,256,1152]{2,1,0:T(8,128)(2,1)} %copy-done.12) | copy-start | bytes 5308420
  505.9 14.3 %copy-start.18 = (bf16[3,256,16,72]{1,3,2,0:T(8,128)(2,1)S(1)}, bf16[3,256,16,72]{1,3,2,0:T(8,128)(2,1)}, u32[]{:S(2)}) copy-start(bf16[3,256,16,72]{1,3,2,0:T(8,128)(2,1)} %convert_bitcast_fusion) | copy-start | bytes 5308420
  535.0 12.6 %copy-start.17 = (bf16[3,256,16,72]{1,0,3,2:T(4,128)(2,1)S(1)}, bf16[3,256,16,72]{1,0,3,2:T(4,128)(2,1)}, u32[]{:S(2)}) copy-start(bf16[3,256,16,72]{1,0,3,2:T(4,128)(2,1)} %copy.117) | copy-start | bytes 5308420
  755.2 58.7 %all-to-all-start.2 = ((bf16[3,8,864]{2,0,1:T(4,128)(2,1)}), bf16[3,8,864]{2,0,1:T(4,128)(2,1)S(1)}, u32[]{:S(2)}, u32[]{:S(2)}) async-start(bf16[3,8,864]{2,0,1:T(4,128)(2,1)} %copy.115), calls=%async_computation.2 | async-start | bytes 114688 | tf_op jit(solution)/shard_map/all_to_all | solution.py:538
  758.5 113.2 %all-reduce.7.cloned.1.call-start = ((), (), s32[]{:S(2)}) async-start(), calls=%async_computation.4 | async-start | bytes 221184
  758.6 5.1 copy-start.15
  770.6 52.0 %copy-start.36 = (bf16[96,1152]{1,0:T(8,128)(2,1)S(1)}, bf16[96,1152]{1,0:T(8,128)(2,1)}, u32[]{:S(2)}) copy-start(bf16[96,1152]{1,0:T(8,128)(2,1)} %copy-done.35) | copy-start | bytes 663556
  813.1 58.7 %copy-start.44 = (bf16[1152,16]{1,0:T(8,128)(2,1)S(1)}, bf16[1152,16]{1,0:T(8,128)(2,1)}, u32[]{:S(2)}) copy-start(bf16[1152,16]{1,0:T(8,128)(2,1)} %copy-done.43) | copy-start | bytes 110596
  813.1 58.7 %copy-start.51 = (f32[3,1152]{1,0:T(4,128)S(1)}, f32[3,1152]{1,0:T(4,128)}, u32[]{:S(2)}) copy-start(f32[3,1152]{1,0:T(4,128)} %copy-done.50) | copy-start | bytes 41476
  822.6 94.7 %copy-start.61 = (s32[96]{0:T(128)S(1)}, s32[96]{0:T(128)}, u32[]{:S(2)}) copy-start(s32[96]{0:T(128)} %copy-done.60) | copy-start | bytes 1156
  822.6 95.8 %copy-start.48 = (bf16[96,128]{1,0:T(8,128)(2,1)S(1)}, bf16[96,128]{1,0:T(8,128)(2,1)}, u32[]{:S(2)}) copy-start(bf16[96,128]{1,0:T(8,128)(2,1)} %get-tuple-element.57) | copy-start | bytes 73732
  822.6 95.8 %copy-start.49 = (bf16[96,128]{1,0:T(8,128)(2,1)S(1)}, bf16[96,128]{1,0:T(8,128)(2,1)}, u32[]{:S(2)}) copy-start(bf16[96,128]{1,0:T(8,128)(2,1)} %get-tuple-element.58) | copy-start | bytes 73732
  (38 other events, 104.0 us)
Sparse Core Ops, SparseCore 0:
  63.8 73.3 all-reduce.4
  822.7 49.0 all-reduce.6

commit v2 on v1

--- a/solution.py
+++ b/solution.py
@@ -47,8 +47,9 @@
 
 
 class Place:
-    def __init__(self, ring):
-        self.ring = ring
+    def __init__(self, dp, fsdp):
+        ring = fsdp // 2
+        self.dp, self.fsdp, self.ring = dp, fsdp, ring
         d = lax.axis_index("dp")
         f = lax.axis_index("fsdp")
         self.d, self.f = d, f
@@ -69,9 +70,15 @@
     def shard(self, back):
         return ((self.z + self.ring - back) % self.ring) * 2 + self.c
 
+    def mates(self):
+        return [(self.d, (self.f + offset) % self.fsdp) for offset in range(1, self.fsdp)]
+
+    def cousins(self):
+        return [((self.d + offset) % self.dp, self.f) for offset in range(1, self.dp)]
+
     def greet(self):
         barrier = pltpu.get_barrier_semaphore()
-        near = [self.core, self.x, self.y, self.up, self.down]
+        near = self.mates() + self.cousins()
         for other in near:
             pl.semaphore_signal(barrier, inc=1, device_id=other, device_id_type=MESH)
         pl.semaphore_wait(barrier, len(near))
@@ -81,6 +88,26 @@
     return pltpu.make_async_remote_copy(
         src_ref=src, dst_ref=dst, send_sem=send, recv_sem=recv, device_id=device, device_id_type=MESH
     )
+
+
+class Swap:
+    def __init__(self, partners, send, recv):
+        self.partners, self.send, self.recv = partners, send, recv
+        self.copies = []
+
+    def start(self, source, landing):
+        for i, device in enumerate(self.partners):
+            copy = remote(source(device), landing, self.send.at[i], self.recv.at[i], device)
+            copy.start()
+            self.copies.append(copy)
+
+    def arrived(self):
+        for copy in self.copies:
+            copy.wait_recv()
+
+    def left(self):
+        for copy in self.copies:
+            copy.wait_send()
 
 
 def cut(width):
@@ -97,14 +124,29 @@
     return ref.at[(*lead, q, slice(None), pl.ds(start, size))]
 
 
-def gather_kernel(ring, width, *refs):
+def gather_kernel(dp, fsdp, width, *refs):
     weights = 3
-    shards, fulls = refs[:weights], refs[weights : 2 * weights]
-    (own_sem, core_s, core_r, ring_s, ring_r, x_s, x_r, y_s, y_r, a_s, a_r, b_s, b_r) = refs[2 * weights :]
-    at = Place(ring)
+    ring = fsdp // 2
+    shards, refs = refs[:weights], refs[weights:]
+    ask_ref, time_ref, table_ref, ada_ref, router_ref = refs[:5]
+    refs = refs[5:]
+    fulls, refs = refs[:weights], refs[weights:]
+    pre_ref, mod_ref, routers_ref, all_cond_ref, all_ask_ref = refs[:5]
+    refs = refs[5:]
+    asks, parts, mine_in, conds, columns = refs[:5]
+    refs = refs[5:]
+    (own_sem, core_s, core_r, ring_s, ring_r, x_s, x_r, y_s, y_r, a_s, a_r, b_s, b_r) = refs[:13]
+    mate_s, mate_r, cousin_s, cousin_r, small_sem = refs[13:]
+    at = Place(dp, fsdp)
     part_a, part_b = cut(width)
     at.greet()
     sent, landed = [], []
+    mates, cousins = at.mates(), at.cousins()
+    swaps = [Swap(mates, mate_s.at[i], mate_r.at[i]) for i in range(5)]
+    far = [Swap(cousins, cousin_s.at[i], cousin_r.at[i]) for i in range(2)]
+    pad = ask_ref.shape[0]
+    group = fsdp * pad
+    rows = table_ref.shape[1]
 
     def go(copy):
         copy.start()
@@ -118,6 +160,58 @@
         else:
             src = view(fulls[k], (index,), at.q, width)
         return remote(src, view(fulls[k], (index,), at.q, width), ring_s.at[k, step - 1], ring_r.at[k, step - 1], at.up)
+
+    small = []
+
+    def keep(src, dst):
+        copy = pltpu.make_async_copy(src, dst, small_sem.at[len(small)])
+        copy.start()
+        small.append(copy)
+
+    def cond_one():
+        swaps[0].arrived()
+        asks[at.f] = ask_ref[...]
+        every = asks[...].reshape(group, asks.shape[2])
+        entries = every.shape[1] - 128
+        own_rows = time_ref.shape[0]
+        lanes = lax.broadcasted_iota(jnp.int32, (group, entries), 1)
+        held = (lanes >= at.f * own_rows) & (lanes < (at.f + 1) * own_rows)
+        embedded = jnp.where(held, every[:, :entries], 0.0).astype(jnp.bfloat16)
+        stacked = jnp.concatenate([time_ref[...]] * fsdp, axis=0)
+        label = every[:, entries : entries + 1].astype(jnp.int32)
+        classes = table_ref.shape[0]
+        picks = (label == lax.broadcasted_iota(jnp.int32, (group, classes), 1)).astype(jnp.float32)
+        picked = matmul(picks.astype(jnp.bfloat16), table_ref[...]).astype(jnp.bfloat16)
+        spot = lax.broadcasted_iota(jnp.int32, (rows, width), 1)
+        line = lax.broadcasted_iota(jnp.int32, (rows, width), 0)
+        place = (spot == line + at.f * rows).astype(jnp.float32).astype(jnp.bfloat16)
+        partial_sum = matmul(embedded, stacked) + matmul(picked, place)
+        parts[...] = partial_sum.reshape(fsdp, pad, width)
+        swaps[1].start(lambda device: parts.at[device[1]], mine_in.at[at.f])
+        far[1].start(lambda device: asks, all_ask_ref.at[at.d])
+        keep(asks, all_ask_ref.at[at.d])
+
+    def cond_two():
+        swaps[1].arrived()
+        mine_in[at.f] = parts[at.f]
+        pre_cond = jnp.sum(mine_in[...], axis=0)
+        pre_ref[...] = pre_cond
+        conds[at.f] = (pre_cond * jax.nn.sigmoid(pre_cond)).astype(jnp.bfloat16).astype(jnp.float32)
+        swaps[2].start(lambda device: conds.at[at.f], conds.at[at.f])
+
+    def cond_three():
+        swaps[2].arrived()
+        every = conds[...].reshape(group, width).astype(jnp.bfloat16)
+        columns[...] = matmul(every, ada_ref[...]).reshape(columns.shape)
+        swaps[3].start(lambda device: columns.at[device[1]], mod_ref.at[at.f])
+        far[0].start(lambda device: conds, all_cond_ref.at[at.d])
+        keep(conds, all_cond_ref.at[at.d])
+        keep(columns.at[at.f], mod_ref.at[at.f])
+
+    extra = {0: cond_one, 1: cond_two, 2: cond_three}
+    swaps[0].start(lambda device: ask_ref, asks.at[at.f])
+    swaps[4].start(lambda device: router_ref, routers_ref.at[at.f])
+    keep(router_ref, routers_ref.at[at.f])
 
     items = [(k, step) for k in range(weights) for step in range(1, ring)]
     rings = {items[0]: go(ring_copy(*items[0]))}
@@ -155,38 +249,76 @@
                 copy.wait_recv()
             whole = fulls[k].at[at.shard(step)]
             landed.append(go(remote(whole, whole, core_s.at[k, step], core_r.at[k, step], at.core)))
+        if turn in extra:
+            extra[turn]()
+    for swap in (swaps[3], swaps[4], far[0], far[1]):
+        swap.arrived()
     for copy in landed:
         copy.wait_recv()
-    for copy in locals_:
+    for copy in locals_ + small:
         copy.wait()
+    for swap in swaps + far:
+        swap.left()
     for copy in sent:
         copy.wait_send()
 
 
-def gather_weights(shards, width, fsdp):
+def gather_weights(shards, asked, time_weight, class_table, ada_weight, routers, width, dp, fsdp):
     ring = fsdp // 2
     dma = pltpu.SemaphoreType.DMA
+    vmem = pltpu.VMEM
+    f32 = jnp.float32
     steps = dma((3, ring - 1))
+    pad, asking = asked.shape
+    columns = ada_weight.shape[1]
+    out = jax.ShapeDtypeStruct
+    any_space, in_vmem = pl.BlockSpec(memory_space=pl.ANY), pl.BlockSpec(memory_space=vmem)
     return pl.pallas_call(
-        partial(gather_kernel, ring, width),
-        out_shape=[jax.ShapeDtypeStruct((fsdp, *s.shape), s.dtype) for s in shards],
-        in_specs=[pl.BlockSpec(memory_space=pl.ANY)] * 3,
-        out_specs=[pl.BlockSpec(memory_space=pl.ANY)] * 3,
-        scratch_shapes=[dma((3,)), dma((3, ring)), dma((3, ring))] + [steps] * 10,
-        compiler_params=pltpu.CompilerParams(collective_id=0, has_side_effects=True),
+        partial(gather_kernel, dp, fsdp, width),
+        out_shape=[out((fsdp, *s.shape), s.dtype) for s in shards]
+        + [
+            out((pad, width), f32),
+            out((fsdp, pad, columns), f32),
+            out((fsdp, *routers.shape), routers.dtype),
+            out((dp, fsdp, pad, width), f32),
+            out((dp, fsdp, pad, asking), f32),
+        ],
+        in_specs=[any_space] * 3 + [in_vmem] * 5,
+        out_specs=[any_space] * 3 + [in_vmem] + [any_space] * 4,
+        scratch_shapes=[
+            vmem((fsdp, pad, asking), f32),
+            vmem((fsdp, pad, width), f32),
+            vmem((fsdp, pad, width), f32),
+            vmem((fsdp, pad, width), f32),
+            vmem((fsdp, pad, columns), f32),
+        ]
+        + [dma((3,)), dma((3, ring)), dma((3, ring))]
+        + [steps] * 10
+        + [dma((5, fsdp - 1))] * 2
+        + [dma((2, dp - 1))] * 2
+        + [dma((4,))],
+        compiler_params=pltpu.CompilerParams(
+            collective_id=0, has_side_effects=True, vmem_limit_bytes=32 * 2**20
+        ),
         name="gather",
-    )(*shards)
-
-
-def reduce_kernel(ring, width, *refs):
+    )(*shards, asked, time_weight, class_table, ada_weight, routers)
+
+
+def reduce_kernel(dp, fsdp, width, *refs):
     weights = 3
-    terms, outs = refs[:weights], refs[weights : 2 * weights]
+    ring = fsdp // 2
+    terms, refs = refs[:weights], refs[weights:]
+    gm_ref, ada_ref, routed_ref, pre_ref, last_ref = refs[:5]
+    refs = refs[5:]
+    outs, refs = refs[:weights], refs[weights:]
+    all_gm_ref, all_pre_ref = refs[:2]
+    refs = refs[2:]
     (
-        own, pair, first_a, first_b, second_a, second_b, hops, done,
+        own, pair, first_a, first_b, second_a, second_b, hops, done, gms, parts, mine_in, pres,
         load, core_s, core_r, xa_s, xa_r, yb_s, yb_r, ya_s, ya_r, xb_s, xb_r, ring_s, ring_r,
-        end_s, end_r, out_sem,
-    ) = refs[2 * weights :]
-    at = Place(ring)
+        end_s, end_r, out_sem, mate_s, mate_r, cousin_s, cousin_r, small_sem,
+    ) = refs
+    at = Place(dp, fsdp)
     part_a, part_b = cut(width)
     cols_a, cols_b = pl.ds(*part_a), pl.ds(*part_b)
     rows = slice(None)
@@ -215,6 +347,46 @@
         ]
     flights, rings, ends = {}, {}, {}
 
+    mates, cousins = at.mates(), at.cousins()
+    swaps = [Swap(mates, mate_s.at[i], mate_r.at[i]) for i in range(3)]
+    far = [Swap(cousins, cousin_s.at[i], cousin_r.at[i]) for i in range(2)]
+    pad = pre_ref.shape[0]
+    small = []
+
+    def keep(src, dst):
+        copy = pltpu.make_async_copy(src, dst, small_sem.at[len(small)])
+        copy.start()
+        small.append(copy)
+
+    def cond_one():
+        swaps[0].arrived()
+        gms[at.f] = gm_ref[at.f]
+        every = gms[...].reshape(fsdp * pad, gms.shape[2]).astype(jnp.bfloat16)
+        parts[...] = times_back(every, ada_ref[...]).reshape(parts.shape)
+        swaps[1].start(lambda device: parts.at[device[1]], mine_in.at[at.f])
+        far[0].start(lambda device: gms, all_gm_ref.at[at.d])
+        keep(gms, all_gm_ref.at[at.d])
+
+    def cond_two():
+        swaps[1].arrived()
+        mine_in[at.f] = parts[at.f]
+        grad_cond = jnp.sum(mine_in[...], axis=0) + routed_ref[...]
+        pre_cond = pre_ref[...]
+        sig = jax.nn.sigmoid(pre_cond)
+        grad_pre = grad_cond * (sig * (1.0 + pre_cond * (1.0 - sig)))
+        grad_pre = grad_pre.astype(jnp.bfloat16).astype(jnp.float32)
+        pres[at.f, :, :width] = grad_pre + last_ref[:, :width]
+        pres[at.f, :, width:] = last_ref[:, width:]
+        swaps[2].start(lambda device: pres.at[at.f], pres.at[at.f])
+
+    def cond_three():
+        swaps[2].arrived()
+        far[1].start(lambda device: pres, all_pre_ref.at[at.d])
+        keep(pres, all_pre_ref.at[at.d])
+
+    extra = {1: cond_one, 3: cond_two, 5: cond_three}
+    swaps[0].start(lambda device: gm_ref.at[device[1]], gms.at[at.f])
+
     def stage_one(k, j):
         for q in range(QUARTERS):
             loads[k, j][q].wait()
@@ -289,18 +461,28 @@
             stage_four(items[turn - 3][0])
         if 0 <= turn - 4 < len(items) and items[turn - 4][1] == ring - 1:
             stage_five(items[turn - 4][0])
-    for copy in outgoing:
+        if turn in extra:
+            extra[turn]()
+    for swap in far:
+        swap.arrived()
+    for copy in outgoing + small:
         copy.wait()
+    for swap in swaps + far:
+        swap.left()
     for copy in sent:
         copy.wait_send()
 
 
-def reduce_terms(terms, rows, width, fsdp):
+def reduce_terms(terms, grad_modulation, ada_weight, routed, pre_cond, last, rows, width, dp, fsdp):
     ring = fsdp // 2
     dma = pltpu.SemaphoreType.DMA
     low = jnp.bfloat16
     (_, size_a), (_, size_b) = cut(width)
     vmem = pltpu.VMEM
+    f32 = jnp.float32
+    pad = pre_cond.shape[0]
+    out = jax.ShapeDtypeStruct
+    any_space, in_vmem = pl.BlockSpec(memory_space=pl.ANY), pl.BlockSpec(memory_space=vmem)
     scratch = [
         vmem((3, ring, QUARTERS, rows, width), low),
         vmem((3, ring, QUARTERS, rows, width), low),
@@ -310,6 +492,10 @@
         vmem((3, ring, rows, size_b), low),
         vmem((3, ring - 1, rows, width), low),
         vmem((3, QUARTERS, rows, width), low),
+        vmem(grad_modulation.shape, f32),
+        vmem((fsdp, pad, width), f32),
+        vmem((fsdp, pad, width), f32),
+        vmem((fsdp, *last.shape), f32),
     ]
     sems = (
         [dma((3, ring, QUARTERS))] * 3
@@ -318,18 +504,22 @@
         + [dma((3, ring - 1))] * 2
         + [dma((3, 4))] * 2
         + [dma((3,))]
+        + [dma((3, fsdp - 1))] * 2
+        + [dma((2, dp - 1))] * 2
+        + [dma((2,))]
     )
     return pl.pallas_call(
-        partial(reduce_kernel, ring, width),
-        out_shape=[jax.ShapeDtypeStruct((QUARTERS, rows, width), low)] * 3,
-        in_specs=[pl.BlockSpec(memory_space=pl.ANY)] * 3,
-        out_specs=[pl.BlockSpec(memory_space=pl.ANY)] * 3,
+        partial(reduce_kernel, dp, fsdp, width),
+        out_shape=[out((QUARTERS, rows, width), low)] * 3
+        + [out((dp, *grad_modulation.shape), f32), out((dp, fsdp, *last.shape), f32)],
+        in_specs=[any_space] * 3 + [in_vmem] * 5,
+        out_specs=[any_space] * 5,
         scratch_shapes=scratch + sems,
         compiler_params=pltpu.CompilerParams(
             collective_id=1, has_side_effects=True, vmem_limit_bytes=60 * 2**20
         ),
         name="reduce",
-    )(*terms)
+    )(*terms, grad_modulation, ada_weight, routed, pre_cond, last)
 
 
 def body(
@@ -359,50 +549,50 @@
     rows = qkv_weight.shape[0]
     hidden = fc1_weight.shape[1]
     entries = time_weight.shape[0] * fsdp
-    group = images * fsdp
-    me_dp, me_fsdp = lax.axis_index("dp"), lax.axis_index("fsdp")
-    everyone = ("dp", "fsdp")
-
-    joint_full, fc1_full, fc2_full = gather_weights(
+    me_fsdp = lax.axis_index("fsdp")
+    pad = (images // 8 + 1) * 8
+
+    def padded(array, value=0.0):
+        return jnp.pad(array, ((0, pad - images), (0, 0)), constant_values=value)
+
+    embedded = sinusoid(timesteps, entries).astype(jnp.bfloat16)
+    asked = jnp.concatenate(
+        [
+            padded(embedded.astype(jnp.float32)),
+            padded(jnp.broadcast_to(labels.astype(jnp.float32)[:, None], (images, 128)), -1.0),
+        ],
+        axis=1,
+    )
+    routers = jnp.pad(
+        jnp.concatenate([head_router, token_router], axis=1), ((0, 0), (0, 127 - heads))
+    )
+    joint_full, fc1_full, fc2_full, pre_cond_pad, modulation, routers_full, all_cond, all_asked = gather_weights(
         [
             jnp.concatenate([qkv_weight, proj_weight], axis=1),
             fc1_weight,
             fc2_weight.reshape(QUARTERS, rows, width),
         ],
+        asked,
+        time_weight,
+        class_table,
+        ada_weight,
+        routers,
         width,
+        dp,
         fsdp,
     )
     joint_full = joint_full.reshape(width, 4 * width)
     triple, merger = joint_full[:, : 3 * width], joint_full[:, 3 * width :]
     expand = fc1_full.reshape(width, hidden)
     shrink = fc2_full.reshape(hidden, width)
-
-    asked = lax.all_gather(jnp.stack([timesteps, labels], axis=1), everyone, axis=0, tiled=True)
-    all_steps, all_labels = asked[:, 0], asked[:, 1]
-    packed = jnp.concatenate(
-        [time_weight.reshape(-1), head_router.reshape(-1), token_router.reshape(-1)]
-    )
-    parts = lax.all_gather(packed, "fsdp", axis=0, tiled=False)
-    cut_one = time_weight.size
-    cut_two = cut_one + head_router.size
-    time_full = parts[:, :cut_one].reshape(entries, width)
-    chooser = parts[:, cut_one:cut_two].reshape(width, heads)
-    picker = parts[:, cut_two:].reshape(width, 1)
-
-    table_rows = jnp.arange(class_table.shape[0], dtype=jnp.int32)
-    all_rows = (all_labels[:, None] == table_rows[None, :]).astype(jnp.bfloat16)
-    group_rows = lax.dynamic_slice_in_dim(all_rows, me_dp * group, group, axis=0)
-    picked = matmul(group_rows, class_table).astype(jnp.bfloat16)
-    class_part = lax.all_to_all(picked, "fsdp", split_axis=0, concat_axis=1, tiled=True)
-    all_embedded = sinusoid(all_steps, entries).astype(jnp.bfloat16)
-    embedded = sinusoid(timesteps, entries).astype(jnp.bfloat16)
-    pre_cond = matmul(embedded, time_full) + class_part.astype(jnp.float32)
+    routers_full = routers_full.reshape(width, 128)
+    chooser, picker = routers_full[:, :heads], routers_full[:, heads : heads + 1]
+    everyone = dp * fsdp * pad
+    all_cond = all_cond.reshape(everyone, width).astype(jnp.bfloat16)
+    all_asked = all_asked.reshape(everyone, asked.shape[1])
+    pre_cond = pre_cond_pad[:images]
     cond = jax.nn.silu(pre_cond).astype(jnp.bfloat16)
-    all_cond = lax.all_gather(cond, everyone, axis=0, tiled=True)
-    group_cond = lax.dynamic_slice_in_dim(all_cond, me_dp * group, group, axis=0)
-    modulation = lax.all_to_all(
-        matmul(group_cond, ada_weight), "fsdp", split_axis=0, concat_axis=1, tiled=True
-    )
+    modulation = modulation[:, :images].transpose(1, 0, 2).reshape(images, 6 * width)
     shift_one, scale_one, gate_one, shift_two, scale_two, gate_two = jnp.split(
         modulation[:, None, :], 6, axis=2
     )
@@ -510,14 +700,27 @@
         axis=1,
     ).astype(jnp.bfloat16)
 
-    sums = reduce_terms(
+    last = jnp.concatenate(
+        [
+            jnp.pad(grad_picker, ((pad - 1, 0), (0, 0))),
+            padded(jnp.pad(grad_router.astype(jnp.float32), ((0, 0), (0, 128 - heads)))),
+        ],
+        axis=1,
+    )
+    *sums, all_grad, all_pre = reduce_terms(
         [
             jnp.concatenate([grad_triple, grad_merger], axis=1).reshape(fsdp, rows, 4 * width),
             grad_expand.reshape(fsdp, rows, hidden),
             grad_shrink.reshape(fsdp, QUARTERS, rows, width),
         ],
+        padded(grad_modulation.astype(jnp.float32)).reshape(pad, fsdp, -1).transpose(1, 0, 2),
+        ada_weight,
+        padded(times_back(grad_router, chooser)),
+        pre_cond_pad,
+        last,
         rows,
         width,
+        dp,
         fsdp,
     )
     if dp > QUARTERS:
@@ -535,33 +738,27 @@
     sum_expand = jnp.concatenate([sums[1][i] for i in range(QUARTERS)], axis=1)
     sum_shrink = sums[2].reshape(QUARTERS * rows, width)
 
-    group_grad = lax.all_to_all(grad_modulation, "fsdp", split_axis=1, concat_axis=0, tiled=True)
-    all_grad = lax.all_gather(group_grad, "dp", axis=0, tiled=True)
-    sum_ada = times_rows(all_cond, all_grad)
-    grad_cond = lax.psum_scatter(
-        times_back(group_grad, ada_weight), "fsdp", scatter_dimension=0, tiled=True
-    )
-    grad_cond = grad_cond + times_back(grad_router, chooser)
-    _, silu_pull = jax.vjp(jax.nn.silu, pre_cond)
-    grad_pre = silu_pull(grad_cond)[0].astype(jnp.bfloat16)
-    both = lax.all_gather(
-        jnp.concatenate([grad_pre, grad_router], axis=1), everyone, axis=0, tiled=True
-    )
-    all_pre, all_router = both[:, :width], both[:, width:]
-    sum_time = times_rows(
-        lax.dynamic_slice_in_dim(all_embedded, me_fsdp * (entries // fsdp), entries // fsdp, axis=1),
-        all_pre,
-    )
+    sum_ada = times_rows(all_cond, all_grad.reshape(everyone, -1).astype(jnp.bfloat16))
+    sum_picker = lax.dynamic_slice_in_dim(
+        jnp.sum(all_pre[:, :, pad - 1, :width], axis=(0, 1)), me_fsdp * rows, rows, axis=0
+    )[:, None]
+    is_image = (jnp.arange(pad) < images)[None, None, :, None]
+    all_pre = jnp.where(is_image, all_pre, 0.0).reshape(everyone, -1).astype(jnp.bfloat16)
+    all_router = all_pre[:, width : width + heads]
+    all_pre = all_pre[:, :width]
+    own_entries = entries // fsdp
+    all_embedded = lax.dynamic_slice_in_dim(
+        all_asked[:, :entries], me_fsdp * own_entries, own_entries, axis=1
+    ).astype(jnp.bfloat16)
+    classes = jnp.arange(class_table.shape[0], dtype=jnp.float32)
+    all_rows = (all_asked[:, entries : entries + 1] == classes[None, :]).astype(jnp.bfloat16)
+    sum_time = times_rows(all_embedded, all_pre)
     sum_table = times_rows(
         all_rows, lax.dynamic_slice_in_dim(all_pre, me_fsdp * rows, rows, axis=1)
     )
     sum_chooser = times_rows(
         lax.dynamic_slice_in_dim(all_cond, me_fsdp * rows, rows, axis=1), all_router
     )
-    all_picker = lax.all_gather(grad_picker, everyone, axis=0, tiled=True)
-    sum_picker = lax.dynamic_slice_in_dim(
-        jnp.sum(all_picker, axis=0), me_fsdp * rows, rows, axis=0
-    )[:, None]
     return (
         output,
         grad_inputs,

time: 933 us -> 723 us (0.77)
  blocking collectives: 174 us -> 0 us
  Pallas kernels: 313 us -> 365 us
  waiting for transfers between devices: 52 us -> 0 us
  between operations: 16.7 us -> 2.04 us
  matrix products: 226 us -> 215 us
  starting transfers between devices: 10.3 us -> 0 us
    all_gather x5 -> x0, blocking collectives: 174 us -> none  [the longest x1 43.3 us: body(): lax.all_gather(jnp.stack([timesteps, labels], axis=1), everyone, axis=0,...]
    pallas_call x2, Pallas kernels: 313 us -> 365 us  [the longest x1 218 us: reduce_terms(): pl.pallas_call(partial(reduce_kernel, dp, fsdp, width), out_shape=[out((Q...]
    unnamed x4 -> x0, waiting for transfers between devices: 46.5 us -> none
    all_to_all x3 -> x0, starting transfers between devices: 10.2 us -> none  [the longest x1 3.54 us: body(): lax.all_to_all(matmul(group_cond, ada_weight), 'fsdp', split_axis=0, conc...]
    dot_general x6 -> x5, matrix products: 50.7 us -> 42.3 us  [times_back(): lax.dot_general(left, right, (((1,), (1,)), ((), ())), preferred_element_...]
    unnamed x150 -> x152, local copies, waits for them, and re-layouts: 20 us -> 24.6 us
    dot_general x9 -> x6, matrix products: 63.1 us -> 60.3 us  [matmul(): return jnp.dot(left, right, preferred_element_type=jnp.float32)]
  transfers between devices with their start and end apart: 5 -> 0, of which waited for: 2 -> 0; matrix products, arithmetic and copies ran while one was open for 3% -> 0% of each run, Pallas kernels for 14% -> 0%
where the time goes in v2:
time: 723 us; the launch traced here: 714 us
  Pallas kernels  365 us (50%)
  matrix products  215 us (30%)
  local copies, waits for them, and re-layouts  83.9 us (12%)
  other arithmetic  48.1 us (7%)
    pallas_call x1, Pallas kernels, reduce_terms(): pl.pallas_call(partial(reduce_kernel, dp, fsdp, width), out_shape=[out((Q...  218 us
    pallas_call x1, Pallas kernels, gather_weights(): pl.pallas_call(partial(gather_kernel, dp, fsdp, width), out_shape=[out((f...  147 us
    dot_general x6, matrix products, matmul(): return jnp.dot(left, right, preferred_element_type=jnp.float32)  60.3 us
    dot_general x9, matrix products, times_rows(): lax.dot_general(left, right, (((0,), (0,)), ((), ())), preferred_element_...  51 us
    dot_general x5, matrix products, times_back(): lax.dot_general(left, right, (((1,), (1,)), ((), ())), preferred_element_...  42.3 us
    unnamed x152, local copies, waits for them, and re-layouts  24.6 us
    dot_general x1, matrix products, body(): jnp.einsum('ihst,ithe->ishe', grad_scores, keys, preferred_element_type=j...  19.9 us
    dot_general x1, matrix products, body(): jnp.einsum('ihst,ishe->ithe', grad_scores, query, preferred_element_type=...  19.2 us

profile of v2, /device:TPU:0, one launch (start us, length us, event | category | flops | bytes accessed | tf_op | source)
XLA Modules:
  0.0 713.5 jit_solution(8341188415287822119)
XLA Ops:
  15.2 146.7 %gather.1 = (bf16[8,144,4608]{2,1,0:T(8,128)(2,1)S(1)}, bf16[8,144,4608]{2,1,0:T(8,128)(2,1)}, bf16[8,4,144,1152]{3,2,1,0:T(8,128)(2,1)}, f32[8,1152]{1,0:T(8,12...) custom-call(bf16[144,4608]{1,0:T(8,128)(2,1)S(1)} %pad_maximum_fusio, ...), custom_call_target="tpu_custom_call" | custom-call | tf_op jit(solution)/shard_map/gather/pallas_call | solution.py:276
  162.9 4.0 copy-done.10
  176.7 10.3 %fusion.23 = bf16[768,3456]{1,0:T(8,128)(2,1)S(1)} fusion(bf16[768,1152]{1,0:T(8,128)(2,1)S(1)} %bitcast.171, bf16[1152,4608]{1,0:T(8,128)(2,1)} %bitcast.141), kind=kOutput, calls=%fused_computation.31 | convolution fusion | flops 6117949440 | bytes 15040512 | tf_op jit(solution)/shard_map/dot_general | solution.py:34
  189.6 6.9 reshape.267
  196.4 3.1 copy.82
  199.5 6.9 reshape.266
  206.4 3.1 copy.81
  209.6 7.1 reshape.265
  216.6 3.1 copy.83
  219.7 3.9 multiply_reduce_fusion.1
  228.4 4.6 fusion.56
  236.2 6.5 fusion.114
  248.4 15.0 %fusion.116 = f32[768,4608]{1,0:T(8,128)} fusion(bf16[768,1152]{1,0:T(8,128)(2,1)S(1)} %bitcast.173, bf16[4608,1152]{1,0:T(8,128)(2,1)} %bitcast.183), kind=kOutput, calls=%fused_computation.196 | convolution fusion | flops 8153726976 | bytes 26542080 | tf_op jit(solution)/shard_map/dot_general | solution.py:44
  263.4 24.9 %fusion.7 = (bf16[768,4608]{1,0:T(8,128)(2,1)}, bf16[768,4608]{1,0:T(8,128)(2,1)}) fusion(f32[768,4608]{1,0:T(8,128)} %fusion.116, bf16[768,1152]{1,0:T(8,128)(2,1)S(1)} %bitcast.152, bf16[1152,4608]{1,0:T(8,128)(2,1)} %bitcast.181), kind=kOutput, calls=%fused_computation.12 | convolution fusion | flops 8231583744 | bytes 40697856 | tf_op jit(solution)/shard_map/dot_general | solution.py:34
  288.3 17.2 %fusion.55 = (bf16[3,1152]{1,0:T(4,128)(2,1)}, f32[3,256]{1,0:T(4,128)S(1)}, bf16[3,256,1152]{2,1,0:T(8,128)(2,1)}) fusion(bf16[3,256,1152]{2,1,0:T(8,128)(2,1)S(1)} %copy-done.19, f32[3,256]{1,0:T(4,128)S(1)} %convert_multiply_fusion.2, f32[3,1152]{1,0:T(4,128)S(1)} %get-tuple-element.65, f32[3,256,1152]{2,1,0:T(8,128)} %copy-done.15, ...), kind=kOutput, calls=%fused_computation.66 | convolution fusion | flops 8163454976 | bytes 24799488 | tf_op jit(solution)/shard_map/dot_general | solution.py:34
  305.5 13.6 %convolution_add_fusion = f32[768,1152]{1,0:T(8,128)S(1)} fusion(bf16[768,4608]{1,0:T(8,128)(2,1)} %get-tuple-element.49, bf16[1152,4608]{1,0:T(8,128)(2,1)} %bitcast.182, f32[1152]{0:T(1024)S(1)} %convert.62, f32[768]{0:T(1024)S(1)} %reshape.251), kind=kOutput, calls=%fused_computation.56 | convolution fusion | flops 8155496448 | bytes 21241344 | tf_op jit(solution)/shard_map/dot_general | solution.py:44
  321.5 3.0 fusion.113
  327.2 4.0 convolution_convert_fusion.3
  331.2 6.3 fusion.58
  337.4 8.0 %reshape.268 = f32[3,256,16,72]{3,2,1,0:T(8,128)} reshape(f32[768,1152]{1,0:T(8,128)} %fusion.58) | data formatting | bytes 7077888 | tf_op jit(solution)/shard_map/convert_element_type | solution.py:656
  345.4 5.9 copy.88
  351.3 3.6 fusion.57
  356.5 7.2 %convert_bitcast_fusion = bf16[3,256,16,72]{1,3,2,0:T(8,128)(2,1)S(1)} fusion(f32[3,16,256,256]{2,3,1,0:T(8,128)} %copy-done.11, f32[3,16,256]{2,1,0:T(8,128)S(1)} %copy-done.48, f32[3,256,16,72]{1,3,2,0:T(8,128)S(1)} %copy-done.12, f32[3,16]{1,0:T(4,128)S(1)} %get-tuple-element.75), kind=kOutput, calls=%fused_computation.89 | convolution fusion | flops 465076224 | bytes 17940672 | tf_op jit(solution)/shard_map/ihst,ishe->ithe/dot_general | solution.py:661
  366.8 14.3 %convolution_convert_fusion.1 = bf16[1152,4608]{1,0:T(8,128)(2,1)} fusion(bf16[768,1152]{1,0:T(8,128)(2,1)S(1)} %bitcast.153, bf16[768,4608]{1,0:T(8,128)(2,1)} %get-tuple-element.49), kind=kOutput, calls=%fused_computation.4 | convolution fusion | flops 8159035392 | bytes 19464192 | tf_op jit(solution)/shard_map/dot_general | solution.py:38
  381.2 6.4 fusion.74
  387.6 19.9 %convert_bitcast_fusion.2 = bf16[3,256,16,72]{1,3,2,0:T(8,128)(2,1)} fusion(bf16[3,256,16,72]{1,3,2,0:T(8,128)(2,1)S(1)} %copy-done.23, f32[3,16,256,256]{2,3,1,0:T(8,128)} %fusion.74, f32[3,16,256,256]{2,3,1,0:T(8,128)} %copy-done.11, f32[3,16,256]{2,1,0:T(8,128)} %log_add_fusion), kind=kOutput, calls=%fused_computation.91 | convolution fusion | flops 482193664 | bytes 28753920 | tf_op jit(solution)/shard_map/ihst,ithe->ishe/dot_general | solution.py:672
  407.5 19.2 %convert_bitcast_fusion.1 = bf16[3,256,16,72]{1,3,2,0:T(8,128)(2,1)S(1)} fusion(bf16[3,256,16,72]{1,3,2,0:T(8,128)(2,1)S(1)} %copy-done.24, f32[3,16,256,256]{2,3,1,0:T(8,128)} %fusion.74, f32[3,16,256,256]{2,3,1,0:T(8,128)} %copy-done.11, f32[3,16,256]{2,1,0:T(8,128)} %log_add_fusion), kind=kOutput, calls=%fused_computation.90 | convolution fusion | flops 482193664 | bytes 28753920 | tf_op jit(solution)/shard_map/ihst,ishe->ithe/dot_general | solution.py:675
  433.0 7.3 %fusion.19 = f32[768,1152]{1,0:T(8,128)S(1)} fusion(bf16[768,3456]{0,1:T(8,128)(2,1)S(1)} %constant_dynamic-update-slice_fusion, bf16[1152,4608]{1,0:T(8,128)(2,1)S(1)} %bitcast.146), kind=kOutput, calls=%fused_computation.27 | convolution fusion | flops 6115295232 | bytes 16809984 | tf_op jit(solution)/shard_map/dot_general | solution.py:44
  447.8 9.8 %convolution_convert_fusion.2 = bf16[1152,3456]{1,0:T(8,128)(2,1)S(1)} fusion(bf16[768,1152]{1,0:T(8,128)(2,1)S(1)} %bitcast.172, bf16[768,3456]{0,1:T(8,128)(2,1)} %copy-done.42), kind=kOutput, calls=%fused_computation.5 | convolution fusion | flops 6119276544 | bytes 15040512 | tf_op jit(solution)/shard_map/dot_general | solution.py:38
  457.6 4.6 pad_maximum_fusion
  462.2 16.8 %convolution_convert_fusion = bf16[4608,1152]{1,0:T(8,128)(2,1)} fusion(bf16[768,4608]{1,0:T(8,128)(2,1)} %get-tuple-element.50, bf16[768,1152]{1,0:T(8,128)(2,1)S(1)} %bitcast.174), kind=kOutput, calls=%fused_computation.3 | convolution fusion | flops 8159035392 | bytes 19464192 | tf_op jit(solution)/shard_map/dot_general | solution.py:38
  479.1 217.9 %reduce.6 = (bf16[4,144,1152]{2,1,0:T(8,128)(2,1)}, bf16[4,144,1152]{2,1,0:T(8,128)(2,1)}, bf16[4,144,1152]{2,1,0:T(8,128)(2,1)}, f32[4,8,8,864]{3,2,1,0:T(8,128)}, f32[4,8,8,1280]{3,2,1,0:T(8,128)}) custom-call(bf16[8,144,4608]{2,1,0:T(8,128)(2,1)} %bitcast.147, bf16[8,144,4608]{2,1,0:T(8,128)(2,1)} %bitcast.156, bf16[8,4,144,1152]{3,2,1,0:T(8,128)(2,1)} %bitcast.157, ...), custom_call_target="tpu_custom_call" | custom-call | tf_op jit(solution)/shard_map/reduce/pallas_call | solution.py:511
  (233 shorter events, 80.5 us)
Async XLA Ops:
  0.6 6.7 copy-start.64
  0.7 7.8 %copy-start.45 = (bf16[144,1152]{1,0:T(8,128)(2,1)S(1)}, bf16[144,1152]{1,0:T(8,128)(2,1)}, u32[]{:S(2)}) copy-start(bf16[144,1152]{1,0:T(8,128)(2,1)} %param.26) | copy-start | bytes 995332
  0.7 7.8 %copy-start.40 = (bf16[144,3456]{1,0:T(8,128)(2,1)S(1)}, bf16[144,3456]{1,0:T(8,128)(2,1)}, u32[]{:S(2)}) copy-start(bf16[144,3456]{1,0:T(8,128)(2,1)} %param.25) | copy-start | bytes 2985988
  0.7 6.7 copy-start.59
  0.7 6.8 copy-start.46
  4.6 169.3 %copy-start.49 = (f32[3,256]{1,0:T(4,128)}, f32[3,256]{1,0:T(4,128)S(1)}, u32[]{:S(2)}) copy-start(f32[3,256]{1,0:T(4,128)S(1)} %broadcast_multiply_fusion.1) | copy-start | bytes 9220
  6.8 167.2 %copy-start.51 = (f32[3,256]{1,0:T(4,128)}, f32[3,256]{1,0:T(4,128)S(1)}, u32[]{:S(2)}) copy-start(f32[3,256]{1,0:T(4,128)S(1)} %fusion.95) | copy-start | bytes 9220
  15.2 151.8 %copy-start = (bf16[1152,864]{1,0:T(8,128)(2,1)}, bf16[1152,864]{1,0:T(8,128)(2,1)S(1)}, u32[]{:S(2)}) copy-start(bf16[1152,864]{1,0:T(8,128)(2,1)S(1)} %copy.76.refs_6_.refs_4_) | copy-start | bytes 5971972
  15.2 152.4 %copy-start.61 = (s32[3,16]{1,0:T(4,128)S(1)}, s32[3,16]{1,0:T(4,128)}, u32[]{:S(2)}) copy-start(s32[3,16]{1,0:T(4,128)} %param.18) | copy-start | bytes 580
  168.5 18.5 %copy-start.43 = (f32[3,1152]{1,0:T(4,128)}, f32[3,1152]{1,0:T(4,128)S(1)}, u32[]{:S(2)}) copy-start(f32[3,1152]{1,0:T(4,128)S(1)} %get-tuple-element.69) | copy-start | bytes 41476
  176.7 10.4 %copy-start.31 = (bf16[3,256,1152]{2,1,0:T(8,128)(2,1)}, bf16[3,256,1152]{2,1,0:T(8,128)(2,1)S(1)}, u32[]{:S(2)}) copy-start(bf16[3,256,1152]{2,1,0:T(8,128)(2,1)S(1)} %fusion.48) | copy-start | bytes 5308420
  223.6 4.8 copy-start.11
  223.6 4.8 copy-start.25
  263.4 24.9 %copy-start.19 = (bf16[3,256,1152]{2,1,0:T(8,128)(2,1)S(1)}, bf16[3,256,1152]{2,1,0:T(8,128)(2,1)}, u32[]{:S(2)}) copy-start(bf16[3,256,1152]{2,1,0:T(8,128)(2,1)} %param.20) | copy-start | bytes 5308420
  305.5 14.0 %copy-start.16 = (f32[3,256,1152]{2,1,0:T(8,128)S(1)}, f32[3,256,1152]{2,1,0:T(8,128)}, u32[]{:S(2)}) copy-start(f32[3,256,1152]{2,1,0:T(8,128)} %copy-done.15) | copy-start | bytes 10616836
  351.3 5.1 copy-start.12
  351.3 5.1 copy-start.48
  366.8 14.3 %copy-start.26 = (bf16[3,256,16,72]{1,3,2,0:T(8,128)(2,1)S(1)}, bf16[3,256,16,72]{1,3,2,0:T(8,128)(2,1)}, u32[]{:S(2)}) copy-start(bf16[3,256,16,72]{1,3,2,0:T(8,128)(2,1)} %copy.83) | copy-start | bytes 5308420
  381.2 6.4 copy-start.23
  387.6 19.9 %copy-start.24 = (bf16[3,256,16,72]{1,3,2,0:T(8,128)(2,1)S(1)}, bf16[3,256,16,72]{1,3,2,0:T(8,128)(2,1)}, u32[]{:S(2)}) copy-start(bf16[3,256,16,72]{1,3,2,0:T(8,128)(2,1)} %copy.81) | copy-start | bytes 5308420
  426.7 5.6 slice-start
  433.0 7.3 %copy-start.42 = (bf16[768,3456]{0,1:T(8,128)(2,1)}, bf16[768,3456]{0,1:T(8,128)(2,1)S(1)}, u32[]{:S(2)}) copy-start(bf16[768,3456]{0,1:T(8,128)(2,1)S(1)} %constant_dynamic-update-slice_fusion) | copy-start | bytes 15925252
  433.0 7.3 %copy-start.14 = (bf16[3,256,1152]{2,1,0:T(8,128)(2,1)S(1)}, bf16[3,256,1152]{2,1,0:T(8,128)(2,1)}, u32[]{:S(2)}) copy-start(bf16[3,256,1152]{2,1,0:T(8,128)(2,1)} %param.15) | copy-start | bytes 5308420
  433.0 7.3 %copy-start.44 = (f32[3,1152]{1,0:T(4,128)S(1)}, f32[3,1152]{1,0:T(4,128)}, u32[]{:S(2)}) copy-start(f32[3,1152]{1,0:T(4,128)} %copy-done.43) | copy-start | bytes 41476
  433.0 7.4 %copy-start.50 = (f32[3,256]{1,0:T(4,128)S(1)}, f32[3,256]{1,0:T(4,128)}, u32[]{:S(2)}) copy-start(f32[3,256]{1,0:T(4,128)} %copy-done.49) | copy-start | bytes 9220
  447.8 9.8 %copy-start.30 = (bf16[1152,1152]{1,0:T(8,128)(2,1)S(1)}, bf16[1152,1152]{1,0:T(8,128)(2,1)}, u32[]{:S(2)}) copy-start(bf16[1152,1152]{1,0:T(8,128)(2,1)} %convolution_convert_fusion.3) | copy-start | bytes 7962628
  457.6 4.6 copy-start.34
  479.1 219.5 %copy-start.65 = (pred[8]{0:T(512)(128)(4,1)S(1)}, pred[8]{0:T(512)(128)(4,1)}, u32[]{:S(2)}) copy-start(pred[8]{0:T(512)(128)(4,1)} %iota_compare_fusion.4) | copy-start | bytes 28
  479.1 221.6 %copy-start.47 = (bf16[256,256]{1,0:T(8,128)(2,1)S(1)}, bf16[256,256]{1,0:T(8,128)(2,1)}, u32[]{:S(2)}) copy-start(bf16[256,256]{1,0:T(8,128)(2,1)} %slice.95) | copy-start | bytes 393220
  479.1 222.6 %copy-start.29 = (bf16[4,8,8,1152]{3,2,1,0:T(8,128)(2,1)S(1)}, bf16[4,8,8,1152]{3,2,1,0:T(8,128)(2,1)}, u32[]{:S(2)}) copy-start(bf16[4,8,8,1152]{3,2,1,0:T(8,128)(2,1)} %convert_element_type.161) | copy-start | bytes 1769476
  697.0 5.6 copy-start.60
  697.0 6.8 copy-start.39
  (37 other events, 82.4 us)

commit v3 on v2

--- a/solution.py
+++ b/solution.py
@@ -522,6 +522,95 @@
     )(*terms, grad_modulation, ada_weight, routed, pre_cond, last)
 
 
+def window(head, size):
+    low = head * size // 128 * 128
+    high = -(-(head + 1) * size // 128) * 128
+    spot = low + lax.broadcasted_iota(jnp.int32, (1, high - low), 1)
+    own = ((spot >= head * size) & (spot < (head + 1) * size)).astype(jnp.float32).astype(jnp.bfloat16)
+    return low, high - low, own
+
+
+def attend_image(joint, gates, mixed, lse, image, seq, heads):
+    width = mixed.shape[1]
+    size = width // heads
+    scale = size ** (-0.5)
+    lines = pl.ds(pl.multiple_of(image * seq, seq), seq)
+    mixed[lines, :] = jnp.zeros((seq, width), mixed.dtype)
+    for head in range(heads):
+        low, wide, own = window(head, size)
+        query = joint[lines, pl.ds(low, wide)] * own
+        keys = joint[lines, pl.ds(width + low, wide)]
+        values = joint[lines, pl.ds(2 * width + low, wide)] * own
+        raw = times_back(keys, query) * scale
+        peak = jnp.max(raw, axis=0, keepdims=True)
+        expo = jnp.exp(raw - peak)
+        total = jnp.sum(expo, axis=0, keepdims=True)
+        lse[image, head : head + 1, :] = peak + jnp.log(total)
+        probs = (expo * (1.0 / total)).astype(jnp.bfloat16)
+        attended = times_rows(probs, values) * gates[image, 0, head]
+        mixed[lines, pl.ds(low, wide)] = mixed[lines, pl.ds(low, wide)] + attended.astype(jnp.bfloat16)
+
+
+def attend_back_image(joint, grad_mixed, gates, lse, grad_joint, grad_gates, image, seq, heads):
+    width = grad_mixed.shape[1]
+    size = width // heads
+    scale = size ** (-0.5)
+    lines = pl.ds(pl.multiple_of(image * seq, seq), seq)
+    grad_joint[lines, :] = jnp.zeros((seq, 3 * width), grad_joint.dtype)
+
+    def put(column, wide, value):
+        here = pl.ds(column, wide)
+        grad_joint[lines, here] = grad_joint[lines, here] + value.astype(jnp.bfloat16)
+
+    for head in range(heads):
+        low, wide, own = window(head, size)
+        query = joint[lines, pl.ds(low, wide)] * own
+        keys = joint[lines, pl.ds(width + low, wide)] * own
+        values = joint[lines, pl.ds(2 * width + low, wide)]
+        grad = grad_mixed[lines, pl.ds(low, wide)] * own
+        gate = gates[image, 0, head]
+        probs = jnp.exp(times_back(keys, query) * scale - lse[image, head : head + 1, :])
+        put(2 * width + low, wide, matmul(probs.astype(jnp.bfloat16), (grad.astype(jnp.float32) * gate).astype(jnp.bfloat16)))
+        grad_probs = times_back(values, grad)
+        inner = jnp.sum(grad_probs * probs, axis=0, keepdims=True)
+        grad_gates[image, head : head + 1, :] = inner
+        grad_scores = (probs * (grad_probs - inner) * (gate * scale)).astype(jnp.bfloat16)
+        put(low, wide, times_rows(grad_scores, keys))
+        put(width + low, wide, matmul(grad_scores, query))
+
+
+def attend(joint, gates, seq):
+    images, heads = gates.shape
+    def kernel(j, g, m, l):
+        attend_image(j, g, m, l, 0, seq, heads)
+    n = joint.shape[1]
+    return pl.pallas_call(
+        kernel, grid=(images,),
+        out_shape=[jax.ShapeDtypeStruct((joint.shape[0], n // 3), jnp.bfloat16), jax.ShapeDtypeStruct((images, heads, seq), jnp.float32)],
+        in_specs=[
+            pl.BlockSpec((seq, n), lambda i: (i, 0)),
+            pl.BlockSpec((1, 1, heads), lambda i: (i, 0, 0), memory_space=pltpu.SMEM),
+        ],
+        out_specs=[pl.BlockSpec((seq, n // 3), lambda i: (i, 0)), pl.BlockSpec((1, heads, seq), lambda i: (i, 0, 0))],
+        compiler_params=pltpu.CompilerParams(vmem_limit_bytes=48*2**20),
+        name="attend",
+    )(joint, gates[:, None, :])
+def attend_back(joint, grad_mixed, gates, lse, seq):
+    images, heads = gates.shape
+    n = joint.shape[1]
+    def kernel(j, gm, g, l, gj, gg):
+        attend_back_image(j, gm, g, l, gj, gg, 0, seq, heads)
+    gj, gg = pl.pallas_call(
+        kernel, grid=(images,),
+        out_shape=[jax.ShapeDtypeStruct(joint.shape, jnp.bfloat16), jax.ShapeDtypeStruct((images, heads, seq), jnp.float32)],
+        in_specs=[pl.BlockSpec((seq, n), lambda i: (i, 0)), pl.BlockSpec((seq, n//3), lambda i: (i, 0)), pl.BlockSpec((1, 1, heads), lambda i: (i, 0, 0), memory_space=pltpu.SMEM), pl.BlockSpec((1, heads, seq), lambda i: (i, 0, 0))],
+        out_specs=[pl.BlockSpec((seq, n), lambda i: (i, 0)), pl.BlockSpec((1, heads, seq), lambda i: (i, 0, 0))],
+        compiler_params=pltpu.CompilerParams(vmem_limit_bytes=48*2**20),
+        name="attend_back",
+    )(joint, grad_mixed, gates[:, None, :], lse)
+    return gj, jnp.sum(gg, axis=-1)
+
+
 def body(
     dp,
     fsdp,
@@ -543,8 +632,6 @@
 ):
     images, seq, width = tokens.shape
     heads = head_mask.shape[1]
-    size = width // heads
-    scale = size ** (-0.5)
     count = images * seq
     rows = qkv_weight.shape[0]
     hidden = fc1_weight.shape[1]
@@ -605,17 +692,7 @@
         (normed_one * (1.0 + scale_one) + shift_one).astype(jnp.bfloat16).reshape(count, width)
     )
     joint = matmul(flat_one, triple).astype(jnp.bfloat16)
-    query = joint[:, :width].reshape(images, seq, heads, size)
-    keys = joint[:, width : 2 * width].reshape(images, seq, heads, size)
-    values = joint[:, 2 * width :].reshape(images, seq, heads, size)
-    raw = jnp.einsum("ishe,ithe->ihst", query, keys, preferred_element_type=jnp.float32) * scale
-    peak = jnp.max(raw, axis=-1, keepdims=True)
-    expo = jnp.exp(raw - peak)
-    total = jnp.sum(expo, axis=-1, keepdims=True)
-    log_total = peak + jnp.log(total)
-    probs_low = (expo / total).astype(jnp.bfloat16)
-    attended = jnp.einsum("ihst,ithe->ishe", probs_low, values, preferred_element_type=jnp.float32)
-    mixed = (attended * head_gates[:, None, :, None]).astype(jnp.bfloat16).reshape(count, width)
+    mixed, log_total = attend(joint, head_gates, seq)
     attn = matmul(mixed, merger).reshape(images, seq, width)
     middle = inputs + gate_one * attn
     normed_two = layer_norm(middle)
@@ -648,41 +725,9 @@
     grad_gate_one = jnp.sum(grad_middle * attn, axis=1)
     grad_attn = (grad_middle * gate_one).astype(jnp.bfloat16).reshape(count, width)
     grad_merger = times_rows(mixed, grad_attn).astype(jnp.bfloat16)
-    grad_mixed = (
-        times_back(grad_attn, merger).astype(jnp.bfloat16).reshape(images, seq, heads, size)
-    )
-    grad_gates = jnp.sum(grad_mixed * attended, axis=(1, 3))
+    grad_mixed = times_back(grad_attn, merger).astype(jnp.bfloat16)
+    grad_joint, grad_gates = attend_back(joint, grad_mixed, head_gates, log_total, seq)
     grad_router = (grad_gates * mask_float * router_sig * (1.0 - router_sig)).astype(jnp.bfloat16)
-    grad_attended = (grad_mixed * head_gates[:, None, :, None]).astype(jnp.bfloat16)
-    again_raw = (
-        jnp.einsum("ishe,ithe->ihst", query, keys, preferred_element_type=jnp.float32) * scale
-    )
-    probs = jnp.exp(again_raw - log_total)
-    grad_values = jnp.einsum(
-        "ihst,ishe->ithe",
-        probs.astype(jnp.bfloat16),
-        grad_attended,
-        preferred_element_type=jnp.float32,
-    )
-    grad_probs = jnp.einsum(
-        "ishe,ithe->ihst", grad_attended, values, preferred_element_type=jnp.float32
-    )
-    inner = jnp.sum(grad_probs * probs, axis=-1, keepdims=True)
-    grad_scores = (probs * (grad_probs - inner) * scale).astype(jnp.bfloat16)
-    grad_query = jnp.einsum(
-        "ihst,ithe->ishe", grad_scores, keys, preferred_element_type=jnp.float32
-    )
-    grad_keys = jnp.einsum(
-        "ihst,ishe->ithe", grad_scores, query, preferred_element_type=jnp.float32
-    )
-    grad_joint = jnp.concatenate(
-        [
-            grad_query.reshape(count, width),
-            grad_keys.reshape(count, width),
-            grad_values.reshape(count, width),
-        ],
-        axis=1,
-    ).astype(jnp.bfloat16)
     grad_triple = times_rows(flat_one, grad_joint).astype(jnp.bfloat16)
     grad_h_one = times_back(grad_joint, triple).reshape(images, seq, width)
     grad_shift_one = jnp.sum(grad_h_one, axis=1)

time: 723 us -> 626 us (0.87)
  matrix products: 215 us -> 148 us
  local copies, waits for them, and re-layouts: 83.9 us -> 26.7 us
  Pallas kernels: 365 us -> 398 us
    dot_general x6 -> x0, matrix products: 61.2 us -> none  [the longest x1 19.9 us: body(): jnp.einsum('ihst,ithe->ishe', grad_scores, keys, preferred_element_type=j...]
    pallas_call x0 -> x2, Pallas kernels: none -> 33.3 us  [the longest x1 23.5 us: attend_back(): pl.pallas_call(kernel, grid=(images,), out_shape=[jax.ShapeDtypeStruct(jo...]
    reshape x6 -> x0, local copies, waits for them, and re-layouts: 30.1 us -> none  [the longest x2 10.1 us: body(): values = joint[:, 2 * width:].reshape(images, seq, heads, size)]
    convert_element_type x3 -> x0, local copies, waits for them, and re-layouts: 15.4 us -> none  [the longest x2 13.9 us: body(): grad_mixed * head_gates[:, None, :, None]]
    unnamed x152 -> x134, local copies, waits for them, and re-layouts: 24.6 us -> 20.1 us
where the time goes in v3:
time: 626 us; the launch traced here: 618 us
  Pallas kernels  398 us (64%)
  matrix products  148 us (24%)
  other arithmetic  43.8 us (7%)
  local copies, waits for them, and re-layouts  26.7 us (4%)
    pallas_call x1, Pallas kernels, reduce_terms(): pl.pallas_call(partial(reduce_kernel, dp, fsdp, width), out_shape=[out((Q...  218 us
    pallas_call x1, Pallas kernels, gather_weights(): pl.pallas_call(partial(gather_kernel, dp, fsdp, width), out_shape=[out((f...  147 us
    dot_general x6, matrix products, matmul(): return jnp.dot(left, right, preferred_element_type=jnp.float32)  59.5 us
    dot_general x9, matrix products, times_rows(): lax.dot_general(left, right, (((0,), (0,)), ((), ())), preferred_element_...  45.8 us
    dot_general x5, matrix products, times_back(): lax.dot_general(left, right, (((1,), (1,)), ((), ())), preferred_element_...  42.3 us
    pallas_call x1, Pallas kernels, attend_back(): pl.pallas_call(kernel, grid=(images,), out_shape=[jax.ShapeDtypeStruct(jo...  23.5 us
    unnamed x134, local copies, waits for them, and re-layouts  20.1 us

profile of v3, /device:TPU:0, one launch (start us, length us, event | category | flops | bytes accessed | tf_op | source)
XLA Modules:
  0.0 617.8 jit_solution(2253505431787421930)
XLA Ops:
  2.8 1.8 convert_reduce_fusion
  4.7 2.1 fusion.27
  8.6 2.9 copy.48.refs_6_.refs_4_
  15.2 146.7 %gather.1 = (bf16[8,144,4608]{2,1,0:T(8,128)(2,1)S(1)}, bf16[8,144,4608]{2,1,0:T(8,128)(2,1)}, bf16[8,4,144,1152]{3,2,1,0:T(8,128)(2,1)}, f32[8,1152]{1,0:T(8,12...) custom-call(bf16[144,4608]{1,0:T(8,128)(2,1)S(1)} %pad_maximum_fusio, ...), custom_call_target="tpu_custom_call" | custom-call | tf_op jit(solution)/shard_map/gather/pallas_call | solution.py:276
  162.9 3.9 copy-done.10
  169.0 1.6 slice.80
  171.3 2.1 convert_element_type.131
  173.4 2.8 fusion.23
  177.4 12.2 %fusion.11.j = bf16[768,3456]{1,0:T(8,128)(2,1)} fusion(bf16[768,1152]{1,0:T(8,128)(2,1)S(1)} %bitcast.124, bf16[1152,4608]{1,0:T(8,128)(2,1)} %bitcast.99), kind=kOutput, calls=%fused_computation.19 | convolution fusion | flops 6117949440 | bytes 15040512 | tf_op jit(solution)/shard_map/dot_general | solution.py:34
  189.6 9.7 %attend.1 = (bf16[768,1152]{1,0:T(8,128)(2,1)S(1)}, f32[3,16,256]{2,1,0:T(8,128)S(1)}) custom-call(bf16[768,3456]{1,0:T(8,128)(2,1)} %fusion.11.j, f32[3,1,16]{2,1,0:T(1,128)S(1)} %copy.50.g), custom_call_target="tpu_custom_call" | custom-call | tf_op jit(solution)/shard_map/attend/pallas_call | solution.py:587
  199.4 4.6 fusion.32
  209.4 1.9 fusion.25
  212.6 15.1 %fusion.71 = f32[768,4608]{1,0:T(8,128)} fusion(bf16[768,1152]{1,0:T(8,128)(2,1)S(1)} %bitcast.126, bf16[4608,1152]{1,0:T(8,128)(2,1)} %bitcast.134), kind=kOutput, calls=%fused_computation.154 | convolution fusion | flops 8153726976 | bytes 26542080 | tf_op jit(solution)/shard_map/dot_general | solution.py:44
  227.7 24.7 %fusion.6 = (bf16[768,4608]{1,0:T(8,128)(2,1)}, bf16[768,4608]{1,0:T(8,128)(2,1)}) fusion(f32[768,4608]{1,0:T(8,128)} %fusion.71, bf16[768,1152]{1,0:T(8,128)(2,1)S(1)} %bitcast.110, bf16[1152,4608]{1,0:T(8,128)(2,1)} %bitcast.132), kind=kOutput, calls=%fused_computation.11 | convolution fusion | flops 8231583744 | bytes 40697856 | tf_op jit(solution)/shard_map/dot_general | solution.py:34
  252.4 17.3 %fusion.30 = (bf16[3,1152]{1,0:T(4,128)(2,1)S(1)}, f32[3,256]{1,0:T(4,128)S(1)}, bf16[3,256,1152]{2,1,0:T(8,128)(2,1)}) fusion(bf16[3,256,1152]{2,1,0:T(8,128)(2,1)} %param.20, f32[3,256]{1,0:T(4,128)S(1)} %convert_multiply_fusion.2, f32[3,1152]{1,0:T(4,128)S(1)} %get-tuple-element.70, f32[3,256,1152]{2,1,0:T(8,128)} %copy-done.11, ...), kind=kOutput, calls=%fused_computation.46 | convolution fusion | flops 8163454976 | bytes 24799488 | tf_op jit(solution)/shard_map/dot_general | solution.py:34
  269.7 13.6 %convolution_add_fusion = f32[768,1152]{1,0:T(8,128)S(1)} fusion(bf16[768,4608]{1,0:T(8,128)(2,1)} %get-tuple-element.57, bf16[1152,4608]{1,0:T(8,128)(2,1)} %bitcast.133, f32[1152]{0:T(1024)S(1)} %convert.46, f32[768]{0:T(1024)S(1)} %reshape.206), kind=kOutput, calls=%fused_computation.36 | convolution fusion | flops 8155496448 | bytes 21241344 | tf_op jit(solution)/shard_map/dot_general | solution.py:44
  285.2 2.9 fusion.69
  289.9 4.0 convolution_convert_fusion.3
  293.9 2.7 convolution_convert_fusion.4.gm
  296.7 23.5 %attend_back.1 = (bf16[768,3456]{1,0:T(8,128)(2,1)}, f32[3,16,256]{2,1,0:T(8,128)S(1)}) custom-call(bf16[768,3456]{1,0:T(8,128)(2,1)} %fusion.11.j, bf16[768,1152]{1,0:T(8,128)(2,1)S(1)} %convolution_convert_fusion.4.gm, f32[3,1,16]{2,1,0:T(1,128)S(1)} %copy.50.g, f32[3,16,256]{2,1,0:T(8,128)S(1)} %get-tuple-element.35.l), custom_call_target="tpu_custom_call" | custom-call | tf_op jit(solution)/shard_map/attend_back/pallas_call | solution.py:603
  320.2 10.7 %fusion.7 = f32[768,1152]{1,0:T(8,128)} fusion(bf16[768,3456]{1,0:T(8,128)(2,1)} %get-tuple-element.36, bf16[1152,4608]{1,0:T(8,128)(2,1)S(1)} %bitcast.104), kind=kOutput, calls=%fused_computation.15 | convolution fusion | flops 6115295232 | bytes 16809984 | tf_op jit(solution)/shard_map/dot_general | solution.py:44
  331.2 3.4 fusion.28
  335.3 3.3 fusion.24
  338.7 2.8 add_add_fusion.2
  343.2 13.9 %convolution_convert_fusion.1 = bf16[1152,4608]{1,0:T(8,128)(2,1)} fusion(bf16[768,1152]{1,0:T(8,128)(2,1)S(1)} %bitcast.111, bf16[768,4608]{1,0:T(8,128)(2,1)} %get-tuple-element.57), kind=kOutput, calls=%fused_computation.3 | convolution fusion | flops 8159035392 | bytes 19464192 | tf_op jit(solution)/shard_map/dot_general | solution.py:38
  357.2 9.7 %convolution_convert_fusion.2 = bf16[1152,3456]{1,0:T(8,128)(2,1)S(1)} fusion(bf16[768,1152]{1,0:T(8,128)(2,1)S(1)} %bitcast.125, bf16[768,3456]{1,0:T(8,128)(2,1)} %get-tuple-element.36), kind=kOutput, calls=%fused_computation.4 | convolution fusion | flops 6119276544 | bytes 15040512 | tf_op jit(solution)/shard_map/dot_general | solution.py:38
  366.9 4.6 pad_maximum_fusion
  371.5 12.0 %convolution_convert_fusion = bf16[4608,1152]{1,0:T(8,128)(2,1)} fusion(bf16[768,4608]{1,0:T(8,128)(2,1)S(1)} %bitcast.138, bf16[768,1152]{1,0:T(8,128)(2,1)S(1)} %bitcast.127), kind=kOutput, calls=%fused_computation.2 | convolution fusion | flops 8159035392 | bytes 19464192 | tf_op jit(solution)/shard_map/dot_general | solution.py:38
  383.5 217.8 %reduce.6 = (bf16[4,144,1152]{2,1,0:T(8,128)(2,1)}, bf16[4,144,1152]{2,1,0:T(8,128)(2,1)}, bf16[4,144,1152]{2,1,0:T(8,128)(2,1)}, f32[4,8,8,864]{3,2,1,0:T(8,128)}, f32[4,8,8,1280]{3,2,1,0:T(8,128)}) custom-call(bf16[8,144,4608]{2,1,0:T(8,128)(2,1)} %bitcast.105, bf16[8,144,4608]{2,1,0:T(8,128)(2,1)} %bitcast.116, bf16[8,4,144,1152]{3,2,1,0:T(8,128)(2,1)} %bitcast.117, ...), custom_call_target="tpu_custom_call" | custom-call | tf_op jit(solution)/shard_map/reduce/pallas_call | solution.py:511
  611.1 1.8 pad_maximum_fusion.1
  612.9 1.8 bitcast_convert_fusion
  614.7 2.7 convolution_bitcast_fusion
  (199 shorter events, 35.2 us)
Async XLA Ops:
  0.6 6.7 %copy-start.56 = (bf16[144,1]{0,1:T(2,128)(2,1)S(1)}, bf16[144,1]{0,1:T(2,128)(2,1)}, u32[]{:S(2)}) copy-start(bf16[144,1]{0,1:T(2,128)(2,1)} %param.29) | copy-start | bytes 868
  0.7 7.9 %copy-start.40 = (bf16[144,1152]{1,0:T(8,128)(2,1)S(1)}, bf16[144,1152]{1,0:T(8,128)(2,1)}, u32[]{:S(2)}) copy-start(bf16[144,1152]{1,0:T(8,128)(2,1)} %param.26) | copy-start | bytes 995332
  0.7 7.8 %copy-start.36 = (bf16[144,3456]{1,0:T(8,128)(2,1)S(1)}, bf16[144,3456]{1,0:T(8,128)(2,1)}, u32[]{:S(2)}) copy-start(bf16[144,3456]{1,0:T(8,128)(2,1)} %param.25) | copy-start | bytes 2985988
  0.7 6.7 %copy-start.54 = (bf16[144,16]{0,1:T(8,128)(2,1)S(1)}, bf16[144,16]{0,1:T(8,128)(2,1)}, u32[]{:S(2)}) copy-start(bf16[144,16]{0,1:T(8,128)(2,1)} %param.24) | copy-start | bytes 13828
  0.7 6.8 %copy-start.41 = (bf16[1000,144]{0,1:T(8,128)(2,1)S(1)}, bf16[1000,144]{0,1:T(8,128)(2,1)}, u32[]{:S(2)}) copy-start(bf16[1000,144]{0,1:T(8,128)(2,1)} %param.22) | copy-start | bytes 864004
  4.6 168.8 %copy-start.43 = (f32[3,256]{1,0:T(4,128)}, f32[3,256]{1,0:T(4,128)S(1)}, u32[]{:S(2)}) copy-start(f32[3,256]{1,0:T(4,128)S(1)} %broadcast_multiply_fusion.1) | copy-start | bytes 9220
  6.8 166.7 %copy-start.45 = (f32[3,256]{1,0:T(4,128)}, f32[3,256]{1,0:T(4,128)S(1)}, u32[]{:S(2)}) copy-start(f32[3,256]{1,0:T(4,128)S(1)} %fusion.59) | copy-start | bytes 9220
  15.2 151.7 %copy-start = (bf16[1152,864]{1,0:T(8,128)(2,1)}, bf16[1152,864]{1,0:T(8,128)(2,1)S(1)}, u32[]{:S(2)}) copy-start(bf16[1152,864]{1,0:T(8,128)(2,1)S(1)} %copy.48.refs_6_.refs_4_) | copy-start | bytes 5971972
  15.2 151.8 %copy-start.50 = (s32[3,16]{1,0:T(4,128)S(1)}, s32[3,16]{1,0:T(4,128)}, u32[]{:S(2)}) copy-start(s32[3,16]{1,0:T(4,128)} %param.18) | copy-start | bytes 580
  168.1 8.1 %copy-start.38 = (f32[3,1152]{1,0:T(4,128)}, f32[3,1152]{1,0:T(4,128)S(1)}, u32[]{:S(2)}) copy-start(f32[3,1152]{1,0:T(4,128)S(1)} %get-tuple-element.74) | copy-start | bytes 41476
  199.3 4.6 copy-start.13
  212.6 15.1 %copy-start.19 = (bf16[3,256,1152]{2,1,0:T(8,128)(2,1)S(1)}, bf16[3,256,1152]{2,1,0:T(8,128)(2,1)}, u32[]{:S(2)}) copy-start(bf16[3,256,1152]{2,1,0:T(8,128)(2,1)} %copy-done.18) | copy-start | bytes 5308420
  269.7 13.7 %copy-start.20 = (bf16[3,256,1152]{2,1,0:T(8,128)(2,1)S(1)}, bf16[3,256,1152]{2,1,0:T(8,128)(2,1)}, u32[]{:S(2)}) copy-start(bf16[3,256,1152]{2,1,0:T(8,128)(2,1)} %copy-done.18) | copy-start | bytes 5308420
  269.7 14.0 %copy-start.12 = (f32[3,256,1152]{2,1,0:T(8,128)S(1)}, f32[3,256,1152]{2,1,0:T(8,128)}, u32[]{:S(2)}) copy-start(f32[3,256,1152]{2,1,0:T(8,128)} %copy-done.11) | copy-start | bytes 10616836
  288.8 5.2 slice-start
  288.8 5.2 slice-start.1
  320.2 10.8 %copy-start.51 = (s32[3,16]{1,0:T(4,128)S(1)}, s32[3,16]{1,0:T(4,128)}, u32[]{:S(2)}) copy-start(s32[3,16]{1,0:T(4,128)} %param.18) | copy-start | bytes 580
  320.2 10.8 %copy-start.53 = (f32[3,16]{1,0:T(4,128)S(1)}, f32[3,16]{1,0:T(4,128)}, u32[]{:S(2)}) copy-start(f32[3,16]{1,0:T(4,128)} %copy-done.52) | copy-start | bytes 580
  320.2 11.0 %copy-start.39 = (f32[3,1152]{1,0:T(4,128)S(1)}, f32[3,1152]{1,0:T(4,128)}, u32[]{:S(2)}) copy-start(f32[3,1152]{1,0:T(4,128)} %copy-done.38) | copy-start | bytes 41476
  320.2 11.0 %copy-start.44 = (f32[3,256]{1,0:T(4,128)S(1)}, f32[3,256]{1,0:T(4,128)}, u32[]{:S(2)}) copy-start(f32[3,256]{1,0:T(4,128)} %copy-done.43) | copy-start | bytes 9220
  331.2 7.4 %copy-start.23 = (bf16[3,256,1152]{2,1,0:T(8,128)(2,1)S(1)}, bf16[3,256,1152]{2,1,0:T(8,128)(2,1)}, u32[]{:S(2)}) copy-start(bf16[3,256,1152]{2,1,0:T(8,128)(2,1)} %param.20) | copy-start | bytes 5308420
  338.7 4.5 copy-start.21
  343.2 13.9 %copy-start.30 = (bf16[3,256,1152]{2,1,0:T(8,128)(2,1)S(1)}, bf16[3,256,1152]{2,1,0:T(8,128)(2,1)}, u32[]{:S(2)}) copy-start(bf16[3,256,1152]{2,1,0:T(8,128)(2,1)} %copy-done.29) | copy-start | bytes 5308420
  343.2 28.3 %slice-start.3 = ((s8[7077888]{0:T(1024)(128)(4,1)}), s8[4194304]{0:T(1024)(128)(4,1)S(1)}, s32[]{:S(2)}) async-start(s8[7077888]{0:T(1024)(128)(4,1)} %bitcast.137), calls=%async_computation.3 | async-start | bytes 8388608
  357.2 9.8 %copy-start.28 = (bf16[1152,1152]{1,0:T(8,128)(2,1)S(1)}, bf16[1152,1152]{1,0:T(8,128)(2,1)}, u32[]{:S(2)}) copy-start(bf16[1152,1152]{1,0:T(8,128)(2,1)} %convolution_convert_fusion.3) | copy-start | bytes 7962628
  357.2 14.3 %slice-start.4 = ((s8[7077888]{0:T(1024)(128)(4,1)}), s8[2883584]{0:T(1024)(128)(4,1)S(1)}, s32[]{:S(2)}) async-start(s8[7077888]{0:T(1024)(128)(4,1)} %bitcast.137), calls=%async_computation.4 | async-start | bytes 5767168
  366.9 4.6 copy-start.32
  383.5 219.3 %copy-start.57 = (pred[8]{0:T(512)(128)(4,1)S(1)}, pred[8]{0:T(512)(128)(4,1)}, u32[]{:S(2)}) copy-start(pred[8]{0:T(512)(128)(4,1)} %iota_compare_fusion.4) | copy-start | bytes 28
  383.5 221.5 %copy-start.42 = (bf16[256,256]{1,0:T(8,128)(2,1)S(1)}, bf16[256,256]{1,0:T(8,128)(2,1)}, u32[]{:S(2)}) copy-start(bf16[256,256]{1,0:T(8,128)(2,1)} %slice.80) | copy-start | bytes 393220
  383.5 222.4 %copy-start.27 = (bf16[4,8,8,1152]{3,2,1,0:T(8,128)(2,1)S(1)}, bf16[4,8,8,1152]{3,2,1,0:T(8,128)(2,1)}, u32[]{:S(2)}) copy-start(bf16[4,8,8,1152]{3,2,1,0:T(8,128)(2,1)} %convert_element_type.131) | copy-start | bytes 1769476
  601.3 5.6 copy-start.55
  601.3 6.8 %copy-start.35 = (bf16[4,144,1152]{2,1,0:T(8,128)(2,1)S(1)}, bf16[4,144,1152]{2,1,0:T(8,128)(2,1)}, u32[]{:S(2)}) copy-start(bf16[4,144,1152]{2,1,0:T(8,128)(2,1)} %get-tuple-element.42) | copy-start | bytes 3981316
  (31 other events, 71.4 us)

commit v4 on v3

--- a/solution.py
+++ b/solution.py
@@ -304,224 +304,6 @@
     )(*shards, asked, time_weight, class_table, ada_weight, routers)
 
 
-def reduce_kernel(dp, fsdp, width, *refs):
-    weights = 3
-    ring = fsdp // 2
-    terms, refs = refs[:weights], refs[weights:]
-    gm_ref, ada_ref, routed_ref, pre_ref, last_ref = refs[:5]
-    refs = refs[5:]
-    outs, refs = refs[:weights], refs[weights:]
-    all_gm_ref, all_pre_ref = refs[:2]
-    refs = refs[2:]
-    (
-        own, pair, first_a, first_b, second_a, second_b, hops, done, gms, parts, mine_in, pres,
-        load, core_s, core_r, xa_s, xa_r, yb_s, yb_r, ya_s, ya_r, xb_s, xb_r, ring_s, ring_r,
-        end_s, end_r, out_sem, mate_s, mate_r, cousin_s, cousin_r, small_sem,
-    ) = refs
-    at = Place(dp, fsdp)
-    part_a, part_b = cut(width)
-    cols_a, cols_b = pl.ds(*part_a), pl.ds(*part_b)
-    rows = slice(None)
-    sent = []
-
-    def go(copy):
-        copy.start()
-        sent.append(copy)
-        return copy
-
-    at.greet()
-    items = [(k, j) for k in range(weights) for j in range(ring)]
-    loads, pairs = {}, {}
-    other = 1 - 2 * at.c
-    for k, j in items:
-        back = (j + 1) % ring
-        mine = at.shard(back)
-        loads[k, j] = []
-        for q in range(QUARTERS):
-            copy = pltpu.make_async_copy(view(terms[k], (mine,), q, width), own.at[k, j, q], load.at[k, j, q])
-            copy.start()
-            loads[k, j].append(copy)
-        pairs[k, j] = [
-            go(remote(view(terms[k], (mine + other,), q, width), pair.at[k, j, q], core_s.at[k, j, q], core_r.at[k, j, q], at.core))
-            for q in range(QUARTERS)
-        ]
-    flights, rings, ends = {}, {}, {}
-
-    mates, cousins = at.mates(), at.cousins()
-    swaps = [Swap(mates, mate_s.at[i], mate_r.at[i]) for i in range(3)]
-    far = [Swap(cousins, cousin_s.at[i], cousin_r.at[i]) for i in range(2)]
-    pad = pre_ref.shape[0]
-    small = []
-
-    def keep(src, dst):
-        copy = pltpu.make_async_copy(src, dst, small_sem.at[len(small)])
-        copy.start()
-        small.append(copy)
-
-    def cond_one():
-        swaps[0].arrived()
-        gms[at.f] = gm_ref[at.f]
-        every = gms[...].reshape(fsdp * pad, gms.shape[2]).astype(jnp.bfloat16)
-        parts[...] = times_back(every, ada_ref[...]).reshape(parts.shape)
-        swaps[1].start(lambda device: parts.at[device[1]], mine_in.at[at.f])
-        far[0].start(lambda device: gms, all_gm_ref.at[at.d])
-        keep(gms, all_gm_ref.at[at.d])
-
-    def cond_two():
-        swaps[1].arrived()
-        mine_in[at.f] = parts[at.f]
-        grad_cond = jnp.sum(mine_in[...], axis=0) + routed_ref[...]
-        pre_cond = pre_ref[...]
-        sig = jax.nn.sigmoid(pre_cond)
-        grad_pre = grad_cond * (sig * (1.0 + pre_cond * (1.0 - sig)))
-        grad_pre = grad_pre.astype(jnp.bfloat16).astype(jnp.float32)
-        pres[at.f, :, :width] = grad_pre + last_ref[:, :width]
-        pres[at.f, :, width:] = last_ref[:, width:]
-        swaps[2].start(lambda device: pres.at[at.f], pres.at[at.f])
-
-    def cond_three():
-        swaps[2].arrived()
-        far[1].start(lambda device: pres, all_pre_ref.at[at.d])
-        keep(pres, all_pre_ref.at[at.d])
-
-    extra = {1: cond_one, 3: cond_two, 5: cond_three}
-    swaps[0].start(lambda device: gm_ref.at[device[1]], gms.at[at.f])
-
-    def stage_one(k, j):
-        for q in range(QUARTERS):
-            loads[k, j][q].wait()
-            pairs[k, j][q].wait_recv()
-            own[k, j, q] = own[k, j, q] + pair[k, j, q]
-        flights[k, j] = [
-            go(remote(own.at[k, j, at.qx, rows, cols_a], first_a.at[k, j, 0], xa_s.at[k, j, 0], xa_r.at[k, j, 0], at.x)),
-            go(remote(own.at[k, j, at.qd, rows, cols_a], first_a.at[k, j, 1], xa_s.at[k, j, 1], xa_r.at[k, j, 1], at.x)),
-            go(remote(own.at[k, j, at.qy, rows, cols_b], first_b.at[k, j, 0], yb_s.at[k, j, 0], yb_r.at[k, j, 0], at.y)),
-            go(remote(own.at[k, j, at.qd, rows, cols_b], first_b.at[k, j, 1], yb_s.at[k, j, 1], yb_r.at[k, j, 1], at.y)),
-        ]
-
-    def stage_two(k, j):
-        one, two, three, four = flights[k, j]
-        two.wait_recv()
-        own[k, j, at.qy, :, cols_a] = own[k, j, at.qy, :, cols_a] + first_a[k, j, 1]
-        next_a = go(remote(own.at[k, j, at.qy, rows, cols_a], second_a.at[k, j], ya_s.at[k, j], ya_r.at[k, j], at.y))
-        four.wait_recv()
-        own[k, j, at.qx, :, cols_b] = own[k, j, at.qx, :, cols_b] + first_b[k, j, 1]
-        next_b = go(remote(own.at[k, j, at.qx, rows, cols_b], second_b.at[k, j], xb_s.at[k, j], xb_r.at[k, j], at.x))
-        one.wait_recv()
-        own[k, j, at.q, :, cols_a] = own[k, j, at.q, :, cols_a] + first_a[k, j, 0]
-        three.wait_recv()
-        own[k, j, at.q, :, cols_b] = own[k, j, at.q, :, cols_b] + first_b[k, j, 0]
-        flights[k, j] = [next_a, next_b]
-
-    def stage_three(k, j):
-        for copy in flights[k, j]:
-            copy.wait_recv()
-        own[k, j, at.q, :, cols_a] = own[k, j, at.q, :, cols_a] + second_a[k, j]
-        own[k, j, at.q, :, cols_b] = own[k, j, at.q, :, cols_b] + second_b[k, j]
-        if j > 0:
-            rings[k, j - 1].wait_recv()
-            own[k, j, at.q] = own[k, j, at.q] + hops[k, j - 1]
-        if j < ring - 1:
-            rings[k, j] = go(remote(own.at[k, j, at.q], hops.at[k, j], ring_s.at[k, j], ring_r.at[k, j], at.up))
-            return
-        done[k, at.q] = own[k, j, at.q]
-        mine = done.at[k, at.q]
-        ends[k] = [
-            go(remote(mine, mine, end_s.at[k, 0], end_r.at[k, 0], at.x)),
-            go(remote(mine, mine, end_s.at[k, 1], end_r.at[k, 1], at.y)),
-        ]
-
-    def stage_four(k):
-        by_x, by_y = ends[k]
-        by_x.wait_recv()
-        half = done.at[k, at.qx, rows, cols_a]
-        first = go(remote(half, half, end_s.at[k, 2], end_r.at[k, 2], at.y))
-        by_y.wait_recv()
-        half = done.at[k, at.qy, rows, cols_b]
-        second = go(remote(half, half, end_s.at[k, 3], end_r.at[k, 3], at.x))
-        ends[k] = [first, second]
-
-    outgoing = []
-
-    def stage_five(k):
-        for copy in ends[k]:
-            copy.wait_recv()
-        copy = pltpu.make_async_copy(done.at[k], outs[k], out_sem.at[k])
-        copy.start()
-        outgoing.append(copy)
-
-    for turn in range(len(items) + 4):
-        if turn < len(items):
-            stage_one(*items[turn])
-        if 0 <= turn - 1 < len(items):
-            stage_two(*items[turn - 1])
-        if 0 <= turn - 2 < len(items):
-            stage_three(*items[turn - 2])
-        if 0 <= turn - 3 < len(items) and items[turn - 3][1] == ring - 1:
-            stage_four(items[turn - 3][0])
-        if 0 <= turn - 4 < len(items) and items[turn - 4][1] == ring - 1:
-            stage_five(items[turn - 4][0])
-        if turn in extra:
-            extra[turn]()
-    for swap in far:
-        swap.arrived()
-    for copy in outgoing + small:
-        copy.wait()
-    for swap in swaps + far:
-        swap.left()
-    for copy in sent:
-        copy.wait_send()
-
-
-def reduce_terms(terms, grad_modulation, ada_weight, routed, pre_cond, last, rows, width, dp, fsdp):
-    ring = fsdp // 2
-    dma = pltpu.SemaphoreType.DMA
-    low = jnp.bfloat16
-    (_, size_a), (_, size_b) = cut(width)
-    vmem = pltpu.VMEM
-    f32 = jnp.float32
-    pad = pre_cond.shape[0]
-    out = jax.ShapeDtypeStruct
-    any_space, in_vmem = pl.BlockSpec(memory_space=pl.ANY), pl.BlockSpec(memory_space=vmem)
-    scratch = [
-        vmem((3, ring, QUARTERS, rows, width), low),
-        vmem((3, ring, QUARTERS, rows, width), low),
-        vmem((3, ring, 2, rows, size_a), low),
-        vmem((3, ring, 2, rows, size_b), low),
-        vmem((3, ring, rows, size_a), low),
-        vmem((3, ring, rows, size_b), low),
-        vmem((3, ring - 1, rows, width), low),
-        vmem((3, QUARTERS, rows, width), low),
-        vmem(grad_modulation.shape, f32),
-        vmem((fsdp, pad, width), f32),
-        vmem((fsdp, pad, width), f32),
-        vmem((fsdp, *last.shape), f32),
-    ]
-    sems = (
-        [dma((3, ring, QUARTERS))] * 3
-        + [dma((3, ring, 2))] * 4
-        + [dma((3, ring))] * 4
-        + [dma((3, ring - 1))] * 2
-        + [dma((3, 4))] * 2
-        + [dma((3,))]
-        + [dma((3, fsdp - 1))] * 2
-        + [dma((2, dp - 1))] * 2
-        + [dma((2,))]
-    )
-    return pl.pallas_call(
-        partial(reduce_kernel, dp, fsdp, width),
-        out_shape=[out((QUARTERS, rows, width), low)] * 3
-        + [out((dp, *grad_modulation.shape), f32), out((dp, fsdp, *last.shape), f32)],
-        in_specs=[any_space] * 3 + [in_vmem] * 5,
-        out_specs=[any_space] * 5,
-        scratch_shapes=scratch + sems,
-        compiler_params=pltpu.CompilerParams(
-            collective_id=1, has_side_effects=True, vmem_limit_bytes=60 * 2**20
-        ),
-        name="reduce",
-    )(*terms, grad_modulation, ada_weight, routed, pre_cond, last)
-
-
 def window(head, size):
     low = head * size // 128 * 128
     high = -(-(head + 1) * size // 128) * 128
@@ -551,23 +333,23 @@
         mixed[lines, pl.ds(low, wide)] = mixed[lines, pl.ds(low, wide)] + attended.astype(jnp.bfloat16)
 
 
-def attend_back_image(joint, grad_mixed, gates, lse, grad_joint, grad_gates, image, seq, heads):
+def attend_back_image(joint, grad_mixed, gates, lse, grad_joint, grad_gates, image, seq, heads, span):
     width = grad_mixed.shape[1]
     size = width // heads
     scale = size ** (-0.5)
-    lines = pl.ds(pl.multiple_of(image * seq, seq), seq)
-    grad_joint[lines, :] = jnp.zeros((seq, 3 * width), grad_joint.dtype)
+    if span[0] == 0:
+        grad_joint[...] = jnp.zeros((seq, 3 * width), grad_joint.dtype)
 
     def put(column, wide, value):
         here = pl.ds(column, wide)
-        grad_joint[lines, here] = grad_joint[lines, here] + value.astype(jnp.bfloat16)
-
-    for head in range(heads):
+        grad_joint[:, here] = grad_joint[:, here] + value.astype(jnp.bfloat16)
+
+    for head in span:
         low, wide, own = window(head, size)
-        query = joint[lines, pl.ds(low, wide)] * own
-        keys = joint[lines, pl.ds(width + low, wide)] * own
-        values = joint[lines, pl.ds(2 * width + low, wide)]
-        grad = grad_mixed[lines, pl.ds(low, wide)] * own
+        query = joint[:, pl.ds(low, wide)] * own
+        keys = joint[:, pl.ds(width + low, wide)] * own
+        values = joint[:, pl.ds(2 * width + low, wide)]
+        grad = grad_mixed[:, pl.ds(low, wide)] * own
         gate = gates[image, 0, head]
         probs = jnp.exp(times_back(keys, query) * scale - lse[image, head : head + 1, :])
         put(2 * width + low, wide, matmul(probs.astype(jnp.bfloat16), (grad.astype(jnp.float32) * gate).astype(jnp.bfloat16)))
@@ -595,20 +377,543 @@
         compiler_params=pltpu.CompilerParams(vmem_limit_bytes=48*2**20),
         name="attend",
     )(joint, gates[:, None, :])
-def attend_back(joint, grad_mixed, gates, lse, seq):
-    images, heads = gates.shape
-    n = joint.shape[1]
-    def kernel(j, gm, g, l, gj, gg):
-        attend_back_image(j, gm, g, l, gj, gg, 0, seq, heads)
-    gj, gg = pl.pallas_call(
-        kernel, grid=(images,),
-        out_shape=[jax.ShapeDtypeStruct(joint.shape, jnp.bfloat16), jax.ShapeDtypeStruct((images, heads, seq), jnp.float32)],
-        in_specs=[pl.BlockSpec((seq, n), lambda i: (i, 0)), pl.BlockSpec((seq, n//3), lambda i: (i, 0)), pl.BlockSpec((1, 1, heads), lambda i: (i, 0, 0), memory_space=pltpu.SMEM), pl.BlockSpec((1, heads, seq), lambda i: (i, 0, 0))],
-        out_specs=[pl.BlockSpec((seq, n), lambda i: (i, 0)), pl.BlockSpec((1, heads, seq), lambda i: (i, 0, 0))],
-        compiler_params=pltpu.CompilerParams(vmem_limit_bytes=48*2**20),
-        name="attend_back",
-    )(joint, grad_mixed, gates[:, None, :], lse)
-    return gj, jnp.sum(gg, axis=-1)
+def thirds(width):
+    tiles = width // 128
+    a, b = tiles // 3, tiles // 3
+    c = tiles - a - b
+    sizes = [a, b, (c + 1) // 2, c // 2]
+    starts = [sum(sizes[:i]) for i in range(4)]
+    return [(128 * s, 128 * n) for s, n in zip(starts, sizes)]
+
+
+OWN_SLOTS = 5
+PAIR_SLOTS = 3
+
+
+class Reducer:
+    def __init__(self, at, piece, outs, scratch, width):
+        self.at, self.piece, self.outs, self.width = at, piece, outs, width
+        (
+            self.own, self.pair, self.first_a, self.first_b, self.second_a, self.second_b,
+            self.hops, self.hops_c, self.flat_a, self.flat_b, self.last_a, self.last_b, self.done,
+            self.own_in, self.core_s, self.core_r, self.fa_s, self.fa_r, self.fb_s, self.fb_r,
+            self.sa_s, self.sa_r, self.sb_s, self.sb_r, self.hop_s, self.hop_r, self.hopc_s, self.hopc_r,
+            self.ca_s, self.ca_r, self.cb_s, self.cb_r, self.end_s, self.end_r, self.out_sem, self.credit,
+        ) = scratch
+        self.ring = at.ring
+        self.total = 3 * self.ring
+        self.sent, self.flights = {}, {}
+        self.loose, self.outgoing = [], []
+        self.cols = [pl.ds(*part) for part in thirds(width)]
+        a, b = thirds(width)[1]
+        self.cols_ab = pl.ds(0, a + b)
+        self.cols_c = pl.ds(a + b, width - a - b)
+
+    @staticmethod
+    def scratch(rows, width, fsdp):
+        ring = fsdp // 2
+        total = 3 * ring
+        low, vmem, dma = jnp.bfloat16, pltpu.VMEM, pltpu.SemaphoreType.DMA
+        a, b, c, d = [size for _, size in thirds(width)]
+        arrays = [
+            vmem((OWN_SLOTS, QUARTERS, rows, width), low),
+            vmem((PAIR_SLOTS, QUARTERS, rows, width), low),
+            vmem((total, 2, rows, a), low),
+            vmem((total, 2, rows, b), low),
+            vmem((total, rows, a), low),
+            vmem((total, rows, b), low),
+            vmem((3, ring - 1, rows, a + b), low),
+            vmem((3, ring - 1, QUARTERS, rows, c + d), low),
+            vmem((3, 2, rows, c), low),
+            vmem((3, 2, rows, d), low),
+            vmem((3, rows, c), low),
+            vmem((3, rows, d), low),
+            vmem((3, QUARTERS, rows, width), low),
+        ]
+        sems = (
+            [dma((total, QUARTERS))] * 3
+            + [dma((total, 2))] * 4
+            + [dma((total,))] * 4
+            + [dma((3, ring - 1))] * 4
+            + [dma((3, 3))] * 4
+            + [dma((3, 4))] * 2
+            + [dma((3,))]
+            + [pltpu.SemaphoreType.REGULAR]
+        )
+        return arrays + sems
+
+    def go(self, n, *parts):
+        copy = remote(*parts)
+        copy.start()
+        self.sent.setdefault(n, []).append(copy)
+        return copy
+
+    def prefetch(self, n):
+        at = self.at
+        k, j = divmod(n, self.ring)
+        slot, pair_slot = n % OWN_SLOTS, n % PAIR_SLOTS
+        for copy in self.sent.pop(n - OWN_SLOTS, []):
+            copy.wait_send()
+        mine = at.shard((j + 1) % self.ring)
+        other = mine + 1 - 2 * at.c
+        if n >= PAIR_SLOTS:
+            pl.semaphore_wait(self.credit, 1)
+        loads, pairs = [], []
+        for q in range(QUARTERS):
+            copy = pltpu.make_async_copy(self.piece(k, mine, q), self.own.at[slot, q], self.own_in.at[n, q])
+            copy.start()
+            loads.append(copy)
+            copy = remote(self.piece(k, other, q), self.pair.at[pair_slot, q], self.core_s.at[n, q], self.core_r.at[n, q], at.core)
+            copy.start()
+            pairs.append(copy)
+        self.loose += pairs
+        self.flights[n] = (loads, pairs)
+
+    def plane_first(self, n, slot, cols_a, cols_b, land_a, land_b, sems):
+        at, own = self.at, self.own
+        rows = slice(None)
+        (sa, ra), (sb, rb) = sems
+        return [
+            self.go(n, own.at[slot, at.qd, rows, cols_a], land_a.at[1], sa.at[1], ra.at[1], at.x),
+            self.go(n, own.at[slot, at.qd, rows, cols_b], land_b.at[1], sb.at[1], rb.at[1], at.y),
+            self.go(n, own.at[slot, at.qx, rows, cols_a], land_a.at[0], sa.at[0], ra.at[0], at.x),
+            self.go(n, own.at[slot, at.qy, rows, cols_b], land_b.at[0], sb.at[0], rb.at[0], at.y),
+        ]
+
+    def plane_second(self, n, slot, copies, cols_a, cols_b, land_a, land_b, next_a, next_b, sems):
+        at, own = self.at, self.own
+        rows = slice(None)
+        one_d, two_d, one, two = copies
+        (sa, ra), (sb, rb) = sems
+        one_d.wait_recv()
+        own[slot, at.qy, :, cols_a] = own[slot, at.qy, :, cols_a] + land_a[1]
+        on_a = self.go(n, own.at[slot, at.qy, rows, cols_a], next_a, sa, ra, at.y)
+        two_d.wait_recv()
+        own[slot, at.qx, :, cols_b] = own[slot, at.qx, :, cols_b] + land_b[1]
+        on_b = self.go(n, own.at[slot, at.qx, rows, cols_b], next_b, sb, rb, at.x)
+        one.wait_recv()
+        own[slot, at.q, :, cols_a] = own[slot, at.q, :, cols_a] + land_a[0]
+        two.wait_recv()
+        own[slot, at.q, :, cols_b] = own[slot, at.q, :, cols_b] + land_b[0]
+        return [on_a, on_b]
+
+    def plane_third(self, slot, copies, cols_a, cols_b, next_a, next_b):
+        at, own = self.at, self.own
+        for copy in copies:
+            copy.wait_recv()
+        own[slot, at.q, :, cols_a] = own[slot, at.q, :, cols_a] + next_a[...]
+        own[slot, at.q, :, cols_b] = own[slot, at.q, :, cols_b] + next_b[...]
+
+    def one(self, n):
+        at, own, pair = self.at, self.own, self.pair
+        k, j = divmod(n, self.ring)
+        slot, pair_slot = n % OWN_SLOTS, n % PAIR_SLOTS
+        loads, pairs = self.flights[n]
+        for q in range(QUARTERS):
+            loads[q].wait()
+            pairs[q].wait_recv()
+
+        @pl.loop(0, QUARTERS)
+        def _(q):
+            own[slot, q] = own[slot, q] + pair[pair_slot, q]
+
+        if n + PAIR_SLOTS < self.total:
+            pl.semaphore_signal(self.credit, inc=1, device_id=at.core, device_id_type=MESH)
+        a, b, c, d = self.cols
+        self.flights[n] = self.plane_first(
+            n, slot, a, b, self.first_a.at[n], self.first_b.at[n],
+            ((self.fa_s.at[n], self.fa_r.at[n]), (self.fb_s.at[n], self.fb_r.at[n])),
+        )
+        if j > 0:
+            self.flights[k, "c"].wait_recv()
+
+            @pl.loop(0, QUARTERS)
+            def _(q):
+                own[slot, q, :, self.cols_c] = own[slot, q, :, self.cols_c] + self.hops_c[k, j - 1, q]
+
+        rows = slice(None)
+        if j < self.ring - 1:
+            self.flights[k, "c"] = self.go(
+                n, own.at[slot, rows, rows, self.cols_c], self.hops_c.at[k, j], self.hopc_s.at[k, j], self.hopc_r.at[k, j], at.up
+            )
+        else:
+            self.flights[k, "flat"] = self.plane_first(
+                n, slot, c, d, self.flat_a.at[k], self.flat_b.at[k],
+                ((self.ca_s.at[k], self.ca_r.at[k]), (self.cb_s.at[k], self.cb_r.at[k])),
+            )
+
+    def two(self, n):
+        k, j = divmod(n, self.ring)
+        slot = n % OWN_SLOTS
+        a, b, c, d = self.cols
+        self.flights[n] = self.plane_second(
+            n, slot, self.flights[n], a, b, self.first_a.at[n], self.first_b.at[n], self.second_a.at[n], self.second_b.at[n],
+            ((self.sa_s.at[n], self.sa_r.at[n]), (self.sb_s.at[n], self.sb_r.at[n])),
+        )
+        if j == self.ring - 1:
+            self.flights[k, "flat"] = self.plane_second(
+                n, slot, self.flights[k, "flat"], c, d, self.flat_a.at[k], self.flat_b.at[k], self.last_a.at[k], self.last_b.at[k],
+                ((self.ca_s.at[k, 2], self.ca_r.at[k, 2]), (self.cb_s.at[k, 2], self.cb_r.at[k, 2])),
+            )
+
+    def three(self, n):
+        at, own = self.at, self.own
+        k, j = divmod(n, self.ring)
+        slot = n % OWN_SLOTS
+        a, b, c, d = self.cols
+        rows = slice(None)
+        self.plane_third(slot, self.flights[n], a, b, self.second_a.at[n], self.second_b.at[n])
+        if j > 0:
+            self.flights[k, "ab"].wait_recv()
+            own[slot, at.q, :, self.cols_ab] = own[slot, at.q, :, self.cols_ab] + self.hops[k, j - 1]
+        if j < self.ring - 1:
+            self.flights[k, "ab"] = self.go(
+                n, own.at[slot, at.q, rows, self.cols_ab], self.hops.at[k, j], self.hop_s.at[k, j], self.hop_r.at[k, j], at.up
+            )
+            return
+        self.plane_third(slot, self.flights[k, "flat"], c, d, self.last_a.at[k], self.last_b.at[k])
+        self.done[k, at.q] = own[slot, at.q]
+        mine = self.done.at[k, at.q]
+        self.flights[k, "end"] = [
+            self.keep(remote(mine, mine, self.end_s.at[k, 0], self.end_r.at[k, 0], at.x)),
+            self.keep(remote(mine, mine, self.end_s.at[k, 1], self.end_r.at[k, 1], at.y)),
+        ]
+
+    def keep(self, copy):
+        copy.start()
+        self.loose.append(copy)
+        return copy
+
+    def four(self, k):
+        at, done = self.at, self.done
+        (start_a, size_a), (start_b, size_b) = cut(self.width)
+        rows = slice(None)
+        by_x, by_y = self.flights[k, "end"]
+        by_x.wait_recv()
+        half = done.at[k, at.qx, rows, pl.ds(start_a, size_a)]
+        first = self.keep(remote(half, half, self.end_s.at[k, 2], self.end_r.at[k, 2], at.y))
+        by_y.wait_recv()
+        half = done.at[k, at.qy, rows, pl.ds(start_b, size_b)]
+        second = self.keep(remote(half, half, self.end_s.at[k, 3], self.end_r.at[k, 3], at.x))
+        self.flights[k, "end"] = [first, second]
+
+    def five(self, k):
+        for copy in self.flights[k, "end"]:
+            copy.wait_recv()
+        copy = pltpu.make_async_copy(self.done.at[k], self.outs[k], self.out_sem.at[k])
+        copy.start()
+        self.outgoing.append(copy)
+
+    def turn(self, t, first, last):
+        items = last - first
+        if t + 2 < items:
+            self.prefetch(first + t + 2)
+        if t < items:
+            self.one(first + t)
+        if 0 <= t - 1 < items:
+            self.two(first + t - 1)
+        if 0 <= t - 2 < items:
+            self.three(first + t - 2)
+        for lag, stage in ((3, self.four), (4, self.five)):
+            n = first + t - lag
+            if first <= n < last and n % self.ring == self.ring - 1:
+                stage(n // self.ring)
+
+    def finish(self):
+        for copy in self.outgoing:
+            copy.wait()
+        for copies in self.sent.values():
+            for copy in copies:
+                copy.wait_send()
+        for copy in self.loose:
+            copy.wait_send()
+
+
+def back_kernel(dp, fsdp, width, images, seq, heads, *refs):
+    ring = fsdp // 2
+    fc2_ref, fc1_ref, proj_ref, joint_ref, mixed_ref, h1_ref, tokens_ref, middle_ref, weight_ref = refs[:9]
+    lse_ref, gates_ref, vectors_ref, scales_ref, factor_ref, routers_ref, ada_ref, pre_ref, picker_ref = refs[9:18]
+    refs = refs[18:]
+    outs, refs = refs[:3], refs[3:]
+    all_gm_ref, all_pre_ref, grad_tokens_ref, triple_ref = refs[:4]
+    refs = refs[4:]
+    joint, mixed, h1, middle, grad_joint, stage, total, inner, gm_row, gms, parts, mine_in, pres = refs[:13]
+    in_sem, out_sem, mate_s, mate_r, cousin_s, cousin_r = refs[13:19]
+    at = Place(dp, fsdp)
+    at.greet()
+    rows = fc1_ref.shape[1]
+    count = images * seq
+    pad = pre_ref.shape[0]
+
+    def piece(k, index, q):
+        if k == 0:
+            return fc2_ref.at[index, q]
+        if k == 1:
+            return fc1_ref.at[index, :, pl.ds(q * width, width)]
+        line = pl.ds(pl.multiple_of(index * rows, 8), rows)
+        if q == 3:
+            return proj_ref.at[line, :]
+        return triple_ref.at[q, line, :]
+
+    work = Reducer(at, piece, outs, refs[19:], width)
+    moves, fetched = {}, []
+
+    def fetch(name, src, dst):
+        copy = pltpu.make_async_copy(src, dst, in_sem.at[len(fetched)])
+        copy.start()
+        fetched.append(copy)
+        moves.setdefault(name, []).append(copy)
+
+    def have(name):
+        for copy in moves.pop(name):
+            copy.wait()
+
+    def store(name, src, dst, i):
+        copy = pltpu.make_async_copy(src, dst, out_sem.at[i])
+        copy.start()
+        moves[name] = [copy]
+
+    work.prefetch(0)
+    work.prefetch(1)
+
+    def lines(image):
+        return pl.ds(image * seq, seq)
+
+    fetch("mixed", mixed_ref, mixed)
+    fetch("joint0", joint_ref.at[lines(0)], joint.at[0])
+    fetch("h1", h1_ref, h1)
+    inner[...] = jnp.zeros_like(inner)
+    gm_row[...] = jnp.zeros_like(gm_row)
+
+    def attention(image, half):
+        slot = image % 2
+        if half == 0:
+            if image == 0:
+                have("mixed")
+            have("joint" + str(image))
+            if image + 1 < images:
+                fetch("joint" + str(image + 1), joint_ref.at[lines(image + 1)], joint.at[1 - slot])
+        span = range(0, heads // 2) if half == 0 else range(heads // 2, heads)
+        attend_back_image(
+            joint.at[slot], mixed.at[lines(image)], gates_ref, lse_ref, grad_joint.at[lines(image)], inner, image, seq, heads, span
+        )
+
+    def weigh(q):
+        if q == 0:
+            have("h1")
+            fetch("tokens", tokens_ref, mixed)
+        slot = q % 2
+        if q >= 2:
+            have("out" + str(q - 2))
+
+        @pl.loop(0, width // 128)
+        def _(m):
+            line = pl.ds(pl.multiple_of(m * 128, 128), 128)
+            stage[slot, line, :] = times_rows(h1[:, line], grad_joint[:, pl.ds(q * width, width)]).astype(jnp.bfloat16)
+
+        store("out" + str(q), stage.at[slot], triple_ref.at[q], q)
+
+    def bring_weight(q):
+        for f in range(fsdp):
+            fetch("w" + str(q), weight_ref.at[f, :, pl.ds(q * width, width)], stage.at[q % 2, pl.ds(f * rows, rows), :])
+
+    def wait_terms():
+        for q in (1, 2):
+            have("out" + str(q))
+        bring_weight(0)
+        bring_weight(1)
+        fetch("middle0", middle_ref.at[lines(0)], middle.at[0])
+
+    def spread(q):
+        slot = q % 2
+        have("w" + str(q))
+
+        @pl.loop(0, images)
+        def _(image):
+            line = pl.ds(pl.multiple_of(image * seq, seq), seq)
+            value = times_back(grad_joint[line, pl.ds(q * width, width)], stage[slot])
+            if q == 0:
+                total[line, :] = value
+            else:
+                total[line, :] = total[line, :] + value
+
+        if q == 0:
+            bring_weight(2)
+
+    def norm(image):
+        slot = image % 2
+        if image == 0:
+            have("tokens")
+        have("middle" + str(image))
+        if image + 1 < images:
+            if image >= 1:
+                have("done" + str(image - 1))
+            fetch("middle" + str(image + 1), middle_ref.at[lines(image + 1)], middle.at[1 - slot])
+        scale = 1.0 + scales_ref[image : image + 1, :]
+        step = 32
+
+        def chunk(i, sums):
+            shift, gain = sums
+            line = pl.ds(pl.multiple_of(image * seq + i * step, step), step)
+            here = pl.ds(pl.multiple_of(i * step, step), step)
+            value = mixed[line, :].astype(jnp.float32)
+            grad = total[line, :]
+            centered = value - jnp.mean(value, axis=-1, keepdims=True)
+            inverse = lax.rsqrt(jnp.mean(centered * centered, axis=-1, keepdims=True) + EPSILON)
+            normed = centered * inverse
+            through = grad * scale
+            back = through - jnp.mean(through, axis=-1, keepdims=True)
+            back = back - normed * jnp.mean(through * normed, axis=-1, keepdims=True)
+            middle[slot, here, :] = middle[slot, here, :] + inverse * back
+            return (
+                shift + jnp.sum(grad, axis=0, keepdims=True),
+                gain + jnp.sum(grad * normed, axis=0, keepdims=True),
+            )
+
+        zero = jnp.zeros((1, width), jnp.float32)
+        shift, gain = lax.fori_loop(0, seq // step, chunk, (zero, zero))
+        store("done" + str(image), middle.at[slot], grad_tokens_ref.at[lines(image)], 3 + image)
+        gm_row[image : image + 1, :width] = shift
+        gm_row[image : image + 1, width : 2 * width] = gain
+
+    mates, cousins = at.mates(), at.cousins()
+    swaps = [Swap(mates, mate_s.at[i], mate_r.at[i]) for i in range(3)]
+    far = [Swap(cousins, cousin_s.at[i], cousin_r.at[i]) for i in range(2)]
+    small = []
+
+    def keep(src, dst):
+        copy = pltpu.make_async_copy(src, dst, out_sem.at[3 + images + len(small)])
+        copy.start()
+        small.append(copy)
+
+    held = gms.shape[3]
+
+    def tail_zero():
+        gm_row[:, 2 * width :] = vectors_ref[...]
+        for f in range(fsdp):
+            gms[0, f] = gm_row[:, f * held : (f + 1) * held].astype(jnp.bfloat16).astype(jnp.float32)
+        swaps[0].start(lambda device: gms.at[0, device[1]], gms.at[1, at.f])
+
+    def tail_one():
+        swaps[0].arrived()
+        gms[1, at.f] = gms[0, at.f]
+        every = gms[1].reshape(fsdp * pad, held).astype(jnp.bfloat16)
+        parts[...] = times_back(every, ada_ref[...]).reshape(parts.shape)
+        swaps[1].start(lambda device: parts.at[device[1]], mine_in.at[at.f])
+        far[0].start(lambda device: gms.at[1], all_gm_ref.at[at.d])
+        keep(gms.at[1], all_gm_ref.at[at.d])
+
+    def tail_two():
+        line = lax.broadcasted_iota(jnp.int32, (pad, 128), 0)
+        gated = jnp.zeros((pad, 128), jnp.float32)
+        for image in range(images):
+            summed = lax.dot_general(
+                jnp.ones((pad, seq), jnp.float32), inner[image], (((1,), (1,)), ((), ())),
+                preferred_element_type=jnp.float32, precision=lax.Precision.HIGHEST,
+            )
+            gated = jnp.where(line == image, summed, gated)
+        router = (gated * factor_ref[...]).astype(jnp.bfloat16)
+        swaps[1].arrived()
+        mine_in[at.f] = parts[at.f]
+        grad_cond = jnp.sum(mine_in[...], axis=0) + times_back(router, routers_ref[...])
+        pre_cond = pre_ref[...]
+        sig = jax.nn.sigmoid(pre_cond)
+        grad_pre = grad_cond * (sig * (1.0 + pre_cond * (1.0 - sig)))
+        grad_pre = grad_pre.astype(jnp.bfloat16).astype(jnp.float32)
+        pres[at.f, :, :width] = grad_pre + picker_ref[...]
+        pres[at.f, :, width:] = router.astype(jnp.float32)
+        swaps[2].start(lambda device: pres.at[at.f], pres.at[at.f])
+
+    def tail_three():
+        swaps[2].arrived()
+        far[1].start(lambda device: pres, all_pre_ref.at[at.d])
+        keep(pres, all_pre_ref.at[at.d])
+
+    early = [partial(attention, image, half) for image in range(images) for half in range(2)]
+    early += [partial(weigh, q) for q in range(3)] + [wait_terms]
+    late = [partial(spread, q) for q in range(3)] + [partial(norm, image) for image in range(images)]
+    late += [tail_zero, tail_one, tail_two, tail_three]
+    split = 2 * ring
+
+    def plan(turns, steps, turn):
+        done = 0
+        for t in range(turns):
+            turn(t)
+            upto = -(-len(steps) * (t + 1) // turns)
+            for step in steps[done:upto]:
+                step()
+            done = upto
+
+    plan(split + 4, early, lambda t: work.turn(t, 0, split))
+    work.prefetch(split)
+    work.prefetch(split + 1)
+    plan(ring + 4, late, lambda t: work.turn(t, split, split + ring))
+    for swap in far:
+        swap.arrived()
+    for copy in small:
+        copy.wait()
+    for image in range(max(images - 2, 0), images):
+        have("done" + str(image))
+    for swap in swaps + far:
+        swap.left()
+    work.finish()
+
+
+def back_half(
+    terms, joint, grad_mixed, flat_one, tokens, grad_middle, joint_full, log_total, gates, vectors, scales, factor,
+    routers, ada_weight, pre_cond, picker, width, images, seq, dp, fsdp,
+):
+    rows = terms[1].shape[1]
+    heads = gates.shape[1]
+    count = images * seq
+    pad = pre_cond.shape[0]
+    columns = ada_weight.shape[1]
+    dma, vmem = pltpu.SemaphoreType.DMA, pltpu.VMEM
+    low, f32 = jnp.bfloat16, jnp.float32
+    out = jax.ShapeDtypeStruct
+    any_space, in_vmem = pl.BlockSpec(memory_space=pl.ANY), pl.BlockSpec(memory_space=vmem)
+    in_smem = pl.BlockSpec(memory_space=pltpu.SMEM)
+    return pl.pallas_call(
+        partial(back_kernel, dp, fsdp, width, images, seq, heads),
+        out_shape=[out((QUARTERS, rows, width), low)] * 3
+        + [
+            out((dp, fsdp, pad, columns), f32),
+            out((dp, fsdp, pad, width + 128), f32),
+            out((count, width), f32),
+            out((3, width, width), low),
+        ],
+        in_specs=[any_space] * 9 + [in_vmem, in_smem] + [in_vmem] * 7,
+        out_specs=[any_space] * 7,
+        scratch_shapes=[
+            vmem((2, seq, 3 * width), low),
+            vmem((count, width), low),
+            vmem((count, width), low),
+            vmem((2, seq, width), f32),
+            vmem((count, 3 * width), low),
+            vmem((2, width, width), low),
+            vmem((count, width), f32),
+            vmem((images, 128, seq), f32),
+            vmem((pad, 6 * width), f32),
+            vmem((2, fsdp, pad, columns), f32),
+            vmem((fsdp, pad, width), f32),
+            vmem((fsdp, pad, width), f32),
+            vmem((fsdp, pad, width + 128), f32),
+            dma((3 * fsdp + 3 + 2 * images,)),
+            dma((5 + images,)),
+            dma((3, fsdp - 1)),
+            dma((3, fsdp - 1)),
+            dma((2, dp - 1)),
+            dma((2, dp - 1)),
+        ]
+        + Reducer.scratch(rows, width, fsdp),
+        compiler_params=pltpu.CompilerParams(
+            collective_id=1, has_side_effects=True, vmem_limit_bytes=60 * 2**20
+        ),
+        name="back",
+    )(
+        *terms, joint, grad_mixed, flat_one, tokens, grad_middle, joint_full, log_total, gates[:, None, :], vectors, scales,
+        factor, routers, ada_weight, pre_cond, picker,
+    )
 
 
 def body(
@@ -653,7 +958,7 @@
     routers = jnp.pad(
         jnp.concatenate([head_router, token_router], axis=1), ((0, 0), (0, 127 - heads))
     )
-    joint_full, fc1_full, fc2_full, pre_cond_pad, modulation, routers_full, all_cond, all_asked = gather_weights(
+    joint_blocks, fc1_full, fc2_full, pre_cond_pad, modulation, routers_full, all_cond, all_asked = gather_weights(
         [
             jnp.concatenate([qkv_weight, proj_weight], axis=1),
             fc1_weight,
@@ -668,7 +973,7 @@
         dp,
         fsdp,
     )
-    joint_full = joint_full.reshape(width, 4 * width)
+    joint_full = joint_blocks.reshape(width, 4 * width)
     triple, merger = joint_full[:, : 3 * width], joint_full[:, 3 * width :]
     expand = fc1_full.reshape(width, hidden)
     shrink = fc2_full.reshape(hidden, width)
@@ -726,48 +1031,35 @@
     grad_attn = (grad_middle * gate_one).astype(jnp.bfloat16).reshape(count, width)
     grad_merger = times_rows(mixed, grad_attn).astype(jnp.bfloat16)
     grad_mixed = times_back(grad_attn, merger).astype(jnp.bfloat16)
-    grad_joint, grad_gates = attend_back(joint, grad_mixed, head_gates, log_total, seq)
-    grad_router = (grad_gates * mask_float * router_sig * (1.0 - router_sig)).astype(jnp.bfloat16)
-    grad_triple = times_rows(flat_one, grad_joint).astype(jnp.bfloat16)
-    grad_h_one = times_back(grad_joint, triple).reshape(images, seq, width)
-    grad_shift_one = jnp.sum(grad_h_one, axis=1)
-    grad_scale_one = jnp.sum(grad_h_one * normed_one, axis=1)
-    grad_inputs = grad_middle + norm_back(inputs, grad_h_one * (1.0 + scale_one))
-    grad_modulation = jnp.concatenate(
+    vectors = jnp.concatenate([grad_gate_one, grad_shift_two, grad_scale_two, grad_gate_two], axis=1)
+    *sums, all_grad, all_pre, grad_inputs, _ = back_half(
         [
-            grad_shift_one,
-            grad_scale_one,
-            grad_gate_one,
-            grad_shift_two,
-            grad_scale_two,
-            grad_gate_two,
+            grad_shrink.reshape(fsdp, QUARTERS, rows, width),
+            grad_expand.reshape(fsdp, rows, hidden),
+            grad_merger,
         ],
-        axis=1,
-    ).astype(jnp.bfloat16)
-
-    last = jnp.concatenate(
-        [
-            jnp.pad(grad_picker, ((pad - 1, 0), (0, 0))),
-            padded(jnp.pad(grad_router.astype(jnp.float32), ((0, 0), (0, 128 - heads)))),
-        ],
-        axis=1,
-    )
-    *sums, all_grad, all_pre = reduce_terms(
-        [
-            jnp.concatenate([grad_triple, grad_merger], axis=1).reshape(fsdp, rows, 4 * width),
-            grad_expand.reshape(fsdp, rows, hidden),
-            grad_shrink.reshape(fsdp, QUARTERS, rows, width),
-        ],
-        padded(grad_modulation.astype(jnp.float32)).reshape(pad, fsdp, -1).transpose(1, 0, 2),
+        joint,
+        grad_mixed,
+        flat_one,
+        tokens.reshape(count, width),
+        grad_middle.reshape(count, width),
+        joint_blocks,
+        log_total,
+        head_gates,
+        padded(vectors),
+        padded(scale_one[:, 0]),
+        padded(jnp.pad(mask_float * router_sig * (1.0 - router_sig), ((0, 0), (0, 128 - heads)))),
+        routers_full,
         ada_weight,
-        padded(times_back(grad_router, chooser)),
         pre_cond_pad,
-        last,
-        rows,
+        jnp.pad(grad_picker, ((pad - 1, 0), (0, 0))),
         width,
+        images,
+        seq,
         dp,
         fsdp,
     )
+    grad_inputs = grad_inputs.reshape(images, seq, width)
     if dp > QUARTERS:
         parts = list(sums)
         for hop in range(QUARTERS, dp, QUARTERS):
@@ -778,10 +1070,10 @@
             ]
         sums = parts
     sums = [s.astype(jnp.float32) for s in sums]
-    sum_triple = jnp.concatenate([sums[0][0], sums[0][1], sums[0][2]], axis=1)
-    sum_merger = sums[0][3]
+    sum_triple = jnp.concatenate([sums[2][0], sums[2][1], sums[2][2]], axis=1)
+    sum_merger = sums[2][3]
     sum_expand = jnp.concatenate([sums[1][i] for i in range(QUARTERS)], axis=1)
-    sum_shrink = sums[2].reshape(QUARTERS * rows, width)
+    sum_shrink = sums[0].reshape(QUARTERS * rows, width)
 
     sum_ada = times_rows(all_cond, all_grad.reshape(everyone, -1).astype(jnp.bfloat16))
     sum_picker = lax.dynamic_slice_in_dim(

time: 626 us -> 576 us (0.920)
  Pallas kernels: 398 us -> 376 us
  matrix products: 148 us -> 127 us
  other arithmetic: 43.8 us -> 33.9 us
    pallas_call x2 -> x1, Pallas kernels: 241 us -> 220 us  [back_half(): pl.pallas_call(partial(back_kernel, dp, fsdp, width, images, seq, heads),...]
    dot_general x9 -> x8, matrix products: 45.8 us -> 32.6 us  [times_rows(): lax.dot_general(left, right, (((0,), (0,)), ((), ())), preferred_element_...]
    dot_general x5 -> x3, matrix products: 42.3 us -> 34.4 us  [times_back(): lax.dot_general(left, right, (((1,), (1,)), ((), ())), preferred_element_...]
    unnamed x134 -> x110, local copies, waits for them, and re-layouts: 20.1 us -> 21.2 us
where the time goes in v4:
time: 576 us; the launch traced here: 568 us
  Pallas kernels  376 us (65%)
  matrix products  127 us (22%)
  other arithmetic  33.9 us (6%)
  local copies, waits for them, and re-layouts  30.1 us (5%)
    pallas_call x1, Pallas kernels, back_half(): pl.pallas_call(partial(back_kernel, dp, fsdp, width, images, seq, heads),...  220 us
    pallas_call x1, Pallas kernels, gather_weights(): pl.pallas_call(partial(gather_kernel, dp, fsdp, width), out_shape=[out((f...  147 us
    dot_general x6, matrix products, matmul(): return jnp.dot(left, right, preferred_element_type=jnp.float32)  59.7 us
    dot_general x3, matrix products, times_back(): lax.dot_general(left, right, (((1,), (1,)), ((), ())), preferred_element_...  34.4 us
    dot_general x8, matrix products, times_rows(): lax.dot_general(left, right, (((0,), (0,)), ((), ())), preferred_element_...  32.6 us
    unnamed x110, local copies, waits for them, and re-layouts  21.2 us

profile of v4, /device:TPU:0, one launch (start us, length us, event | category | flops | bytes accessed | tf_op | source)
XLA Modules:
  0.0 568.0 jit_solution(3385927974103781861)
XLA Ops:
  2.8 1.8 convert_reduce_fusion
  4.6 2.1 fusion.18
  8.1 2.9 copy.45.refs_6_.refs_15_
  12.0 1.3 copy-done.3
  13.3 1.3 copy-done.4
  14.6 146.7 %gather.1 = (bf16[8,144,4608]{2,1,0:T(8,128)(2,1)S(1)}, bf16[8,144,4608]{2,1,0:T(8,128)(2,1)}, bf16[8,4,144,1152]{3,2,1,0:T(8,128)(2,1)}, f32[8,1152]{1,0:T(8,12...) custom-call(bf16[144,4608]{1,0:T(8,128)(2,1)S(1)} %pad_maximum_fusio, ...), custom_call_target="tpu_custom_call" | custom-call | tf_op jit(solution)/shard_map/gather/pallas_call | solution.py:276
  161.4 4.0 copy-done.1
  171.4 1.6 slice.80
  173.7 2.1 convert_element_type.120
  175.8 2.8 fusion.21
  179.8 12.2 %fusion.9.j.refs_3_ = bf16[768,3456]{1,0:T(8,128)(2,1)} fusion(bf16[768,1152]{1,0:T(8,128)(2,1)S(1)} %bitcast.110, bf16[1152,4608]{1,0:T(8,128)(2,1)} %bitcast.89), kind=kOutput, calls=%fused_computation.15 | convolution fusion | flops 6117949440 | bytes 15040512 | tf_op jit(solution)/shard_map/dot_general | solution.py:34
  192.0 9.5 %attend.1 = (bf16[768,1152]{1,0:T(8,128)(2,1)S(1)}, f32[3,16,256]{2,1,0:T(8,128)S(1)}) custom-call(bf16[768,3456]{1,0:T(8,128)(2,1)} %fusion.9.j.refs_3_, f32[3,1,16]{2,1,0:T(1,128)S(1)} %copy.47.g.refs_10_), custom_call_target="tpu_custom_call" | custom-call | tf_op jit(solution)/shard_map/attend/pallas_call | solution.py:369
  201.6 4.5 fusion.25
  212.6 1.9 fusion.16
  215.7 15.0 %fusion.64 = f32[768,4608]{1,0:T(8,128)} fusion(bf16[768,1152]{1,0:T(8,128)(2,1)S(1)} %bitcast.119, bf16[4608,1152]{1,0:T(8,128)(2,1)} %bitcast.126), kind=kOutput, calls=%fused_computation.131 | convolution fusion | flops 8153726976 | bytes 26542080 | tf_op jit(solution)/shard_map/dot_general | solution.py:44
  230.8 24.7 %fusion.6 = (bf16[768,4608]{1,0:T(8,128)(2,1)}, bf16[768,4608]{1,0:T(8,128)(2,1)}) fusion(f32[768,4608]{1,0:T(8,128)} %fusion.64, bf16[768,1152]{1,0:T(8,128)(2,1)S(1)} %bitcast.104, bf16[1152,4608]{1,0:T(8,128)(2,1)} %bitcast.124), kind=kOutput, calls=%fused_computation.10 | convolution fusion | flops 8231583744 | bytes 40697856 | tf_op jit(solution)/shard_map/dot_general | solution.py:34
  255.5 17.5 %fusion.23 = (f32[3,1152]{1,0:T(4,128)}, f32[3,256]{1,0:T(4,128)S(1)}, bf16[3,256,1152]{2,1,0:T(8,128)(2,1)}) fusion(bf16[3,256,1152]{2,1,0:T(8,128)(2,1)S(1)} %copy-done.19, f32[3,256]{1,0:T(4,128)S(1)} %convert_multiply_fusion.2, f32[3,1152]{1,0:T(4,128)S(1)} %copy-done.38, f32[3,256,1152]{2,1,0:T(8,128)} %copy-done.12, ...), kind=kOutput, calls=%fused_computation.36 | convolution fusion | flops 8163454976 | bytes 24806400 | tf_op jit(solution)/shard_map/dot_general | solution.py:34
  274.2 13.6 %convolution_add_fusion = f32[768,1152]{1,0:T(8,128)S(1)} fusion(bf16[768,4608]{1,0:T(8,128)(2,1)} %get-tuple-element.53, bf16[1152,4608]{1,0:T(8,128)(2,1)} %bitcast.125, f32[1152]{0:T(1024)} %convert.20, f32[768]{0:T(1024)S(1)} %reshape.193), kind=kOutput, calls=%fused_computation.27 | convolution fusion | flops 8155496448 | bytes 21241344 | tf_op jit(solution)/shard_map/dot_general | solution.py:44
  289.7 1.5 multiply_reduce_fusion
  292.2 3.6 multiply_reduce_fusion.1
  297.9 4.0 convolution_convert_fusion.2.refs_2_
  301.9 5.7 %convolution_convert_fusion.3.refs_4_ = bf16[768,1152]{1,0:T(8,128)(2,1)} fusion(bf16[768,1152]{1,0:T(8,128)(2,1)S(1)} %bitcast.118, bf16[1152,4608]{1,0:T(8,128)(2,1)} %bitcast.91), kind=kOutput, calls=%fused_computation.44 | convolution fusion | flops 2039316480 | bytes 6193152 | tf_op jit(solution)/shard_map/dot_general | solution.py:44
  307.7 10.7 %convolution_convert_fusion = bf16[1152,4608]{1,0:T(8,128)(2,1)} fusion(bf16[768,1152]{1,0:T(8,128)(2,1)S(1)} %bitcast.105, bf16[768,4608]{1,0:T(8,128)(2,1)S(1)} %bitcast.132), kind=kOutput, calls=%fused_computation.2 | convolution fusion | flops 8159035392 | bytes 19464192 | tf_op jit(solution)/shard_map/dot_general | solution.py:38
  318.4 11.7 %convolution_convert_fusion.1 = bf16[4608,1152]{1,0:T(8,128)(2,1)} fusion(bf16[768,4608]{1,0:T(8,128)(2,1)S(1)} %bitcast.130, bf16[768,1152]{1,0:T(8,128)(2,1)S(1)} %bitcast.120), kind=kOutput, calls=%fused_computation.3 | convolution fusion | flops 8159035392 | bytes 19464192 | tf_op jit(solution)/shard_map/dot_general | solution.py:38
  330.2 219.5 %back.1 = (bf16[4,144,1152]{2,1,0:T(8,128)(2,1)}, bf16[4,144,1152]{2,1,0:T(8,128)(2,1)}, bf16[4,144,1152]{2,1,0:T(8,128)(2,1)}, f32[4,8,8,864]{3,2,1,0:T(8,128)}...) custom-call(bf16[8,4,144,1152]{3,2,1,0:T(8,128)(2,1)} %bitcast.109, ...), custom_call_target="tpu_custom_call" | custom-call | tf_op jit(solution)/shard_map/back/pallas_call | solution.py:876
  549.7 1.5 slice_reduce_fusion.1
  551.3 1.5 select_convert_fusion
  557.7 1.4 pad_maximum_fusion.1
  559.5 1.8 pad_maximum_fusion
  561.3 1.8 bitcast_convert_fusion
  563.1 2.7 convolution_bitcast_fusion
  565.8 1.8 copy.57
  (161 shorter events, 31.4 us)
Async XLA Ops:
  0.6 6.1 %copy-start.46 = (bf16[144,1]{0,1:T(2,128)(2,1)S(1)}, bf16[144,1]{0,1:T(2,128)(2,1)}, u32[]{:S(2)}) copy-start(bf16[144,1]{0,1:T(2,128)(2,1)} %param.29) | copy-start | bytes 868
  0.7 7.3 %copy-start.33 = (bf16[144,1152]{1,0:T(8,128)(2,1)S(1)}, bf16[144,1152]{1,0:T(8,128)(2,1)}, u32[]{:S(2)}) copy-start(bf16[144,1152]{1,0:T(8,128)(2,1)} %param.26) | copy-start | bytes 995332
  0.7 7.3 %copy-start.29 = (bf16[144,3456]{1,0:T(8,128)(2,1)S(1)}, bf16[144,3456]{1,0:T(8,128)(2,1)}, u32[]{:S(2)}) copy-start(bf16[144,3456]{1,0:T(8,128)(2,1)} %param.25) | copy-start | bytes 2985988
  0.7 6.1 %copy-start.44 = (bf16[144,16]{0,1:T(8,128)(2,1)S(1)}, bf16[144,16]{0,1:T(8,128)(2,1)}, u32[]{:S(2)}) copy-start(bf16[144,16]{0,1:T(8,128)(2,1)} %param.24) | copy-start | bytes 13828
  0.7 6.3 %copy-start.34 = (bf16[1000,144]{0,1:T(8,128)(2,1)S(1)}, bf16[1000,144]{0,1:T(8,128)(2,1)}, u32[]{:S(2)}) copy-start(bf16[1000,144]{0,1:T(8,128)(2,1)} %param.22) | copy-start | bytes 864004
  14.6 151.8 %copy-start = (bf16[1152,864]{1,0:T(8,128)(2,1)}, bf16[1152,864]{1,0:T(8,128)(2,1)S(1)}, u32[]{:S(2)}) copy-start(bf16[1152,864]{1,0:T(8,128)(2,1)S(1)} %copy.45.refs_6_.refs_15_) | copy-start | bytes 5971972
  14.6 152.5 %copy-start.48 = (s32[3,16]{1,0:T(4,128)S(1)}, s32[3,16]{1,0:T(4,128)}, u32[]{:S(2)}) copy-start(s32[3,16]{1,0:T(4,128)} %param.18) | copy-start | bytes 580
  161.3 4.1 copy-start.1
  167.3 24.7 %copy-start.11 = (f32[3,1,16]{2,1,0:T(1,128)}, f32[3,1,16]{2,1,0:T(1,128)S(1)}, u32[]{:S(2)}) copy-start(f32[3,1,16]{2,1,0:T(1,128)S(1)} %copy.47.g.refs_10_) | copy-start | bytes 580
  169.9 36.3 %copy-start.36 = (f32[3,1152]{1,0:T(4,128)}, f32[3,1152]{1,0:T(4,128)S(1)}, u32[]{:S(2)}) copy-start(f32[3,1152]{1,0:T(4,128)S(1)} %get-tuple-element.70) | copy-start | bytes 41476
  201.6 4.6 copy-start.9
  201.6 4.6 copy-start.14
  230.8 24.7 %copy-start.19 = (bf16[3,256,1152]{2,1,0:T(8,128)(2,1)S(1)}, bf16[3,256,1152]{2,1,0:T(8,128)(2,1)}, u32[]{:S(2)}) copy-start(bf16[3,256,1152]{2,1,0:T(8,128)(2,1)} %param.20) | copy-start | bytes 5308420
  230.8 24.7 %copy-start.38 = (f32[3,1152]{1,0:T(4,128)S(1)}, f32[3,1152]{1,0:T(4,128)}, u32[]{:S(2)}) copy-start(f32[3,1152]{1,0:T(4,128)} %get-tuple-element.67) | copy-start | bytes 41476
  255.5 17.5 %copy-start.43 = (s32[3,256]{1,0:T(4,128)S(1)}, s32[3,256]{1,0:T(4,128)}, u32[]{:S(2)}) copy-start(s32[3,256]{1,0:T(4,128)} %param.19) | copy-start | bytes 9220
  274.2 13.7 %copy-start.40 = (bf16[3,256]{1,0:T(4,128)(2,1)S(1)}, bf16[3,256]{1,0:T(4,128)(2,1)}, u32[]{:S(2)}) copy-start(bf16[3,256]{1,0:T(4,128)(2,1)} %multiply_convert_fusion.2) | copy-start | bytes 4612
  274.2 14.0 %copy-start.13 = (f32[3,256,1152]{2,1,0:T(8,128)S(1)}, f32[3,256,1152]{2,1,0:T(8,128)}, u32[]{:S(2)}) copy-start(f32[3,256,1152]{2,1,0:T(8,128)} %copy-done.12) | copy-start | bytes 10616836
  274.2 14.0 %copy-start.32 = (f32[3,1152]{1,0:T(4,128)S(1)}, f32[3,1152]{1,0:T(4,128)}, u32[]{:S(2)}) copy-start(f32[3,1152]{1,0:T(4,128)} %get-tuple-element.66) | copy-start | bytes 41476
  292.2 4.3 copy-start.41
  292.2 5.4 copy-start.37
  295.8 6.1 %copy-start.15 = (f32[3,256,1152]{2,1,0:T(8,128)}, f32[3,256,1152]{2,1,0:T(8,128)S(1)}, u32[]{:S(2)}) copy-start(f32[3,256,1152]{2,1,0:T(8,128)S(1)} %get-tuple-element.50) | copy-start | bytes 10616836
  297.9 9.8 %slice-start.2 = ((s8[7077888]{0:T(1024)(128)(4,1)}), s8[4194304]{0:T(1024)(128)(4,1)S(1)}, s32[]{:S(2)}) async-start(s8[7077888]{0:T(1024)(128)(4,1)} %bitcast.131), calls=%async_computation.2 | async-start | bytes 8388608
  301.9 5.7 %slice-start.3 = ((s8[7077888]{0:T(1024)(128)(4,1)}), s8[2883584]{0:T(1024)(128)(4,1)S(1)}, s32[]{:S(2)}) async-start(s8[7077888]{0:T(1024)(128)(4,1)} %bitcast.131), calls=%async_computation.3 | async-start | bytes 5767168
  301.9 16.5 %slice-start = ((s8[7077888]{0:T(1024)(128)(4,1)}), s8[4194304]{0:T(1024)(128)(4,1)S(1)}, s32[]{:S(2)}) async-start(s8[7077888]{0:T(1024)(128)(4,1)} %bitcast.129), calls=%async_computation | async-start | bytes 8388608
  307.6 10.7 %copy-start.25 = (bf16[3,256,1152]{2,1,0:T(8,128)(2,1)S(1)}, bf16[3,256,1152]{2,1,0:T(8,128)(2,1)}, u32[]{:S(2)}) copy-start(bf16[3,256,1152]{2,1,0:T(8,128)(2,1)} %copy-done.24) | copy-start | bytes 5308420
  307.7 10.7 %slice-start.1 = ((s8[7077888]{0:T(1024)(128)(4,1)}), s8[2883584]{0:T(1024)(128)(4,1)S(1)}, s32[]{:S(2)}) async-start(s8[7077888]{0:T(1024)(128)(4,1)} %bitcast.129), calls=%async_computation.1 | async-start | bytes 5767168
  330.2 221.1 %copy-start.47 = (pred[8]{0:T(512)(128)(4,1)S(1)}, pred[8]{0:T(512)(128)(4,1)}, u32[]{:S(2)}) copy-start(pred[8]{0:T(512)(128)(4,1)} %iota_compare_fusion.4) | copy-start | bytes 28
  330.2 223.2 %copy-start.35 = (bf16[256,256]{1,0:T(8,128)(2,1)S(1)}, bf16[256,256]{1,0:T(8,128)(2,1)}, u32[]{:S(2)}) copy-start(bf16[256,256]{1,0:T(8,128)(2,1)} %slice.80) | copy-start | bytes 393220
  330.2 224.2 %copy-start.23 = (bf16[4,8,8,1152]{3,2,1,0:T(8,128)(2,1)S(1)}, bf16[4,8,8,1152]{3,2,1,0:T(8,128)(2,1)}, u32[]{:S(2)}) copy-start(bf16[4,8,8,1152]{3,2,1,0:T(8,128)(2,1)} %convert_element_type.120) | copy-start | bytes 1769476
  549.7 5.6 copy-start.45
  549.7 6.8 %copy-start.28 = (bf16[4,144,1152]{2,1,0:T(8,128)(2,1)S(1)}, bf16[4,144,1152]{2,1,0:T(8,128)(2,1)}, u32[]{:S(2)}) copy-start(bf16[4,144,1152]{2,1,0:T(8,128)(2,1)} %get-tuple-element.40) | copy-start | bytes 3981316
  559.5 3.6 copy-start.30
  (21 other events, 32.8 us)

commit v5 on v4

--- a/solution.py
+++ b/solution.py
@@ -11,6 +11,7 @@
 EPSILON = 1e-06
 MESH = pl.DeviceIdType.MESH
 QUARTERS = 4
+DIGIT = 256
 
 
 def sinusoid(steps, entries):
@@ -171,14 +172,14 @@
     def cond_one():
         swaps[0].arrived()
         asks[at.f] = ask_ref[...]
-        every = asks[...].reshape(group, asks.shape[2])
+        every = asks[...].astype(jnp.float32).reshape(group, asks.shape[2])
         entries = every.shape[1] - 128
         own_rows = time_ref.shape[0]
         lanes = lax.broadcasted_iota(jnp.int32, (group, entries), 1)
         held = (lanes >= at.f * own_rows) & (lanes < (at.f + 1) * own_rows)
         embedded = jnp.where(held, every[:, :entries], 0.0).astype(jnp.bfloat16)
         stacked = jnp.concatenate([time_ref[...]] * fsdp, axis=0)
-        label = every[:, entries : entries + 1].astype(jnp.int32)
+        label = (every[:, entries : entries + 1] * DIGIT + every[:, entries + 1 : entries + 2]).astype(jnp.int32)
         classes = table_ref.shape[0]
         picks = (label == lax.broadcasted_iota(jnp.int32, (group, classes), 1)).astype(jnp.float32)
         picked = matmul(picks.astype(jnp.bfloat16), table_ref[...]).astype(jnp.bfloat16)
@@ -196,12 +197,12 @@
         mine_in[at.f] = parts[at.f]
         pre_cond = jnp.sum(mine_in[...], axis=0)
         pre_ref[...] = pre_cond
-        conds[at.f] = (pre_cond * jax.nn.sigmoid(pre_cond)).astype(jnp.bfloat16).astype(jnp.float32)
+        conds[at.f] = (pre_cond * jax.nn.sigmoid(pre_cond)).astype(jnp.bfloat16)
         swaps[2].start(lambda device: conds.at[at.f], conds.at[at.f])
 
     def cond_three():
         swaps[2].arrived()
-        every = conds[...].reshape(group, width).astype(jnp.bfloat16)
+        every = conds[...].astype(jnp.float32).reshape(group, width).astype(jnp.bfloat16)
         columns[...] = matmul(every, ada_ref[...]).reshape(columns.shape)
         swaps[3].start(lambda device: columns.at[device[1]], mod_ref.at[at.f])
         far[0].start(lambda device: conds, all_cond_ref.at[at.d])
@@ -280,16 +281,16 @@
             out((pad, width), f32),
             out((fsdp, pad, columns), f32),
             out((fsdp, *routers.shape), routers.dtype),
-            out((dp, fsdp, pad, width), f32),
-            out((dp, fsdp, pad, asking), f32),
+            out((dp, fsdp, pad, width), jnp.bfloat16),
+            out((dp, fsdp, pad, asking), jnp.bfloat16),
         ],
         in_specs=[any_space] * 3 + [in_vmem] * 5,
         out_specs=[any_space] * 3 + [in_vmem] + [any_space] * 4,
         scratch_shapes=[
-            vmem((fsdp, pad, asking), f32),
+            vmem((fsdp, pad, asking), jnp.bfloat16),
             vmem((fsdp, pad, width), f32),
             vmem((fsdp, pad, width), f32),
-            vmem((fsdp, pad, width), f32),
+            vmem((fsdp, pad, width), jnp.bfloat16),
             vmem((fsdp, pad, columns), f32),
         ]
         + [dma((3,)), dma((3, ring)), dma((3, ring))]
@@ -386,12 +387,14 @@
     return [(128 * s, 128 * n) for s, n in zip(starts, sizes)]
 
 
-OWN_SLOTS = 5
-PAIR_SLOTS = 3
+OWN_SLOTS = 8
+PAIR_SLOTS = 4
+AHEAD = 3
+LAG = 2
 
 
 class Reducer:
-    def __init__(self, at, piece, outs, scratch, width):
+    def __init__(self, at, piece, outs, scratch, rows, width):
         self.at, self.piece, self.outs, self.width = at, piece, outs, width
         (
             self.own, self.pair, self.first_a, self.first_b, self.second_a, self.second_b,
@@ -401,7 +404,8 @@
             self.ca_s, self.ca_r, self.cb_s, self.cb_r, self.end_s, self.end_r, self.out_sem, self.credit,
         ) = scratch
         self.ring = at.ring
-        self.total = 3 * self.ring
+        self.total = 3 * self.ring * 2
+        self.spans = self.halves(rows)
         self.sent, self.flights = {}, {}
         self.loose, self.outgoing = [], []
         self.cols = [pl.ds(*part) for part in thirds(width)]
@@ -410,9 +414,20 @@
         self.cols_c = pl.ds(a + b, width - a - b)
 
     @staticmethod
+    def halves(rows):
+        top = -(-rows // 32) * 16
+        return (0, top), (top, rows - top)
+
+    def place(self, n):
+        half = n % 2
+        k, j = divmod(n // 2, self.ring)
+        return k, j, half, self.spans[half][1]
+
+    @staticmethod
     def scratch(rows, width, fsdp):
         ring = fsdp // 2
-        total = 3 * ring
+        total = 3 * ring * 2
+        full, rows = rows, Reducer.halves(rows)[0][1]
         low, vmem, dma = jnp.bfloat16, pltpu.VMEM, pltpu.SemaphoreType.DMA
         a, b, c, d = [size for _, size in thirds(width)]
         arrays = [
@@ -422,22 +437,22 @@
             vmem((total, 2, rows, b), low),
             vmem((total, rows, a), low),
             vmem((total, rows, b), low),
-            vmem((3, ring - 1, rows, a + b), low),
-            vmem((3, ring - 1, QUARTERS, rows, c + d), low),
+            vmem((3, 2, ring - 1, rows, a + b), low),
+            vmem((3, 2, ring - 1, QUARTERS, rows, c + d), low),
+            vmem((3, 2, 2, rows, c), low),
+            vmem((3, 2, 2, rows, d), low),
             vmem((3, 2, rows, c), low),
             vmem((3, 2, rows, d), low),
-            vmem((3, rows, c), low),
-            vmem((3, rows, d), low),
-            vmem((3, QUARTERS, rows, width), low),
+            vmem((3, QUARTERS, full, width), low),
         ]
         sems = (
             [dma((total, QUARTERS))] * 3
             + [dma((total, 2))] * 4
             + [dma((total,))] * 4
-            + [dma((3, ring - 1))] * 4
-            + [dma((3, 3))] * 4
-            + [dma((3, 4))] * 2
-            + [dma((3,))]
+            + [dma((3, 2, ring - 1))] * 4
+            + [dma((3, 2, 3))] * 4
+            + [dma((3, 2, 4))] * 2
+            + [dma((3, 2))]
             + [pltpu.SemaphoreType.REGULAR]
         )
         return arrays + sems
@@ -450,7 +465,7 @@
 
     def prefetch(self, n):
         at = self.at
-        k, j = divmod(n, self.ring)
+        k, j, half, size = self.place(n)
         slot, pair_slot = n % OWN_SLOTS, n % PAIR_SLOTS
         for copy in self.sent.pop(n - OWN_SLOTS, []):
             copy.wait_send()
@@ -458,125 +473,130 @@
         other = mine + 1 - 2 * at.c
         if n >= PAIR_SLOTS:
             pl.semaphore_wait(self.credit, 1)
-        loads, pairs = [], []
+        brought, pairs = [], []
+        span, here = pl.ds(*self.spans[half]), pl.ds(0, size)
         for q in range(QUARTERS):
-            copy = pltpu.make_async_copy(self.piece(k, mine, q), self.own.at[slot, q], self.own_in.at[n, q])
+            copy = pltpu.make_async_copy(self.piece(k, mine, q, span), self.own.at[slot, q, here], self.own_in.at[n, q])
             copy.start()
-            loads.append(copy)
-            copy = remote(self.piece(k, other, q), self.pair.at[pair_slot, q], self.core_s.at[n, q], self.core_r.at[n, q], at.core)
+            brought.append(copy)
+            copy = remote(
+                self.piece(k, other, q, span), self.pair.at[pair_slot, q, here], self.core_s.at[n, q], self.core_r.at[n, q], at.core
+            )
             copy.start()
             pairs.append(copy)
         self.loose += pairs
-        self.flights[n] = (loads, pairs)
-
-    def plane_first(self, n, slot, cols_a, cols_b, land_a, land_b, sems):
+        self.flights[n] = (brought, pairs)
+
+    def plane_first(self, n, slot, here, cols_a, cols_b, land_a, land_b, sems):
         at, own = self.at, self.own
-        rows = slice(None)
         (sa, ra), (sb, rb) = sems
         return [
-            self.go(n, own.at[slot, at.qd, rows, cols_a], land_a.at[1], sa.at[1], ra.at[1], at.x),
-            self.go(n, own.at[slot, at.qd, rows, cols_b], land_b.at[1], sb.at[1], rb.at[1], at.y),
-            self.go(n, own.at[slot, at.qx, rows, cols_a], land_a.at[0], sa.at[0], ra.at[0], at.x),
-            self.go(n, own.at[slot, at.qy, rows, cols_b], land_b.at[0], sb.at[0], rb.at[0], at.y),
+            self.go(n, own.at[slot, at.qd, here, cols_a], land_a.at[1, here], sa.at[1], ra.at[1], at.x),
+            self.go(n, own.at[slot, at.qd, here, cols_b], land_b.at[1, here], sb.at[1], rb.at[1], at.y),
+            self.go(n, own.at[slot, at.qx, here, cols_a], land_a.at[0, here], sa.at[0], ra.at[0], at.x),
+            self.go(n, own.at[slot, at.qy, here, cols_b], land_b.at[0, here], sb.at[0], rb.at[0], at.y),
         ]
 
-    def plane_second(self, n, slot, copies, cols_a, cols_b, land_a, land_b, next_a, next_b, sems):
+    def plane_second(self, n, slot, here, copies, cols_a, cols_b, land_a, land_b, next_a, next_b, sems):
         at, own = self.at, self.own
-        rows = slice(None)
         one_d, two_d, one, two = copies
         (sa, ra), (sb, rb) = sems
         one_d.wait_recv()
-        own[slot, at.qy, :, cols_a] = own[slot, at.qy, :, cols_a] + land_a[1]
-        on_a = self.go(n, own.at[slot, at.qy, rows, cols_a], next_a, sa, ra, at.y)
+        own[slot, at.qy, here, cols_a] = own[slot, at.qy, here, cols_a] + land_a[1, here]
+        on_a = self.go(n, own.at[slot, at.qy, here, cols_a], next_a.at[here], sa, ra, at.y)
         two_d.wait_recv()
-        own[slot, at.qx, :, cols_b] = own[slot, at.qx, :, cols_b] + land_b[1]
-        on_b = self.go(n, own.at[slot, at.qx, rows, cols_b], next_b, sb, rb, at.x)
+        own[slot, at.qx, here, cols_b] = own[slot, at.qx, here, cols_b] + land_b[1, here]
+        on_b = self.go(n, own.at[slot, at.qx, here, cols_b], next_b.at[here], sb, rb, at.x)
         one.wait_recv()
-        own[slot, at.q, :, cols_a] = own[slot, at.q, :, cols_a] + land_a[0]
+        own[slot, at.q, here, cols_a] = own[slot, at.q, here, cols_a] + land_a[0, here]
         two.wait_recv()
-        own[slot, at.q, :, cols_b] = own[slot, at.q, :, cols_b] + land_b[0]
+        own[slot, at.q, here, cols_b] = own[slot, at.q, here, cols_b] + land_b[0, here]
         return [on_a, on_b]
 
-    def plane_third(self, slot, copies, cols_a, cols_b, next_a, next_b):
+    def plane_third(self, slot, here, copies, cols_a, cols_b, next_a, next_b):
         at, own = self.at, self.own
         for copy in copies:
             copy.wait_recv()
-        own[slot, at.q, :, cols_a] = own[slot, at.q, :, cols_a] + next_a[...]
-        own[slot, at.q, :, cols_b] = own[slot, at.q, :, cols_b] + next_b[...]
+        own[slot, at.q, here, cols_a] = own[slot, at.q, here, cols_a] + next_a[here, :]
+        own[slot, at.q, here, cols_b] = own[slot, at.q, here, cols_b] + next_b[here, :]
 
     def one(self, n):
         at, own, pair = self.at, self.own, self.pair
-        k, j = divmod(n, self.ring)
+        k, j, half, size = self.place(n)
         slot, pair_slot = n % OWN_SLOTS, n % PAIR_SLOTS
-        loads, pairs = self.flights[n]
+        here = pl.ds(0, size)
+        brought, pairs = self.flights[n]
         for q in range(QUARTERS):
-            loads[q].wait()
+            brought[q].wait()
             pairs[q].wait_recv()
 
         @pl.loop(0, QUARTERS)
         def _(q):
-            own[slot, q] = own[slot, q] + pair[pair_slot, q]
+            own[slot, q, here, :] = own[slot, q, here, :] + pair[pair_slot, q, here, :]
 
         if n + PAIR_SLOTS < self.total:
             pl.semaphore_signal(self.credit, inc=1, device_id=at.core, device_id_type=MESH)
         a, b, c, d = self.cols
         self.flights[n] = self.plane_first(
-            n, slot, a, b, self.first_a.at[n], self.first_b.at[n],
+            n, slot, here, a, b, self.first_a.at[n], self.first_b.at[n],
             ((self.fa_s.at[n], self.fa_r.at[n]), (self.fb_s.at[n], self.fb_r.at[n])),
         )
         if j > 0:
-            self.flights[k, "c"].wait_recv()
+            self.flights[k, half, "c"].wait_recv()
 
             @pl.loop(0, QUARTERS)
             def _(q):
-                own[slot, q, :, self.cols_c] = own[slot, q, :, self.cols_c] + self.hops_c[k, j - 1, q]
-
-        rows = slice(None)
+                own[slot, q, here, self.cols_c] = own[slot, q, here, self.cols_c] + self.hops_c[k, half, j - 1, q, here, :]
+
         if j < self.ring - 1:
-            self.flights[k, "c"] = self.go(
-                n, own.at[slot, rows, rows, self.cols_c], self.hops_c.at[k, j], self.hopc_s.at[k, j], self.hopc_r.at[k, j], at.up
+            self.flights[k, half, "c"] = self.go(
+                n, own.at[slot, slice(None), here, self.cols_c], self.hops_c.at[k, half, j, slice(None), here],
+                self.hopc_s.at[k, half, j], self.hopc_r.at[k, half, j], at.up,
             )
         else:
-            self.flights[k, "flat"] = self.plane_first(
-                n, slot, c, d, self.flat_a.at[k], self.flat_b.at[k],
-                ((self.ca_s.at[k], self.ca_r.at[k]), (self.cb_s.at[k], self.cb_r.at[k])),
+            self.flights[k, half, "flat"] = self.plane_first(
+                n, slot, here, c, d, self.flat_a.at[k, half], self.flat_b.at[k, half],
+                ((self.ca_s.at[k, half], self.ca_r.at[k, half]), (self.cb_s.at[k, half], self.cb_r.at[k, half])),
             )
 
     def two(self, n):
-        k, j = divmod(n, self.ring)
-        slot = n % OWN_SLOTS
+        k, j, half, size = self.place(n)
+        slot, here = n % OWN_SLOTS, pl.ds(0, size)
         a, b, c, d = self.cols
         self.flights[n] = self.plane_second(
-            n, slot, self.flights[n], a, b, self.first_a.at[n], self.first_b.at[n], self.second_a.at[n], self.second_b.at[n],
+            n, slot, here, self.flights[n], a, b, self.first_a.at[n], self.first_b.at[n], self.second_a.at[n], self.second_b.at[n],
             ((self.sa_s.at[n], self.sa_r.at[n]), (self.sb_s.at[n], self.sb_r.at[n])),
         )
         if j == self.ring - 1:
-            self.flights[k, "flat"] = self.plane_second(
-                n, slot, self.flights[k, "flat"], c, d, self.flat_a.at[k], self.flat_b.at[k], self.last_a.at[k], self.last_b.at[k],
-                ((self.ca_s.at[k, 2], self.ca_r.at[k, 2]), (self.cb_s.at[k, 2], self.cb_r.at[k, 2])),
+            self.flights[k, half, "flat"] = self.plane_second(
+                n, slot, here, self.flights[k, half, "flat"], c, d, self.flat_a.at[k, half], self.flat_b.at[k, half],
+                self.last_a.at[k, half], self.last_b.at[k, half],
+                ((self.ca_s.at[k, half, 2], self.ca_r.at[k, half, 2]), (self.cb_s.at[k, half, 2], self.cb_r.at[k, half, 2])),
             )
 
     def three(self, n):
         at, own = self.at, self.own
-        k, j = divmod(n, self.ring)
-        slot = n % OWN_SLOTS
+        k, j, half, size = self.place(n)
+        slot, here = n % OWN_SLOTS, pl.ds(0, size)
         a, b, c, d = self.cols
-        rows = slice(None)
-        self.plane_third(slot, self.flights[n], a, b, self.second_a.at[n], self.second_b.at[n])
+        self.plane_third(slot, here, self.flights[n], a, b, self.second_a.at[n], self.second_b.at[n])
         if j > 0:
-            self.flights[k, "ab"].wait_recv()
-            own[slot, at.q, :, self.cols_ab] = own[slot, at.q, :, self.cols_ab] + self.hops[k, j - 1]
+            self.flights[k, half, "ab"].wait_recv()
+            own[slot, at.q, here, self.cols_ab] = own[slot, at.q, here, self.cols_ab] + self.hops[k, half, j - 1, here, :]
         if j < self.ring - 1:
-            self.flights[k, "ab"] = self.go(
-                n, own.at[slot, at.q, rows, self.cols_ab], self.hops.at[k, j], self.hop_s.at[k, j], self.hop_r.at[k, j], at.up
+            self.flights[k, half, "ab"] = self.go(
+                n, own.at[slot, at.q, here, self.cols_ab], self.hops.at[k, half, j, here],
+                self.hop_s.at[k, half, j], self.hop_r.at[k, half, j], at.up,
             )
             return
-        self.plane_third(slot, self.flights[k, "flat"], c, d, self.last_a.at[k], self.last_b.at[k])
-        self.done[k, at.q] = own[slot, at.q]
-        mine = self.done.at[k, at.q]
-        self.flights[k, "end"] = [
-            self.keep(remote(mine, mine, self.end_s.at[k, 0], self.end_r.at[k, 0], at.x)),
-            self.keep(remote(mine, mine, self.end_s.at[k, 1], self.end_r.at[k, 1], at.y)),
+        self.plane_third(slot, here, self.flights[k, half, "flat"], c, d, self.last_a.at[k, half], self.last_b.at[k, half])
+        span = pl.ds(*self.spans[half])
+        self.done[k, at.q, span, :] = own[slot, at.q, here, :]
+        mine = self.done.at[k, at.q, span]
+        sems = self.end_s.at[k, half], self.end_r.at[k, half]
+        self.flights[k, half, "end"] = [
+            self.keep(remote(mine, mine, sems[0].at[0], sems[1].at[0], at.x)),
+            self.keep(remote(mine, mine, sems[0].at[1], sems[1].at[1], at.y)),
         ]
 
     def keep(self, copy):
@@ -584,40 +604,38 @@
         self.loose.append(copy)
         return copy
 
-    def four(self, k):
+    def four(self, n):
         at, done = self.at, self.done
+        k, _, half, _ = self.place(n)
         (start_a, size_a), (start_b, size_b) = cut(self.width)
-        rows = slice(None)
-        by_x, by_y = self.flights[k, "end"]
+        span = pl.ds(*self.spans[half])
+        sems = self.end_s.at[k, half], self.end_r.at[k, half]
+        by_x, by_y = self.flights[k, half, "end"]
         by_x.wait_recv()
-        half = done.at[k, at.qx, rows, pl.ds(start_a, size_a)]
-        first = self.keep(remote(half, half, self.end_s.at[k, 2], self.end_r.at[k, 2], at.y))
+        part = done.at[k, at.qx, span, pl.ds(start_a, size_a)]
+        first = self.keep(remote(part, part, sems[0].at[2], sems[1].at[2], at.y))
         by_y.wait_recv()
-        half = done.at[k, at.qy, rows, pl.ds(start_b, size_b)]
-        second = self.keep(remote(half, half, self.end_s.at[k, 3], self.end_r.at[k, 3], at.x))
-        self.flights[k, "end"] = [first, second]
-
-    def five(self, k):
-        for copy in self.flights[k, "end"]:
+        part = done.at[k, at.qy, span, pl.ds(start_b, size_b)]
+        second = self.keep(remote(part, part, sems[0].at[3], sems[1].at[3], at.x))
+        self.flights[k, half, "end"] = [first, second]
+
+    def five(self, n):
+        k, _, half, _ = self.place(n)
+        for copy in self.flights[k, half, "end"]:
             copy.wait_recv()
-        copy = pltpu.make_async_copy(self.done.at[k], self.outs[k], self.out_sem.at[k])
+        span = pl.ds(*self.spans[half])
+        copy = pltpu.make_async_copy(self.done.at[k, :, span], self.outs[k].at[:, span], self.out_sem.at[k, half])
         copy.start()
         self.outgoing.append(copy)
 
-    def turn(self, t, first, last):
-        items = last - first
-        if t + 2 < items:
-            self.prefetch(first + t + 2)
-        if t < items:
-            self.one(first + t)
-        if 0 <= t - 1 < items:
-            self.two(first + t - 1)
-        if 0 <= t - 2 < items:
-            self.three(first + t - 2)
-        for lag, stage in ((3, self.four), (4, self.five)):
-            n = first + t - lag
-            if first <= n < last and n % self.ring == self.ring - 1:
-                stage(n // self.ring)
+    def turn(self, t):
+        if t + AHEAD < self.total:
+            self.prefetch(t + AHEAD)
+        stages = (self.one, self.two, self.three, self.four, self.five)
+        for i, stage in enumerate(stages):
+            n = t - LAG * i
+            if 0 <= n < self.total and (i < 3 or self.place(n)[1] == self.ring - 1):
+                stage(n)
 
     def finish(self):
         for copy in self.outgoing:
@@ -645,17 +663,17 @@
     count = images * seq
     pad = pre_ref.shape[0]
 
-    def piece(k, index, q):
+    def piece(k, index, q, span):
         if k == 0:
-            return fc2_ref.at[index, q]
+            return fc2_ref.at[index, q, span]
         if k == 1:
-            return fc1_ref.at[index, :, pl.ds(q * width, width)]
-        line = pl.ds(pl.multiple_of(index * rows, 8), rows)
+            return fc1_ref.at[index, span, pl.ds(q * width, width)]
+        line = pl.ds(pl.multiple_of(index * rows + span.start, 8), span.size)
         if q == 3:
             return proj_ref.at[line, :]
         return triple_ref.at[q, line, :]
 
-    work = Reducer(at, piece, outs, refs[19:], width)
+    work = Reducer(at, piece, outs, refs[19:], rows, width)
     moves, fetched = {}, []
 
     def fetch(name, src, dst):
@@ -673,8 +691,8 @@
         copy.start()
         moves[name] = [copy]
 
-    work.prefetch(0)
-    work.prefetch(1)
+    for n in range(AHEAD):
+        work.prefetch(n)
 
     def lines(image):
         return pl.ds(image * seq, seq)
@@ -791,13 +809,13 @@
     def tail_zero():
         gm_row[:, 2 * width :] = vectors_ref[...]
         for f in range(fsdp):
-            gms[0, f] = gm_row[:, f * held : (f + 1) * held].astype(jnp.bfloat16).astype(jnp.float32)
+            gms[0, f] = gm_row[:, f * held : (f + 1) * held].astype(jnp.bfloat16)
         swaps[0].start(lambda device: gms.at[0, device[1]], gms.at[1, at.f])
 
     def tail_one():
         swaps[0].arrived()
         gms[1, at.f] = gms[0, at.f]
-        every = gms[1].reshape(fsdp * pad, held).astype(jnp.bfloat16)
+        every = gms[1].astype(jnp.float32).reshape(fsdp * pad, held).astype(jnp.bfloat16)
         parts[...] = times_back(every, ada_ref[...]).reshape(parts.shape)
         swaps[1].start(lambda device: parts.at[device[1]], mine_in.at[at.f])
         far[0].start(lambda device: gms.at[1], all_gm_ref.at[at.d])
@@ -819,9 +837,8 @@
         pre_cond = pre_ref[...]
         sig = jax.nn.sigmoid(pre_cond)
         grad_pre = grad_cond * (sig * (1.0 + pre_cond * (1.0 - sig)))
-        grad_pre = grad_pre.astype(jnp.bfloat16).astype(jnp.float32)
-        pres[at.f, :, :width] = grad_pre + picker_ref[...]
-        pres[at.f, :, width:] = router.astype(jnp.float32)
+        pres[at.f, :, :width] = (grad_pre + picker_ref[...]).astype(jnp.bfloat16)
+        pres[at.f, :, width:] = router
         swaps[2].start(lambda device: pres.at[at.f], pres.at[at.f])
 
     def tail_three():
@@ -831,23 +848,15 @@
 
     early = [partial(attention, image, half) for image in range(images) for half in range(2)]
     early += [partial(weigh, q) for q in range(3)] + [wait_terms]
-    late = [partial(spread, q) for q in range(3)] + [partial(norm, image) for image in range(images)]
-    late += [tail_zero, tail_one, tail_two, tail_three]
-    split = 2 * ring
-
-    def plan(turns, steps, turn):
-        done = 0
-        for t in range(turns):
-            turn(t)
-            upto = -(-len(steps) * (t + 1) // turns)
-            for step in steps[done:upto]:
+    norms = [partial(norm, image) for image in range(images)]
+    late = [[partial(spread, q)] for q in range(3)] + [[step] for step in norms]
+    late += [[tail_zero], [], [], [tail_one], [], [], [tail_two], [], [], [tail_three]]
+    steps = [[step] for step in early] + late
+    for t in range(work.total + 4 * LAG):
+        work.turn(t)
+        if t < len(steps):
+            for step in steps[t]:
                 step()
-            done = upto
-
-    plan(split + 4, early, lambda t: work.turn(t, 0, split))
-    work.prefetch(split)
-    work.prefetch(split + 1)
-    plan(ring + 4, late, lambda t: work.turn(t, split, split + ring))
     for swap in far:
         swap.arrived()
     for copy in small:
@@ -877,8 +886,8 @@
         partial(back_kernel, dp, fsdp, width, images, seq, heads),
         out_shape=[out((QUARTERS, rows, width), low)] * 3
         + [
-            out((dp, fsdp, pad, columns), f32),
-            out((dp, fsdp, pad, width + 128), f32),
+            out((dp, fsdp, pad, columns), low),
+            out((dp, fsdp, pad, width + 128), low),
             out((count, width), f32),
             out((3, width, width), low),
         ],
@@ -894,10 +903,10 @@
             vmem((count, width), f32),
             vmem((images, 128, seq), f32),
             vmem((pad, 6 * width), f32),
-            vmem((2, fsdp, pad, columns), f32),
+            vmem((2, fsdp, pad, columns), low),
             vmem((fsdp, pad, width), f32),
             vmem((fsdp, pad, width), f32),
-            vmem((fsdp, pad, width + 128), f32),
+            vmem((fsdp, pad, width + 128), low),
             dma((3 * fsdp + 3 + 2 * images,)),
             dma((5 + images,)),
             dma((3, fsdp - 1)),
@@ -942,18 +951,15 @@
     hidden = fc1_weight.shape[1]
     entries = time_weight.shape[0] * fsdp
     me_fsdp = lax.axis_index("fsdp")
-    pad = (images // 8 + 1) * 8
+    pad = -(-(images + 2) // 8) * 8
 
     def padded(array, value=0.0):
         return jnp.pad(array, ((0, pad - images), (0, 0)), constant_values=value)
 
     embedded = sinusoid(timesteps, entries).astype(jnp.bfloat16)
+    digits = jnp.stack([labels // DIGIT, labels % DIGIT], axis=1).astype(jnp.bfloat16)
     asked = jnp.concatenate(
-        [
-            padded(embedded.astype(jnp.float32)),
-            padded(jnp.broadcast_to(labels.astype(jnp.float32)[:, None], (images, 128)), -1.0),
-        ],
-        axis=1,
+        [padded(embedded), jnp.pad(padded(digits, -1.0), ((0, 0), (0, 126)))], axis=1
     )
     routers = jnp.pad(
         jnp.concatenate([head_router, token_router], axis=1), ((0, 0), (0, 127 - heads))
@@ -980,7 +986,7 @@
     routers_full = routers_full.reshape(width, 128)
     chooser, picker = routers_full[:, :heads], routers_full[:, heads : heads + 1]
     everyone = dp * fsdp * pad
-    all_cond = all_cond.reshape(everyone, width).astype(jnp.bfloat16)
+    all_cond = all_cond.reshape(everyone, width)
     all_asked = all_asked.reshape(everyone, asked.shape[1])
     pre_cond = pre_cond_pad[:images]
     cond = jax.nn.silu(pre_cond).astype(jnp.bfloat16)
@@ -1031,6 +1037,7 @@
     grad_attn = (grad_middle * gate_one).astype(jnp.bfloat16).reshape(count, width)
     grad_merger = times_rows(mixed, grad_attn).astype(jnp.bfloat16)
     grad_mixed = times_back(grad_attn, merger).astype(jnp.bfloat16)
+    picker_high = lax.reduce_precision(grad_picker, 8, 7)
     vectors = jnp.concatenate([grad_gate_one, grad_shift_two, grad_scale_two, grad_gate_two], axis=1)
     *sums, all_grad, all_pre, grad_inputs, _ = back_half(
         [
@@ -1052,7 +1059,7 @@
         routers_full,
         ada_weight,
         pre_cond_pad,
-        jnp.pad(grad_picker, ((pad - 1, 0), (0, 0))),
+        jnp.pad(jnp.concatenate([picker_high, grad_picker - picker_high], axis=0), ((pad - 2, 0), (0, 0))),
         width,
         images,
         seq,
@@ -1075,20 +1082,22 @@
     sum_expand = jnp.concatenate([sums[1][i] for i in range(QUARTERS)], axis=1)
     sum_shrink = sums[0].reshape(QUARTERS * rows, width)
 
-    sum_ada = times_rows(all_cond, all_grad.reshape(everyone, -1).astype(jnp.bfloat16))
+    sum_ada = times_rows(all_cond, all_grad.reshape(everyone, -1))
     sum_picker = lax.dynamic_slice_in_dim(
-        jnp.sum(all_pre[:, :, pad - 1, :width], axis=(0, 1)), me_fsdp * rows, rows, axis=0
+        jnp.sum(all_pre[:, :, pad - 2 :, :width].astype(jnp.float32), axis=(0, 1, 2)), me_fsdp * rows, rows, axis=0
     )[:, None]
     is_image = (jnp.arange(pad) < images)[None, None, :, None]
-    all_pre = jnp.where(is_image, all_pre, 0.0).reshape(everyone, -1).astype(jnp.bfloat16)
+    all_pre = jnp.where(is_image, all_pre, jnp.bfloat16(0.0)).reshape(everyone, -1)
     all_router = all_pre[:, width : width + heads]
     all_pre = all_pre[:, :width]
     own_entries = entries // fsdp
     all_embedded = lax.dynamic_slice_in_dim(
         all_asked[:, :entries], me_fsdp * own_entries, own_entries, axis=1
-    ).astype(jnp.bfloat16)
+    )
     classes = jnp.arange(class_table.shape[0], dtype=jnp.float32)
-    all_rows = (all_asked[:, entries : entries + 1] == classes[None, :]).astype(jnp.bfloat16)
+    all_digits = all_asked[:, entries : entries + 2].astype(jnp.float32)
+    all_labels = all_digits[:, :1] * DIGIT + all_digits[:, 1:]
+    all_rows = (all_labels == classes[None, :]).astype(jnp.bfloat16)
     sum_time = times_rows(all_embedded, all_pre)
     sum_table = times_rows(
         all_rows, lax.dynamic_slice_in_dim(all_pre, me_fsdp * rows, rows, axis=1)

time: 576 us -> 531 us (0.922)
  Pallas kernels: 376 us -> 332 us
    pallas_call x1, Pallas kernels: 220 us -> 184 us  [back_half(): pl.pallas_call(partial(back_kernel, dp, fsdp, width, images, seq, heads),...]
    pallas_call x1, Pallas kernels: 147 us -> 138 us  [gather_weights(): pl.pallas_call(partial(gather_kernel, dp, fsdp, width), out_shape=[out((f...]
where the time goes in v5:
time: 531 us; the launch traced here: 521 us
  Pallas kernels  332 us (63%)
  matrix products  127 us (24%)
  other arithmetic  32.8 us (6%)
  local copies, waits for them, and re-layouts  27.9 us (5%)
    pallas_call x1, Pallas kernels, back_half(): pl.pallas_call(partial(back_kernel, dp, fsdp, width, images, seq, heads),...  184 us
    pallas_call x1, Pallas kernels, gather_weights(): pl.pallas_call(partial(gather_kernel, dp, fsdp, width), out_shape=[out((f...  138 us
    dot_general x6, matrix products, matmul(): return jnp.dot(left, right, preferred_element_type=jnp.float32)  59.7 us
    dot_general x3, matrix products, times_back(): lax.dot_general(left, right, (((1,), (1,)), ((), ())), preferred_element_...  34.4 us
    dot_general x8, matrix products, times_rows(): lax.dot_general(left, right, (((0,), (0,)), ((), ())), preferred_element_...  32.6 us
    unnamed x110, local copies, waits for them, and re-layouts  19.6 us

profile of v5, /device:TPU:0, one launch (start us, length us, event | category | flops | bytes accessed | tf_op | source)
XLA Modules:
  0.0 521.1 jit_solution(16602934307167687941)
XLA Ops:
  3.2 1.8 convert_reduce_fusion
  5.0 2.1 fusion.18
  8.4 2.9 copy.51.refs_6_.refs_15_
  12.3 1.3 copy-done.3
  13.6 1.3 copy-done.4
  14.9 138.3 %gather.1 = (bf16[8,144,4608]{2,1,0:T(8,128)(2,1)S(1)}, bf16[8,144,4608]{2,1,0:T(8,128)(2,1)}, bf16[8,4,144,1152]{3,2,1,0:T(8,128)(2,1)}, f32[8,1152]{1,0:T(8,12...) custom-call(bf16[144,4608]{1,0:T(8,128)(2,1)S(1)} %pad_maximum_fusio, ...), custom_call_target="tpu_custom_call" | custom-call | tf_op jit(solution)/shard_map/gather/pallas_call | solution.py:277
  153.2 4.0 copy-done.1
  162.3 1.6 slice.88
  164.5 2.8 fusion.21
  167.3 1.2 copy-done.22
  168.5 12.2 %fusion.9.j.refs_3_ = bf16[768,3456]{1,0:T(8,128)(2,1)} fusion(bf16[768,1152]{1,0:T(8,128)(2,1)S(1)} %bitcast.114, bf16[1152,4608]{1,0:T(8,128)(2,1)} %bitcast.92), kind=kOutput, calls=%fused_computation.15 | convolution fusion | flops 6117949440 | bytes 15040512 | tf_op jit(solution)/shard_map/dot_general | solution.py:35
  180.7 9.5 %attend.1 = (bf16[768,1152]{1,0:T(8,128)(2,1)S(1)}, f32[3,16,256]{2,1,0:T(8,128)S(1)}) custom-call(bf16[768,3456]{1,0:T(8,128)(2,1)} %fusion.9.j.refs_3_, f32[3,1,16]{2,1,0:T(1,128)S(1)} %copy.53.g.refs_10_), custom_call_target="tpu_custom_call" | custom-call | tf_op jit(solution)/shard_map/attend/pallas_call | solution.py:370
  190.3 4.5 fusion.25
  197.4 1.2 add_convert_fusion.1
  201.3 1.9 fusion.16
  204.4 15.0 %fusion.71 = f32[768,4608]{1,0:T(8,128)} fusion(bf16[768,1152]{1,0:T(8,128)(2,1)S(1)} %bitcast.122, bf16[4608,1152]{1,0:T(8,128)(2,1)} %bitcast.129), kind=kOutput, calls=%fused_computation.149 | convolution fusion | flops 8153726976 | bytes 26542080 | tf_op jit(solution)/shard_map/dot_general | solution.py:45
  219.5 24.7 %fusion.6 = (bf16[768,4608]{1,0:T(8,128)(2,1)}, bf16[768,4608]{1,0:T(8,128)(2,1)}) fusion(f32[768,4608]{1,0:T(8,128)} %fusion.71, bf16[768,1152]{1,0:T(8,128)(2,1)S(1)} %bitcast.108, bf16[1152,4608]{1,0:T(8,128)(2,1)} %bitcast.127), kind=kOutput, calls=%fused_computation.10 | convolution fusion | flops 8231583744 | bytes 40697856 | tf_op jit(solution)/shard_map/dot_general | solution.py:35
  244.2 17.5 %fusion.23 = (f32[3,1152]{1,0:T(4,128)}, f32[3,256]{1,0:T(4,128)S(1)}, bf16[3,256,1152]{2,1,0:T(8,128)(2,1)}) fusion(bf16[3,256,1152]{2,1,0:T(8,128)(2,1)S(1)} %copy-done.20, f32[3,256]{1,0:T(4,128)S(1)} %convert_multiply_fusion.2, f32[3,1152]{1,0:T(4,128)S(1)} %copy-done.38, f32[3,256,1152]{2,1,0:T(8,128)} %copy-done.13, ...), kind=kOutput, calls=%fused_computation.36 | convolution fusion | flops 8163454976 | bytes 24806400 | tf_op jit(solution)/shard_map/dot_general | solution.py:35
  262.9 13.6 %convolution_add_fusion = f32[768,1152]{1,0:T(8,128)S(1)} fusion(bf16[768,4608]{1,0:T(8,128)(2,1)} %get-tuple-element.53, bf16[1152,4608]{1,0:T(8,128)(2,1)} %bitcast.128, f32[1152]{0:T(1024)} %convert.28, f32[768]{0:T(1024)S(1)} %reshape.197), kind=kOutput, calls=%fused_computation.27 | convolution fusion | flops 8155496448 | bytes 21241344 | tf_op jit(solution)/shard_map/dot_general | solution.py:45
  278.4 1.5 multiply_reduce_fusion
  280.9 3.6 multiply_reduce_fusion.1
  286.6 4.0 convolution_convert_fusion.2.refs_2_
  290.6 5.7 %convolution_convert_fusion.3.refs_4_ = bf16[768,1152]{1,0:T(8,128)(2,1)} fusion(bf16[768,1152]{1,0:T(8,128)(2,1)S(1)} %bitcast.121, bf16[1152,4608]{1,0:T(8,128)(2,1)} %bitcast.94), kind=kOutput, calls=%fused_computation.44 | convolution fusion | flops 2039316480 | bytes 6193152 | tf_op jit(solution)/shard_map/dot_general | solution.py:45
  296.4 10.7 %convolution_convert_fusion = bf16[1152,4608]{1,0:T(8,128)(2,1)} fusion(bf16[768,1152]{1,0:T(8,128)(2,1)S(1)} %bitcast.109, bf16[768,4608]{1,0:T(8,128)(2,1)S(1)} %bitcast.135), kind=kOutput, calls=%fused_computation.2 | convolution fusion | flops 8159035392 | bytes 19464192 | tf_op jit(solution)/shard_map/dot_general | solution.py:39
  307.1 11.7 %convolution_convert_fusion.1 = bf16[4608,1152]{1,0:T(8,128)(2,1)} fusion(bf16[768,4608]{1,0:T(8,128)(2,1)S(1)} %bitcast.133, bf16[768,1152]{1,0:T(8,128)(2,1)S(1)} %bitcast.123), kind=kOutput, calls=%fused_computation.3 | convolution fusion | flops 8159035392 | bytes 19464192 | tf_op jit(solution)/shard_map/dot_general | solution.py:39
  318.9 184.3 %back.1 = (bf16[4,144,1152]{2,1,0:T(8,128)(2,1)}, bf16[4,144,1152]{2,1,0:T(8,128)(2,1)}, bf16[4,144,1152]{2,1,0:T(8,128)(2,1)}, bf16[4,8,8,864]{3,2,1,0:T(8,128)...) custom-call(bf16[8,4,144,1152]{3,2,1,0:T(8,128)(2,1)} %bitcast.113, ...), custom_call_target="tpu_custom_call" | custom-call | tf_op jit(solution)/shard_map/back/pallas_call | solution.py:885
  503.2 1.4 convert_reduce_fusion.1
  510.8 1.4 pad_maximum_fusion.1
  512.6 1.8 pad_maximum_fusion
  514.4 1.8 bitcast_convert_fusion
  516.1 2.7 convolution_bitcast_fusion
  518.9 1.8 copy.63
  (166 shorter events, 29.4 us)
Async XLA Ops:
  0.6 6.4 %copy-start.46 = (bf16[144,1]{0,1:T(2,128)(2,1)S(1)}, bf16[144,1]{0,1:T(2,128)(2,1)}, u32[]{:S(2)}) copy-start(bf16[144,1]{0,1:T(2,128)(2,1)} %param.29) | copy-start | bytes 868
  0.7 7.6 %copy-start.33 = (bf16[144,1152]{1,0:T(8,128)(2,1)S(1)}, bf16[144,1152]{1,0:T(8,128)(2,1)}, u32[]{:S(2)}) copy-start(bf16[144,1152]{1,0:T(8,128)(2,1)} %param.26) | copy-start | bytes 995332
  0.7 7.6 %copy-start.29 = (bf16[144,3456]{1,0:T(8,128)(2,1)S(1)}, bf16[144,3456]{1,0:T(8,128)(2,1)}, u32[]{:S(2)}) copy-start(bf16[144,3456]{1,0:T(8,128)(2,1)} %param.25) | copy-start | bytes 2985988
  0.7 6.4 %copy-start.44 = (bf16[144,16]{0,1:T(8,128)(2,1)S(1)}, bf16[144,16]{0,1:T(8,128)(2,1)}, u32[]{:S(2)}) copy-start(bf16[144,16]{0,1:T(8,128)(2,1)} %param.24) | copy-start | bytes 13828
  0.7 6.6 %copy-start.34 = (bf16[1000,144]{0,1:T(8,128)(2,1)S(1)}, bf16[1000,144]{0,1:T(8,128)(2,1)}, u32[]{:S(2)}) copy-start(bf16[1000,144]{0,1:T(8,128)(2,1)} %param.22) | copy-start | bytes 864004
  14.9 142.4 %copy-start = (bf16[1152,864]{1,0:T(8,128)(2,1)}, bf16[1152,864]{1,0:T(8,128)(2,1)S(1)}, u32[]{:S(2)}) copy-start(bf16[1152,864]{1,0:T(8,128)(2,1)S(1)} %copy.51.refs_6_.refs_15_) | copy-start | bytes 5971972
  14.9 143.1 %copy-start.48 = (s32[3,16]{1,0:T(4,128)S(1)}, s32[3,16]{1,0:T(4,128)}, u32[]{:S(2)}) copy-start(s32[3,16]{1,0:T(4,128)} %param.18) | copy-start | bytes 580
  153.2 4.1 copy-start.1
  158.3 22.5 %copy-start.12 = (f32[3,1,16]{2,1,0:T(1,128)}, f32[3,1,16]{2,1,0:T(1,128)S(1)}, u32[]{:S(2)}) copy-start(f32[3,1,16]{2,1,0:T(1,128)S(1)} %copy.53.g.refs_10_) | copy-start | bytes 580
  160.8 34.0 %copy-start.36 = (f32[3,1152]{1,0:T(4,128)}, f32[3,1152]{1,0:T(4,128)S(1)}, u32[]{:S(2)}) copy-start(f32[3,1152]{1,0:T(4,128)S(1)} %get-tuple-element.70) | copy-start | bytes 41476
  190.3 4.6 copy-start.10
  190.3 4.6 copy-start.15
  219.5 24.7 %copy-start.20 = (bf16[3,256,1152]{2,1,0:T(8,128)(2,1)S(1)}, bf16[3,256,1152]{2,1,0:T(8,128)(2,1)}, u32[]{:S(2)}) copy-start(bf16[3,256,1152]{2,1,0:T(8,128)(2,1)} %param.20) | copy-start | bytes 5308420
  219.5 24.7 %copy-start.38 = (f32[3,1152]{1,0:T(4,128)S(1)}, f32[3,1152]{1,0:T(4,128)}, u32[]{:S(2)}) copy-start(f32[3,1152]{1,0:T(4,128)} %get-tuple-element.67) | copy-start | bytes 41476
  244.2 17.5 %copy-start.43 = (s32[3,256]{1,0:T(4,128)S(1)}, s32[3,256]{1,0:T(4,128)}, u32[]{:S(2)}) copy-start(s32[3,256]{1,0:T(4,128)} %param.19) | copy-start | bytes 9220
  262.9 13.7 %copy-start.40 = (bf16[3,256]{1,0:T(4,128)(2,1)S(1)}, bf16[3,256]{1,0:T(4,128)(2,1)}, u32[]{:S(2)}) copy-start(bf16[3,256]{1,0:T(4,128)(2,1)} %multiply_convert_fusion.2) | copy-start | bytes 4612
  262.9 14.1 %copy-start.14 = (f32[3,256,1152]{2,1,0:T(8,128)S(1)}, f32[3,256,1152]{2,1,0:T(8,128)}, u32[]{:S(2)}) copy-start(f32[3,256,1152]{2,1,0:T(8,128)} %copy-done.13) | copy-start | bytes 10616836
  262.9 14.1 %copy-start.31 = (f32[3,1152]{1,0:T(4,128)S(1)}, f32[3,1152]{1,0:T(4,128)}, u32[]{:S(2)}) copy-start(f32[3,1152]{1,0:T(4,128)} %get-tuple-element.66) | copy-start | bytes 41476
  280.9 4.3 copy-start.41
  280.9 5.4 %copy-start.37 = (f32[3,1152]{1,0:T(4,128)S(1)}, f32[3,1152]{1,0:T(4,128)}, u32[]{:S(2)}) copy-start(f32[3,1152]{1,0:T(4,128)} %copy-done.36) | copy-start | bytes 41476
  284.5 6.1 %copy-start.16 = (f32[3,256,1152]{2,1,0:T(8,128)}, f32[3,256,1152]{2,1,0:T(8,128)S(1)}, u32[]{:S(2)}) copy-start(f32[3,256,1152]{2,1,0:T(8,128)S(1)} %get-tuple-element.50) | copy-start | bytes 10616836
  286.6 9.8 %slice-start.2 = ((s8[7077888]{0:T(1024)(128)(4,1)}), s8[4194304]{0:T(1024)(128)(4,1)S(1)}, s32[]{:S(2)}) async-start(s8[7077888]{0:T(1024)(128)(4,1)} %bitcast.134), calls=%async_computation.2 | async-start | bytes 8388608
  290.6 5.7 %slice-start.3 = ((s8[7077888]{0:T(1024)(128)(4,1)}), s8[2883584]{0:T(1024)(128)(4,1)S(1)}, s32[]{:S(2)}) async-start(s8[7077888]{0:T(1024)(128)(4,1)} %bitcast.134), calls=%async_computation.3 | async-start | bytes 5767168
  290.6 16.5 %slice-start = ((s8[7077888]{0:T(1024)(128)(4,1)}), s8[4194304]{0:T(1024)(128)(4,1)S(1)}, s32[]{:S(2)}) async-start(s8[7077888]{0:T(1024)(128)(4,1)} %bitcast.132), calls=%async_computation | async-start | bytes 8388608
  296.3 10.8 %copy-start.25 = (bf16[3,256,1152]{2,1,0:T(8,128)(2,1)S(1)}, bf16[3,256,1152]{2,1,0:T(8,128)(2,1)}, u32[]{:S(2)}) copy-start(bf16[3,256,1152]{2,1,0:T(8,128)(2,1)} %copy-done.24) | copy-start | bytes 5308420
  296.3 10.8 %slice-start.1 = ((s8[7077888]{0:T(1024)(128)(4,1)}), s8[2883584]{0:T(1024)(128)(4,1)S(1)}, s32[]{:S(2)}) async-start(s8[7077888]{0:T(1024)(128)(4,1)} %bitcast.132), calls=%async_computation.1 | async-start | bytes 5767168
  318.9 186.4 %copy-start.47 = (pred[8]{0:T(512)(128)(4,1)S(1)}, pred[8]{0:T(512)(128)(4,1)}, u32[]{:S(2)}) copy-start(pred[8]{0:T(512)(128)(4,1)} %iota_compare_fusion.7) | copy-start | bytes 28
  318.9 187.6 %copy-start.35 = (bf16[256,256]{1,0:T(8,128)(2,1)S(1)}, bf16[256,256]{1,0:T(8,128)(2,1)}, u32[]{:S(2)}) copy-start(bf16[256,256]{1,0:T(8,128)(2,1)} %slice.88) | copy-start | bytes 393220
  318.9 188.6 %copy-start.7 = (bf16[4,8,8,1152]{3,2,1,0:T(8,128)(2,1)S(1)}, bf16[4,8,8,1152]{3,2,1,0:T(8,128)(2,1)}, u32[]{:S(2)}) copy-start(bf16[4,8,8,1152]{3,2,1,0:T(8,128)(2,1)} %copy-done.6) | copy-start | bytes 1769476
  503.2 5.1 copy-start.45
  503.2 6.4 %copy-start.28 = (bf16[4,144,1152]{2,1,0:T(8,128)(2,1)S(1)}, bf16[4,144,1152]{2,1,0:T(8,128)(2,1)}, u32[]{:S(2)}) copy-start(bf16[4,144,1152]{2,1,0:T(8,128)(2,1)} %get-tuple-element.40) | copy-start | bytes 3981316
  514.4 4.5 copy-start.23
  (21 other events, 33.7 us)

commit v6 on v5

--- a/solution.py
+++ b/solution.py
@@ -125,17 +125,19 @@
     return ref.at[(*lead, q, slice(None), pl.ds(start, size))]
 
 
-def gather_kernel(dp, fsdp, width, *refs):
+def front_kernel(dp, fsdp, width, images, seq, heads, *refs):
     weights = 3
     ring = fsdp // 2
     shards, refs = refs[:weights], refs[weights:]
-    ask_ref, time_ref, table_ref, ada_ref, router_ref = refs[:5]
-    refs = refs[5:]
+    ask_ref, time_ref, table_ref, ada_ref, router_ref, mask_ref, tokens_ref = refs[:7]
+    refs = refs[7:]
     fulls, refs = refs[:weights], refs[weights:]
     pre_ref, mod_ref, routers_ref, all_cond_ref, all_ask_ref = refs[:5]
-    refs = refs[5:]
-    asks, parts, mine_in, conds, columns = refs[:5]
-    refs = refs[5:]
+    h1_out, joint_out, lse_out, mixed_out, attn_out, middle_out, h2_out = refs[5:12]
+    refs = refs[12:]
+    asks, parts, mine_in, conds, columns, mods, gates = refs[:7]
+    tokens, h1, joint, lse, mixed, attn, middle, h2, stage, move_sem = refs[7:17]
+    refs = refs[17:]
     (own_sem, core_s, core_r, ring_s, ring_r, x_s, x_r, y_s, y_r, a_s, a_r, b_s, b_r) = refs[:13]
     mate_s, mate_r, cousin_s, cousin_r, small_sem = refs[13:]
     at = Place(dp, fsdp)
@@ -204,15 +206,117 @@
         swaps[2].arrived()
         every = conds[...].astype(jnp.float32).reshape(group, width).astype(jnp.bfloat16)
         columns[...] = matmul(every, ada_ref[...]).reshape(columns.shape)
-        swaps[3].start(lambda device: columns.at[device[1]], mod_ref.at[at.f])
+        swaps[3].start(lambda device: columns.at[device[1]], mods.at[at.f])
         far[0].start(lambda device: conds, all_cond_ref.at[at.d])
         keep(conds, all_cond_ref.at[at.d])
-        keep(columns.at[at.f], mod_ref.at[at.f])
-
-    extra = {0: cond_one, 1: cond_two, 2: cond_three}
+
+    def cond_four():
+        swaps[3].arrived()
+        swaps[4].arrived()
+        mods[at.f] = columns[at.f]
+        routers_ref[at.f] = router_ref[...]
+        held = mods.shape[2]
+        for f in range(fsdp):
+            mod_ref[:, f * held : (f + 1) * held] = mods[f]
+        chosen = matmul(conds[at.f], routers_ref[...].reshape(width, router_ref.shape[1]))
+        gates[...] = mask_ref[...] * jax.nn.sigmoid(chosen)
+
+    moves, moved = {}, []
+
+    def move(name, src, dst):
+        copy = pltpu.make_async_copy(src, dst, move_sem.at[len(moved)])
+        copy.start()
+        moved.append(copy)
+        moves.setdefault(name, []).append(copy)
+
+    def have(name):
+        for copy in moves.pop(name):
+            copy.wait()
+
+    def line_of(image):
+        return pl.ds(image * seq, seq)
+
+    def bring(q):
+        for f in range(fsdp):
+            src = fulls[0].at[f, :, pl.ds(q * width, width)]
+            move("w" + str(q), src, stage.at[q % 2, pl.ds(f * rows, rows), :])
+
+    def modulated(image, index):
+        return mod_ref[image : image + 1, index * width : (index + 1) * width]
+
+    step = 32
+
+    def normed(value, scale, shift):
+        centered = value - jnp.mean(value, axis=-1, keepdims=True)
+        inverse = lax.rsqrt(jnp.mean(centered * centered, axis=-1, keepdims=True) + EPSILON)
+        return (centered * inverse * scale + shift).astype(jnp.bfloat16)
+
+    def joint_here():
+        for copy in first_landed:
+            copy.wait_recv()
+        locals_[0].wait()
+        bring(0)
+        bring(1)
+
+    def norm_one(image):
+        if image == 0:
+            have("tokens")
+        shift, scale = modulated(image, 0), 1.0 + modulated(image, 1)
+
+        @pl.loop(0, seq // step)
+        def _(i):
+            line = pl.ds(pl.multiple_of(image * seq + i * step, step), step)
+            h1[line, :] = normed(tokens[line, :].astype(jnp.float32), scale, shift)
+
+        if image == images - 1:
+            move("h1", h1, h1_out)
+
+    def project(q):
+        have("w" + str(q))
+
+        @pl.loop(0, images)
+        def _(image):
+            line = pl.ds(pl.multiple_of(image * seq, seq), seq)
+            joint[line, pl.ds(q * width, width)] = matmul(h1[line, :], stage[q % 2]).astype(jnp.bfloat16)
+
+        if q + 2 < QUARTERS:
+            bring(q + 2)
+        if q == 2:
+            move("joint", joint, joint_out)
+
+    def attention(image, half):
+        span = range(0, heads // 2) if half == 0 else range(heads // 2, heads)
+        attend_image(joint.at[line_of(image)], gates, mixed.at[line_of(image)], lse, image, seq, heads, span)
+        if image == images - 1 and half == 1:
+            move("mixed", mixed, mixed_out)
+            move("lse", lse, lse_out)
+
+    def merge(image):
+        if image == 0:
+            have("w3")
+        line = line_of(image)
+        attn[line, :] = matmul(mixed[line, :], stage[1])
+        gate, shift, scale = modulated(image, 2), modulated(image, 3), 1.0 + modulated(image, 4)
+
+        @pl.loop(0, seq // step)
+        def _(i):
+            here = pl.ds(pl.multiple_of(image * seq + i * step, step), step)
+            value = tokens[here, :].astype(jnp.float32) + gate * attn[here, :]
+            middle[here, :] = value
+            h2[here, :] = normed(value, scale, shift)
+
+        move("attn", attn.at[line], attn_out.at[line])
+        move("middle", middle.at[line], middle_out.at[line])
+        move("h2", h2.at[line], h2_out.at[line])
+
+    move("tokens", tokens_ref, tokens)
+    work = [joint_here] + [partial(norm_one, image) for image in range(images)]
+    work += [partial(project, q) for q in range(3)]
+    work += [partial(attention, image, half) for image in range(images) for half in range(2)]
+    work += [partial(merge, image) for image in range(images)]
+    extra = {0: cond_one, 1: cond_two, 2: cond_three, 4: cond_four}
     swaps[0].start(lambda device: ask_ref, asks.at[at.f])
     swaps[4].start(lambda device: router_ref, routers_ref.at[at.f])
-    keep(router_ref, routers_ref.at[at.f])
 
     items = [(k, step) for k in range(weights) for step in range(1, ring)]
     rings = {items[0]: go(ring_copy(*items[0]))}
@@ -222,87 +326,114 @@
         copy.start()
         locals_.append(copy)
         landed.append(go(remote(shards[k], fulls[k].at[at.f], core_s.at[k, 0], core_r.at[k, 0], at.core)))
-    flights = {}
-    for turn in range(len(items) + 2):
+    flights, first_landed = {}, [landed[0]]
+    begin, turns = ring + 1, len(items) + 2
+    done = 0
+    for turn in range(turns):
         if turn < len(items):
-            k, step = items[turn]
-            rings[k, step].wait_recv()
+            k, hop = items[turn]
+            rings[k, hop].wait_recv()
             if turn + 1 < len(items):
                 rings[items[turn + 1]] = go(ring_copy(*items[turn + 1]))
-            mine = view(fulls[k], (at.shard(step),), at.q, width)
+            mine = view(fulls[k], (at.shard(hop),), at.q, width)
             flights[turn] = (
-                go(remote(mine, mine, x_s.at[k, step - 1], x_r.at[k, step - 1], at.x)),
-                go(remote(mine, mine, y_s.at[k, step - 1], y_r.at[k, step - 1], at.y)),
+                go(remote(mine, mine, x_s.at[k, hop - 1], x_r.at[k, hop - 1], at.x)),
+                go(remote(mine, mine, y_s.at[k, hop - 1], y_r.at[k, hop - 1], at.y)),
             )
         if 0 <= turn - 1 < len(items):
-            k, step = items[turn - 1]
+            k, hop = items[turn - 1]
             by_x, by_y = flights[turn - 1]
             by_x.wait_recv()
-            half = view(fulls[k], (at.shard(step),), at.qx, width, part_a)
-            first = go(remote(half, half, a_s.at[k, step - 1], a_r.at[k, step - 1], at.y))
+            half = view(fulls[k], (at.shard(hop),), at.qx, width, part_a)
+            first = go(remote(half, half, a_s.at[k, hop - 1], a_r.at[k, hop - 1], at.y))
             by_y.wait_recv()
-            half = view(fulls[k], (at.shard(step),), at.qy, width, part_b)
-            second = go(remote(half, half, b_s.at[k, step - 1], b_r.at[k, step - 1], at.x))
+            half = view(fulls[k], (at.shard(hop),), at.qy, width, part_b)
+            second = go(remote(half, half, b_s.at[k, hop - 1], b_r.at[k, hop - 1], at.x))
             flights[turn - 1] = (first, second)
         if 0 <= turn - 2 < len(items):
-            k, step = items[turn - 2]
+            k, hop = items[turn - 2]
             for copy in flights[turn - 2]:
                 copy.wait_recv()
-            whole = fulls[k].at[at.shard(step)]
-            landed.append(go(remote(whole, whole, core_s.at[k, step], core_r.at[k, step], at.core)))
+            whole = fulls[k].at[at.shard(hop)]
+            copy = go(remote(whole, whole, core_s.at[k, hop], core_r.at[k, hop], at.core))
+            (landed if k else first_landed).append(copy)
         if turn in extra:
             extra[turn]()
-    for swap in (swaps[3], swaps[4], far[0], far[1]):
+        if turn >= begin:
+            upto = -(-len(work) * (turn + 1 - begin) // (turns - begin))
+            for part in work[done:upto]:
+                part()
+            done = upto
+    for swap in far:
         swap.arrived()
-    for copy in landed:
+    for copy in landed[1:]:
         copy.wait_recv()
-    for copy in locals_ + small:
+    for copy in locals_[1:] + small:
         copy.wait()
+    for name in ("h1", "joint", "mixed", "lse", "attn", "middle", "h2"):
+        have(name)
     for swap in swaps + far:
         swap.left()
     for copy in sent:
         copy.wait_send()
 
 
-def gather_weights(shards, asked, time_weight, class_table, ada_weight, routers, width, dp, fsdp):
+def front_half(
+    shards, asked, time_weight, class_table, ada_weight, routers, mask, tokens, width, images, seq, heads, dp, fsdp
+):
     ring = fsdp // 2
-    dma = pltpu.SemaphoreType.DMA
-    vmem = pltpu.VMEM
-    f32 = jnp.float32
+    dma, vmem = pltpu.SemaphoreType.DMA, pltpu.VMEM
+    low, f32 = jnp.bfloat16, jnp.float32
     steps = dma((3, ring - 1))
     pad, asking = asked.shape
     columns = ada_weight.shape[1]
+    count = images * seq
     out = jax.ShapeDtypeStruct
     any_space, in_vmem = pl.BlockSpec(memory_space=pl.ANY), pl.BlockSpec(memory_space=vmem)
+    results = [
+        out((count, width), low),
+        out((count, 3 * width), low),
+        out((images, heads, seq), f32),
+        out((count, width), low),
+        out((count, width), f32),
+        out((count, width), f32),
+        out((count, width), low),
+    ]
     return pl.pallas_call(
-        partial(gather_kernel, dp, fsdp, width),
+        partial(front_kernel, dp, fsdp, width, images, seq, heads),
         out_shape=[out((fsdp, *s.shape), s.dtype) for s in shards]
         + [
             out((pad, width), f32),
-            out((fsdp, pad, columns), f32),
+            out((pad, 6 * width), f32),
             out((fsdp, *routers.shape), routers.dtype),
-            out((dp, fsdp, pad, width), jnp.bfloat16),
-            out((dp, fsdp, pad, asking), jnp.bfloat16),
-        ],
-        in_specs=[any_space] * 3 + [in_vmem] * 5,
-        out_specs=[any_space] * 3 + [in_vmem] + [any_space] * 4,
+            out((dp, fsdp, pad, width), low),
+            out((dp, fsdp, pad, asking), low),
+        ]
+        + results,
+        in_specs=[any_space] * 3 + [in_vmem] * 6 + [any_space],
+        out_specs=[any_space] * 3 + [in_vmem] * 3 + [any_space] * 9,
         scratch_shapes=[
-            vmem((fsdp, pad, asking), jnp.bfloat16),
+            vmem((fsdp, pad, asking), low),
             vmem((fsdp, pad, width), f32),
             vmem((fsdp, pad, width), f32),
-            vmem((fsdp, pad, width), jnp.bfloat16),
+            vmem((fsdp, pad, width), low),
             vmem((fsdp, pad, columns), f32),
+            vmem((fsdp, pad, columns), f32),
+            vmem((pad, 128), f32),
+            vmem((count, width), low),
         ]
+        + [vmem(r.shape, r.dtype) for r in results]
+        + [vmem((2, width, width), low), dma((4 * fsdp + 5 + 3 * images,))]
         + [dma((3,)), dma((3, ring)), dma((3, ring))]
         + [steps] * 10
         + [dma((5, fsdp - 1))] * 2
         + [dma((2, dp - 1))] * 2
-        + [dma((4,))],
+        + [dma((2,))],
         compiler_params=pltpu.CompilerParams(
-            collective_id=0, has_side_effects=True, vmem_limit_bytes=32 * 2**20
+            collective_id=0, has_side_effects=True, vmem_limit_bytes=60 * 2**20
         ),
-        name="gather",
-    )(*shards, asked, time_weight, class_table, ada_weight, routers)
+        name="front",
+    )(*shards, asked, time_weight, class_table, ada_weight, routers, mask, tokens)
 
 
 def window(head, size):
@@ -313,25 +444,25 @@
     return low, high - low, own
 
 
-def attend_image(joint, gates, mixed, lse, image, seq, heads):
+def attend_image(joint, gates, mixed, lse, image, seq, heads, span):
     width = mixed.shape[1]
     size = width // heads
     scale = size ** (-0.5)
-    lines = pl.ds(pl.multiple_of(image * seq, seq), seq)
-    mixed[lines, :] = jnp.zeros((seq, width), mixed.dtype)
-    for head in range(heads):
+    if span[0] == 0:
+        mixed[...] = jnp.zeros((seq, width), mixed.dtype)
+    for head in span:
         low, wide, own = window(head, size)
-        query = joint[lines, pl.ds(low, wide)] * own
-        keys = joint[lines, pl.ds(width + low, wide)]
-        values = joint[lines, pl.ds(2 * width + low, wide)] * own
+        query = joint[:, pl.ds(low, wide)] * own
+        keys = joint[:, pl.ds(width + low, wide)]
+        values = joint[:, pl.ds(2 * width + low, wide)] * own
         raw = times_back(keys, query) * scale
         peak = jnp.max(raw, axis=0, keepdims=True)
         expo = jnp.exp(raw - peak)
         total = jnp.sum(expo, axis=0, keepdims=True)
         lse[image, head : head + 1, :] = peak + jnp.log(total)
         probs = (expo * (1.0 / total)).astype(jnp.bfloat16)
-        attended = times_rows(probs, values) * gates[image, 0, head]
-        mixed[lines, pl.ds(low, wide)] = mixed[lines, pl.ds(low, wide)] + attended.astype(jnp.bfloat16)
+        attended = times_rows(probs, values) * gates[image : image + 1, head : head + 1]
+        mixed[:, pl.ds(low, wide)] = mixed[:, pl.ds(low, wide)] + attended.astype(jnp.bfloat16)
 
 
 def attend_back_image(joint, grad_mixed, gates, lse, grad_joint, grad_gates, image, seq, heads, span):
@@ -362,22 +493,6 @@
         put(width + low, wide, matmul(grad_scores, query))
 
 
-def attend(joint, gates, seq):
-    images, heads = gates.shape
-    def kernel(j, g, m, l):
-        attend_image(j, g, m, l, 0, seq, heads)
-    n = joint.shape[1]
-    return pl.pallas_call(
-        kernel, grid=(images,),
-        out_shape=[jax.ShapeDtypeStruct((joint.shape[0], n // 3), jnp.bfloat16), jax.ShapeDtypeStruct((images, heads, seq), jnp.float32)],
-        in_specs=[
-            pl.BlockSpec((seq, n), lambda i: (i, 0)),
-            pl.BlockSpec((1, 1, heads), lambda i: (i, 0, 0), memory_space=pltpu.SMEM),
-        ],
-        out_specs=[pl.BlockSpec((seq, n // 3), lambda i: (i, 0)), pl.BlockSpec((1, heads, seq), lambda i: (i, 0, 0))],
-        compiler_params=pltpu.CompilerParams(vmem_limit_bytes=48*2**20),
-        name="attend",
-    )(joint, gates[:, None, :])
 def thirds(width):
     tiles = width // 128
     a, b = tiles // 3, tiles // 3
@@ -964,7 +1079,8 @@
     routers = jnp.pad(
         jnp.concatenate([head_router, token_router], axis=1), ((0, 0), (0, 127 - heads))
     )
-    joint_blocks, fc1_full, fc2_full, pre_cond_pad, modulation, routers_full, all_cond, all_asked = gather_weights(
+    mask_float = head_mask.astype(jnp.float32)
+    *gathered, flat_one, joint, log_total, mixed, attn, middle, flat_two = front_half(
         [
             jnp.concatenate([qkv_weight, proj_weight], axis=1),
             fc1_weight,
@@ -975,12 +1091,17 @@
         class_table,
         ada_weight,
         routers,
+        padded(jnp.pad(mask_float, ((0, 0), (0, 128 - heads)))),
+        tokens.reshape(count, width),
         width,
+        images,
+        seq,
+        heads,
         dp,
         fsdp,
     )
-    joint_full = joint_blocks.reshape(width, 4 * width)
-    triple, merger = joint_full[:, : 3 * width], joint_full[:, 3 * width :]
+    joint_blocks, fc1_full, fc2_full, pre_cond_pad, modulation, routers_full, all_cond, all_asked = gathered
+    merger = joint_blocks[:, :, 3 * width :].reshape(width, width)
     expand = fc1_full.reshape(width, hidden)
     shrink = fc2_full.reshape(hidden, width)
     routers_full = routers_full.reshape(width, 128)
@@ -990,26 +1111,15 @@
     all_asked = all_asked.reshape(everyone, asked.shape[1])
     pre_cond = pre_cond_pad[:images]
     cond = jax.nn.silu(pre_cond).astype(jnp.bfloat16)
-    modulation = modulation[:, :images].transpose(1, 0, 2).reshape(images, 6 * width)
+    modulation = modulation[:images]
     shift_one, scale_one, gate_one, shift_two, scale_two, gate_two = jnp.split(
         modulation[:, None, :], 6, axis=2
     )
     router_sig = jax.nn.sigmoid(matmul(cond, chooser))
-    mask_float = head_mask.astype(jnp.float32)
     head_gates = mask_float * router_sig
-    inputs = tokens.astype(jnp.float32)
-    normed_one = layer_norm(inputs)
-    flat_one = (
-        (normed_one * (1.0 + scale_one) + shift_one).astype(jnp.bfloat16).reshape(count, width)
-    )
-    joint = matmul(flat_one, triple).astype(jnp.bfloat16)
-    mixed, log_total = attend(joint, head_gates, seq)
-    attn = matmul(mixed, merger).reshape(images, seq, width)
-    middle = inputs + gate_one * attn
+    attn = attn.reshape(images, seq, width)
+    middle = middle.reshape(images, seq, width)
     normed_two = layer_norm(middle)
-    flat_two = (
-        (normed_two * (1.0 + scale_two) + shift_two).astype(jnp.bfloat16).reshape(count, width)
-    )
     rate = jax.nn.sigmoid(matmul(flat_two, picker)).reshape(images, seq, 1)
     upward = matmul(flat_two, expand)
     active = jax.nn.gelu(upward, approximate=True).astype(jnp.bfloat16)

time: 531 us -> 493 us (0.928); the launches traced: 521 us -> 488 us
  matrix products: 127 us -> 113 us
  other arithmetic: 32.8 us -> 21.3 us
  local copies, waits for them, and re-layouts: 27.9 us -> 19.6 us
    dot_general x6 -> x4, matrix products: 59.7 us -> 44.3 us  [matmul(): return jnp.dot(left, right, preferred_element_type=jnp.float32)]
    unnamed x110 -> x73, local copies, waits for them, and re-layouts: 19.6 us -> 7.94 us
    reduce_sum x4 -> x0, other arithmetic: 7.62 us -> none  [the longest x1 3.56 us: body(): grad_gate_one = jnp.sum(grad_middle * attn, axis=1)]
    pallas_call x2 -> x1, Pallas kernels: 148 us -> 146 us  [front_half(): pl.pallas_call(partial(front_kernel, dp, fsdp, width, images, seq, heads)...]
where the time goes in v6:
time: 493 us; the launch traced here: 488 us
  Pallas kernels  333 us (68%)
  matrix products  113 us (23%)
  other arithmetic  21.3 us (4%)
  local copies, waits for them, and re-layouts  19.6 us (4%)
    pallas_call x1, Pallas kernels, back_half(): pl.pallas_call(partial(back_kernel, dp, fsdp, width, images, seq, heads),...  187 us
    pallas_call x1, Pallas kernels, front_half(): pl.pallas_call(partial(front_kernel, dp, fsdp, width, images, seq, heads)...  146 us
    dot_general x4, matrix products, matmul(): return jnp.dot(left, right, preferred_element_type=jnp.float32)  44.3 us
    dot_general x3, matrix products, times_back(): lax.dot_general(left, right, (((1,), (1,)), ((), ())), preferred_element_...  34.8 us
    dot_general x8, matrix products, times_rows(): lax.dot_general(left, right, (((0,), (0,)), ((), ())), preferred_element_...  33.8 us

profile of v6, /device:TPU:0, one launch (start us, length us, event | category | flops | bytes accessed | tf_op | source)
XLA Modules:
  0.0 488.4 jit_solution(1258895886481562645)
XLA Ops:
  0.7 0.8 convert_element_type.75
  3.2 4.1 copy.47.refs_6_.refs_15_
  7.3 1.2 pad_maximum_fusion.2.refs_0_
  8.4 1.0 copy.46.refs_5_
  10.8 146.4 %front.1 = (bf16[8,144,4608]{2,1,0:T(8,128)(2,1)}, bf16[8,144,4608]{2,1,0:T(8,128)(2,1)}, bf16[8,4,144,1152]{3,2,1,0:T(8,128)(2,1)}, f32[8,1152]{1,0:T(8,128)}, ...) custom-call(bf16[144,4608]{1,0:T(8,128)(2,1)} %pad_maximum_fusion.2., ...), custom_call_target="tpu_custom_call" | custom-call | tf_op jit(solution)/shard_map/front/pallas_call | solution.py:402
  157.3 1.2 slice_reduce_fusion
  158.5 2.1 convolution_reduce_fusion.1
  160.6 1.0 slice_bitcast_fusion.8
  162.7 15.6 %fusion.56 = f32[768,4608]{1,0:T(8,128)} fusion(bf16[768,1152]{1,0:T(8,128)(2,1)S(1)} %bitcast.110, bf16[4608,1152]{1,0:T(8,128)(2,1)} %bitcast.125), kind=kOutput, calls=%fused_computation.130 | convolution fusion | flops 8153726976 | bytes 26542080 | tf_op jit(solution)/shard_map/dot_general | solution.py:45
  178.3 25.5 %fusion.6 = (bf16[768,4608]{1,0:T(8,128)(2,1)}, bf16[768,4608]{1,0:T(8,128)(2,1)}) fusion(f32[768,4608]{1,0:T(8,128)} %fusion.56, bf16[768,1152]{1,0:T(8,128)(2,1)} %get-tuple-element.34, bf16[1152,4608]{1,0:T(8,128)(2,1)} %bitcast.123), kind=kOutput, calls=%fused_computation.10 | convolution fusion | flops 8231583744 | bytes 40697856 | tf_op jit(solution)/shard_map/dot_general | solution.py:35
  203.8 16.6 %fusion.12 = (f32[3,1152]{1,0:T(4,128)}, f32[3,256]{1,0:T(4,128)S(1)}, bf16[3,256,1152]{2,1,0:T(8,128)(2,1)}) fusion(bf16[3,256,1152]{2,1,0:T(8,128)(2,1)S(1)} %copy-done.4, f32[3,256]{1,0:T(4,128)S(1)} %convert_multiply_fusion.2, f32[3,1152]{1,0:T(4,128)S(1)} %get-tuple-element.77, f32[3,256,1152]{2,1,0:T(8,128)S(1)} %bitcast.95, ...), kind=kOutput, calls=%fused_computation.25 | convolution fusion | flops 8163454976 | bytes 24806400 | tf_op jit(solution)/shard_map/dot_general | solution.py:35
  221.8 15.0 %multiply_reduce_fusion.3 = (f32[768]{0:T(1024)S(1)}, f32[768]{0:T(1024)S(1)}, f32[768,1152]{1,0:T(8,128)S(1)}) fusion(f32[768,1152]{1,0:T(8,128)S(1)} %copy-done.1, f32[768]{0:T(1024)S(1)} %broadcast_multiply_fusion, f32[3,1152]{1,0:T(4,128)} %get-tuple-element.76, f32[1152]{0:T(1024)S(1)} %convert.26, f32[768]{0:T(1024)S(1)} %convert.25, ...), kind=kOutput, calls=%fused_computation.33 | convolution fusion | flops 8160802816 | bytes 24803328 | tf_op jit(solution)/shard_map/dot_general | solution.py:45
  236.8 1.0 fusion.14
  237.8 0.8 copy-done.2
  241.1 1.3 fusion.51
  242.4 5.0 %fusion.49 = (f32[3,1152]{1,0:T(4,128)S(1)}, f32[3,1152]{1,0:T(4,128)S(1)}, f32[3,1152]{1,0:T(4,128)S(1)}, f32[3,256,1152]{2,1,0:T(8,128)S(1)}) fusion(f32[3,256,1152]{2,1,0:T(8,128)} %bitcast.97, f32[3,256]{1,0:T(4,128)S(1)} %get-tuple-element.82, f32[3,256,1152]{2,1,0:T(8,128)S(1)} %bitcast.96, f32[3,256]{1,0:T(4,128)S(1)} %div.67, ...), kind=kLoop, calls=%fused_computation.127 | loop fusion | flops 13260672 | bytes 15992832 | tf_op jit(solution)/shard_map/reduce_sum | solution.py:1143
  248.4 2.2 slice.62
  250.7 4.2 convolution_convert_fusion.3.refs_4_
  255.0 4.0 convolution_convert_fusion.2.refs_2_
  259.0 11.7 %convolution_convert_fusion.1 = bf16[4608,1152]{1,0:T(8,128)(2,1)} fusion(bf16[768,4608]{1,0:T(8,128)(2,1)S(1)} %bitcast.129, bf16[768,1152]{1,0:T(8,128)(2,1)S(1)} %bitcast.111), kind=kOutput, calls=%fused_computation.3 | convolution fusion | flops 8159035392 | bytes 19464192 | tf_op jit(solution)/shard_map/dot_general | solution.py:39
  270.8 10.8 %convolution_convert_fusion = bf16[1152,4608]{1,0:T(8,128)(2,1)} fusion(bf16[768,1152]{1,0:T(8,128)(2,1)S(1)} %copy-done.6, bf16[768,4608]{1,0:T(8,128)(2,1)S(1)} %bitcast.131), kind=kOutput, calls=%fused_computation.2 | convolution fusion | flops 8159035392 | bytes 19464192 | tf_op jit(solution)/shard_map/dot_general | solution.py:39
  283.6 186.5 %back.1 = (bf16[4,144,1152]{2,1,0:T(8,128)(2,1)}, bf16[4,144,1152]{2,1,0:T(8,128)(2,1)}, bf16[4,144,1152]{2,1,0:T(8,128)(2,1)}, bf16[4,8,8,864]{3,2,1,0:T(8,128)...) custom-call(bf16[8,4,144,1152]{3,2,1,0:T(8,128)(2,1)} %bitcast.98, ...), custom_call_target="tpu_custom_call" | custom-call | tf_op jit(solution)/shard_map/back/pallas_call | solution.py:1000
  470.2 1.5 convert_element_type.92
  471.9 1.8 pad_maximum_fusion
  473.9 1.0 slice_bitcast_fusion.4
  474.9 1.4 pad_maximum_fusion.1
  476.4 0.9 fusion.21
  477.3 3.9 convolution_bitcast_fusion
  481.3 1.2 fusion.18
  482.6 1.0 fusion.25
  483.6 1.8 bitcast_convert_fusion
  486.2 1.8 copy.55
  (124 shorter events, 12.6 us)
Async XLA Ops:
  0.6 6.6 %copy-start.13 = (bf16[144,3456]{1,0:T(8,128)(2,1)S(1)}, bf16[144,3456]{1,0:T(8,128)(2,1)}, u32[]{:S(2)}) copy-start(bf16[144,3456]{1,0:T(8,128)(2,1)} %param.25) | copy-start | bytes 2985988
  0.7 6.6 %copy-start.16 = (bf16[144,1152]{1,0:T(8,128)(2,1)S(1)}, bf16[144,1152]{1,0:T(8,128)(2,1)}, u32[]{:S(2)}) copy-start(bf16[144,1152]{1,0:T(8,128)(2,1)} %param.26) | copy-start | bytes 995332
  0.7 7.8 %copy-start.17 = (bf16[1000,144]{0,1:T(8,128)(2,1)S(1)}, bf16[1000,144]{0,1:T(8,128)(2,1)}, u32[]{:S(2)}) copy-start(bf16[1000,144]{0,1:T(8,128)(2,1)} %param.22) | copy-start | bytes 864004
  3.2 6.3 %copy-start.25 = (bf16[144,16]{0,1:T(8,128)(2,1)S(1)}, bf16[144,16]{0,1:T(8,128)(2,1)}, u32[]{:S(2)}) copy-start(bf16[144,16]{0,1:T(8,128)(2,1)} %param.24) | copy-start | bytes 13828
  3.2 6.3 %copy-start.28 = (bf16[144,1]{0,1:T(2,128)(2,1)S(1)}, bf16[144,1]{0,1:T(2,128)(2,1)}, u32[]{:S(2)}) copy-start(bf16[144,1]{0,1:T(2,128)(2,1)} %param.29) | copy-start | bytes 868
  3.2 7.0 %copy-start.26 = (s32[3,16]{1,0:T(4,128)S(1)}, s32[3,16]{1,0:T(4,128)}, u32[]{:S(2)}) copy-start(s32[3,16]{1,0:T(4,128)} %param.18) | copy-start | bytes 580
  10.8 149.8 %copy-start.24 = (s32[3,256]{1,0:T(4,128)S(1)}, s32[3,256]{1,0:T(4,128)}, u32[]{:S(2)}) copy-start(s32[3,256]{1,0:T(4,128)} %param.19) | copy-start | bytes 9220
  10.8 151.4 %copy-start.3 = (bf16[3,256,1152]{2,1,0:T(8,128)(2,1)S(1)}, bf16[3,256,1152]{2,1,0:T(8,128)(2,1)}, u32[]{:S(2)}) copy-start(bf16[3,256,1152]{2,1,0:T(8,128)(2,1)} %param.20) | copy-start | bytes 5308420
  162.7 15.7 %copy-start.8 = (bf16[3,256,1152]{2,1,0:T(8,128)(2,1)}, bf16[3,256,1152]{2,1,0:T(8,128)(2,1)S(1)}, u32[]{:S(2)}) copy-start(bf16[3,256,1152]{2,1,0:T(8,128)(2,1)S(1)} %fusion.9) | copy-start | bytes 5308420
  178.3 25.5 %copy-start.1 = (f32[768,1152]{1,0:T(8,128)S(1)}, f32[768,1152]{1,0:T(8,128)}, u32[]{:S(2)}) copy-start(f32[768,1152]{1,0:T(8,128)} %get-tuple-element.32) | copy-start | bytes 10616836
  178.3 25.5 %copy-start.4 = (bf16[3,256,1152]{2,1,0:T(8,128)(2,1)S(1)}, bf16[3,256,1152]{2,1,0:T(8,128)(2,1)}, u32[]{:S(2)}) copy-start(bf16[3,256,1152]{2,1,0:T(8,128)(2,1)} %param.20) | copy-start | bytes 5308420
  203.8 16.6 %copy-start.5 = (bf16[768,1152]{1,0:T(8,128)(2,1)S(1)}, bf16[768,1152]{1,0:T(8,128)(2,1)}, u32[]{:S(2)}) copy-start(bf16[768,1152]{1,0:T(8,128)(2,1)} %get-tuple-element.34) | copy-start | bytes 5308420
  221.8 15.0 %copy-start.19 = (f32[3,1152]{1,0:T(4,128)S(1)}, f32[3,1152]{1,0:T(4,128)}, u32[]{:S(2)}) copy-start(f32[3,1152]{1,0:T(4,128)} %get-tuple-element.76) | copy-start | bytes 41476
  242.4 5.1 %copy-start.23 = (f32[3,1152]{1,0:T(4,128)S(1)}, f32[3,1152]{1,0:T(4,128)}, u32[]{:S(2)}) copy-start(f32[3,1152]{1,0:T(4,128)} %get-tuple-element.53) | copy-start | bytes 41476
  242.4 5.8 %copy-start.20 = (f32[3,1152]{1,0:T(4,128)S(1)}, f32[3,1152]{1,0:T(4,128)}, u32[]{:S(2)}) copy-start(f32[3,1152]{1,0:T(4,128)} %get-tuple-element.75) | copy-start | bytes 41476
  247.4 3.3 copy-start
  248.4 10.6 %slice-start = ((s8[7077888]{0:T(1024)(128)(4,1)}), s8[4194304]{0:T(1024)(128)(4,1)S(1)}, s32[]{:S(2)}) async-start(s8[7077888]{0:T(1024)(128)(4,1)} %bitcast.128), calls=%async_computation | async-start | bytes 8388608
  250.7 4.2 copy-start.29
  250.7 8.3 %slice-start.1 = ((s8[7077888]{0:T(1024)(128)(4,1)}), s8[2883584]{0:T(1024)(128)(4,1)S(1)}, s32[]{:S(2)}) async-start(s8[7077888]{0:T(1024)(128)(4,1)} %bitcast.128), calls=%async_computation.1 | async-start | bytes 5767168
  254.9 4.1 copy-start.9
  255.0 15.8 %slice-start.2 = ((s8[7077888]{0:T(1024)(128)(4,1)}), s8[4194304]{0:T(1024)(128)(4,1)S(1)}, s32[]{:S(2)}) async-start(s8[7077888]{0:T(1024)(128)(4,1)} %bitcast.130), calls=%async_computation.2 | async-start | bytes 8388608
  259.0 11.7 %copy-start.6 = (bf16[768,1152]{1,0:T(8,128)(2,1)S(1)}, bf16[768,1152]{1,0:T(8,128)(2,1)}, u32[]{:S(2)}) copy-start(bf16[768,1152]{1,0:T(8,128)(2,1)} %get-tuple-element.34) | copy-start | bytes 5308420
  259.0 11.7 %slice-start.3 = ((s8[7077888]{0:T(1024)(128)(4,1)}), s8[2883584]{0:T(1024)(128)(4,1)S(1)}, s32[]{:S(2)}) async-start(s8[7077888]{0:T(1024)(128)(4,1)} %bitcast.130), calls=%async_computation.3 | async-start | bytes 5767168
  270.7 10.9 %copy-start.12 = (bf16[8,144,128]{2,1,0:T(8,128)(2,1)S(1)}, bf16[8,144,128]{2,1,0:T(8,128)(2,1)}, u32[]{:S(2)}) copy-start(bf16[8,144,128]{2,1,0:T(8,128)(2,1)} %get-tuple-element.35) | copy-start | bytes 884740
  270.8 10.9 %copy-start.22 = (f32[8,1152]{1,0:T(8,128)S(1)}, f32[8,1152]{1,0:T(8,128)}, u32[]{:S(2)}) copy-start(f32[8,1152]{1,0:T(8,128)} %get-tuple-element.43.refs_16_) | copy-start | bytes 110596
  270.8 10.9 %copy-start.27 = (s32[3,16]{1,0:T(4,128)S(1)}, s32[3,16]{1,0:T(4,128)}, u32[]{:S(2)}) copy-start(s32[3,16]{1,0:T(4,128)} %param.18) | copy-start | bytes 580
  270.8 12.2 %copy-start.21 = (f32[3,1152]{1,0:T(4,128)S(1)}, f32[3,1152]{1,0:T(4,128)}, u32[]{:S(2)}) copy-start(f32[3,1152]{1,0:T(4,128)} %get-tuple-element.74) | copy-start | bytes 41476
  471.9 1.8 copy-start.11
  473.9 2.4 copy-start.14
  476.4 4.8 copy-start.18
  477.3 6.3 %copy-start.10 = (bf16[4,144,1152]{2,1,0:T(8,128)(2,1)S(1)}, bf16[4,144,1152]{2,1,0:T(8,128)(2,1)}, u32[]{:S(2)}) copy-start(bf16[4,144,1152]{2,1,0:T(8,128)(2,1)} %get-tuple-element.52) | copy-start | bytes 3981316
  482.6 3.6 copy-start.7
  (2 other events, 3.4 us)
